TPU v7x, 512 devices: a whole 4x4x16 slice. The times are simulated.
512 devices in a mesh: grp: 16 (over z), seq: 32 (over y, x, core).
Axes of the slice: x: 4, y: 4, z: 16, core: 2. Of those that a mesh axis runs over, the one named last changes fastest.
Arguments:
- queries: bfloat16 [16, 4096, 1024], P('grp', 'seq'), may hold values from -36 to 36
- keys: bfloat16 [16, 4096, 1024], P('grp', 'seq'), may hold values from -36 to 36
- values: bfloat16 [16, 4096, 1024], P('grp', 'seq'), may hold values from -5 to 5
- grad_attended: bfloat16 [16, 4096, 1024], P('grp', 'seq'), may hold values from -5 to 5
- features: float32 [128, 128], replicated, may hold values from -18 to 18
- chain_lengths: int32 [16, 4], P('grp'), may hold values from 1 to 2048, 4096 in all within a row
Outputs:
- attended: bfloat16 [16, 4096, 1024], P('grp', 'seq')
- grad_queries: bfloat16 [16, 4096, 1024], P('grp', 'seq')
- grad_keys: bfloat16 [16, 4096, 1024], P('grp', 'seq')
- grad_values: bfloat16 [16, 4096, 1024], P('grp', 'seq')
Inputs may be any that keep to these rules, and one draw needn't show every extreme that they name: `chain_lengths`: each row lists the lengths of its batch's 4 chains in order of position; they sum to 4096 and the largest is 2048.
All inputs are finite; a program needn't handle non-finite values.
Results may differ from a plain program's by a relative error of at most 0.0034.
Values sent between devices are 32-bit elements; how exact they have to be, the bound alone decides.
No kernel may reach another device: no remote copies, remote signals or barrier semaphores. Data moves between devices by JAX's collectives and lax.ppermute only.
A program may use at most 128 MiB of HBM per device.

v0:
```python
import jax
import jax.numpy as jnp
from jax import lax
from jax.sharding import PartitionSpec as P

H = 8


exact_precision = lax.Precision.HIGHEST
epsilon = 1e-06


def carried_in(part, axis, combine, identity, reverse):
    count = lax.axis_size(axis)
    place = lax.axis_index(axis)
    ahead = count - 1 - place if reverse else place
    gathered = jax.tree.map(lambda a: lax.all_gather(a, axis), part)
    state = jax.tree.map(lambda a, e: jnp.zeros_like(a) + jnp.asarray(e, a.dtype), part, identity)

    def one(step, state):
        source = count - 1 - step if reverse else step
        return combine(
            state, jax.tree.map(lambda a: lax.dynamic_index_in_dim(a, source, 0, False), gathered)
        )

    return lax.fori_loop(0, ahead, one, state)


def feature_logits(block, features):
    row_count = block.shape[0]
    head_size = features.shape[1]
    scaled = block.reshape(row_count, H, head_size).astype(jnp.float32) * head_size ** (-0.25)
    logits = jnp.einsum("phd,md->phm", scaled, features, precision=exact_precision)
    return (scaled, logits - 0.5 * jnp.sum(scaled * scaled, axis=2, keepdims=True))


def logit_grad(grad_feats, raised, scaled, features):
    grad_logits = grad_feats * raised
    back = jnp.einsum("phm,md->phd", grad_logits, features, precision=exact_precision)
    back = back - jnp.sum(grad_logits, axis=2, keepdims=True) * scaled
    return back * scaled.shape[2] ** (-0.25)


def link(earlier, later):
    keep = 1.0 - later[0]
    return (
        jnp.maximum(earlier[0], later[0]),
        later[1] + keep * earlier[1],
        later[2] + keep * earlier[2],
    )


def along_chains(state_pair, total_pair, flags):
    reset_left, reset_right, continue_left, continue_right = flags
    first_parts = (state_pair[0], total_pair[0])
    last_parts = (state_pair[1], total_pair[1])
    empty = (
        jnp.zeros((), jnp.float32),
        jnp.zeros_like(last_parts[0]),
        jnp.zeros_like(last_parts[1]),
    )
    from_left = carried_in((reset_left, last_parts[0], last_parts[1]), "seq", link, empty, False)
    from_right = carried_in((reset_right, first_parts[0], first_parts[1]), "seq", link, empty, True)
    left_pieces = (from_left[1], from_left[2])
    right_pieces = (from_right[1], from_right[2])
    states = jnp.stack([left_pieces[0] * continue_left, right_pieces[0] * continue_right])
    totals = jnp.stack([left_pieces[1] * continue_left, right_pieces[1] * continue_right])
    return (states, totals)


def on_device(queries, keys, values, grad_attended, features, chain_lengths):
    row_count = queries.shape[1]
    head_size = features.shape[1]
    ratio = features.shape[0] ** (-0.5)
    start = lax.axis_index("seq") * row_count
    lengths = chain_lengths[0]
    chain_ends = jnp.cumsum(lengths)
    chain_starts = chain_ends - lengths
    positions = start + jnp.arange(row_count, dtype=jnp.int32)
    chain_id = jnp.sum((positions[:, None] >= chain_ends[None, :]).astype(jnp.int32), axis=1)
    mask_first = (chain_id == chain_id[0]).astype(jnp.float32)
    mask_last = (chain_id == chain_id[row_count - 1]).astype(jnp.float32)
    mask_pair = jnp.stack([mask_first, mask_last])
    single = (chain_id[0] == chain_id[row_count - 1]).astype(jnp.float32)
    continue_left = 1.0 - jnp.any(chain_starts == start).astype(jnp.float32)
    continue_right = 1.0 - jnp.any(chain_ends == start + row_count).astype(jnp.float32)
    flags = (
        1.0 - single * continue_left,
        1.0 - single * continue_right,
        continue_left,
        continue_right,
    )
    key_scaled, key_logits = feature_logits(keys[0], features)
    local_peak = jnp.max(key_logits, axis=(0, 2))
    peak = lax.pmax(local_peak, ("grp", "seq"))
    query_scaled, query_logits = feature_logits(queries[0], features)
    query_raised = jnp.exp(query_logits - jnp.max(query_logits, axis=2, keepdims=True)) * ratio
    query_feature_maps = query_raised + epsilon * ratio
    key_raised = jnp.exp(key_logits - peak[None, :, None]) * ratio
    key_feature_maps = key_raised + epsilon * ratio
    value_matrix_rows = values[0].reshape(row_count, H, head_size).astype(jnp.float32)
    same_chain = (chain_id[:, None] == chain_id[None, :]).astype(jnp.float32)
    scores = (
        jnp.einsum("phm,shm->hps", query_feature_maps, key_feature_maps, precision=exact_precision)
        * same_chain[None]
    )
    local_numer = jnp.einsum("hps,shd->phd", scores, value_matrix_rows, precision=exact_precision)
    local_denom = jnp.sum(scores, axis=2).T
    edge_states = jnp.einsum(
        "cp,phm,phd->chmd",
        mask_pair,
        key_feature_maps,
        value_matrix_rows,
        precision=exact_precision,
    )
    edge_totals = jnp.einsum("cp,phm->chm", mask_pair, key_feature_maps, precision=exact_precision)
    carried_states, carried_totals = along_chains(edge_states, edge_totals, flags)
    numerator_value = local_numer + jnp.einsum(
        "cp,phm,chmd->phd", mask_pair, query_feature_maps, carried_states, precision=exact_precision
    )
    denom = local_denom + jnp.einsum(
        "cp,phm,chm->ph", mask_pair, query_feature_maps, carried_totals, precision=exact_precision
    )
    exact = numerator_value / denom[:, :, None]
    attended = exact.astype(jnp.bfloat16).reshape(1, row_count, H * head_size)
    grad_rows = grad_attended[0].reshape(row_count, H, head_size).astype(jnp.float32)
    numerator_gradient = grad_rows / denom[:, :, None]
    grad_denom = -jnp.sum(grad_rows * exact, axis=2) / denom
    gram = (
        jnp.einsum("phd,shd->hps", numerator_gradient, value_matrix_rows, precision=exact_precision)
        + grad_denom.T[:, :, None]
    )
    gram = gram * same_chain[None]
    grad_query_feats = jnp.einsum("hps,shm->phm", gram, key_feature_maps, precision=exact_precision)
    grad_key_feats = jnp.einsum("hps,phm->shm", gram, query_feature_maps, precision=exact_precision)
    grad_value_rows = jnp.einsum(
        "hps,phd->shd", scores, numerator_gradient, precision=exact_precision
    )
    back_states = jnp.einsum(
        "cp,phm,phd->chmd",
        mask_pair,
        query_feature_maps,
        numerator_gradient,
        precision=exact_precision,
    )
    back_totals = jnp.einsum(
        "cp,phm,ph->chm", mask_pair, query_feature_maps, grad_denom, precision=exact_precision
    )
    returned_states, returned_totals = along_chains(back_states, back_totals, flags)
    grad_query_feats = grad_query_feats + jnp.einsum(
        "cp,phd,chmd->phm", mask_pair, numerator_gradient, carried_states, precision=exact_precision
    )
    grad_query_feats = grad_query_feats + jnp.einsum(
        "cp,ph,chm->phm", mask_pair, grad_denom, carried_totals, precision=exact_precision
    )
    grad_key_feats = grad_key_feats + jnp.einsum(
        "cp,phd,chmd->phm", mask_pair, value_matrix_rows, returned_states, precision=exact_precision
    )
    grad_key_feats = grad_key_feats + jnp.einsum(
        "cp,chm->phm", mask_pair, returned_totals, precision=exact_precision
    )
    grad_value_rows = grad_value_rows + jnp.einsum(
        "cp,phm,chmd->phd", mask_pair, key_feature_maps, returned_states, precision=exact_precision
    )
    grad_queries = logit_grad(grad_query_feats, query_raised, query_scaled, features)
    grad_keys = logit_grad(grad_key_feats, key_raised, key_scaled, features)
    width = H * head_size
    return (
        attended,
        grad_queries.astype(jnp.bfloat16).reshape(1, row_count, width),
        grad_keys.astype(jnp.bfloat16).reshape(1, row_count, width),
        grad_value_rows.astype(jnp.bfloat16).reshape(1, row_count, width),
    )


def solution(mesh):
    return jax.shard_map(
        on_device,
        mesh=mesh,
        in_specs=(
            P("grp", "seq", None),
            P("grp", "seq", None),
            P("grp", "seq", None),
            P("grp", "seq", None),
            P(),
            P("grp", None),
        ),
        out_specs=(
            P("grp", "seq", None),
            P("grp", "seq", None),
            P("grp", "seq", None),
            P("grp", "seq", None),
        ),
        check_vma=False,
    )
```

profile of v0, /device:TPU:63, one launch (start us, length us, event | category | flops | bytes accessed | tf_op | source)
XLA Modules:
  0.0 710.6 jit_solution(5102049428134863735)
XLA Ops:
  10.7 105.5 %pmax.7 = f32[8]{0:T(128)S(1)} all-reduce(f32[8]{0:T(128)S(1)} %get-tuple-element.529), channel_id=1, replica_groups=mesh['grp'=16,'seq'=32] {'grp','seq'}, use_global_device_ids=true, to_apply=%region_4.5 | all-reduce | flops 8 | bytes 64 | tf_op jit(solution)/shard_map/pmax | solution.py:95
  116.6 1.3 compare_bitcast_fusion.1
  123.8 1.9 copy.134
  125.7 1.3 compare_reduce_fusion.1
  131.6 1.3 dynamic-slice
  134.3 63.0 %all-reduce.2 = (f32[32]{0:T(128)S(1)}, f32[32]{0:T(128)S(1)}) all-reduce(f32[32]{0:T(128)S(1)} %dynamic-update-slice.1, f32[32]{0:T(128)S(1)} %dynamic-update-slice), channel_id=1, replica_groups=mesh['grp'=16,'seq'=32] {'seq'}, use_global_device_ids=true, to_apply=%add.1 | all-reduce | flops 64 | bytes 512
  197.8 24.9 %all_gather.47 = f32[32,8,128]{2,1,0:T(8,128)S(1)} all-gather(f32[1,8,128]{2,1,0:T(8,128)S(1)} %bitcast.237), channel_id=1, replica_groups=mesh['grp'=16,'seq'=32] {'seq'}, dimensions={0}, use_global_device_ids=true | all-gather | bytes 135168 | tf_op jit(solution)/shard_map/all_gather | solution.py:17
  222.6 26.4 %all_gather.43 = f32[32,8,128]{2,1,0:T(8,128)} all-gather(f32[1,8,128]{2,1,0:T(8,128)S(1)} %bitcast.235), channel_id=1, replica_groups=mesh['grp'=16,'seq'=32] {'seq'}, dimensions={0}, use_global_device_ids=true | all-gather | bytes 135168 | tf_op jit(solution)/shard_map/all_gather | solution.py:17
  249.1 2.4 fusion.96
  252.2 44.1 %all-gather.5.cloned.1.call-done = f32[32,8,128,128]{3,2,0,1:T(8,128)} async-done(((f32[1,8,128,128]{3,2,0,1:T(8,128)}), f32[32,8,128,128]{3,2,0,1:T(8,128)}) %all-gather.5.cloned.1.call-update) | async-done | bytes 16777232 | tf_op jit(solution)/shard_map/all_gather | solution.py:17
  296.3 98.5 %while.60 = (s32[]{:T(128)}, f32[8,128,128]{2,1,0:T(8,128)S(1)}, f32[8,128]{1,0:T(8,128)S(1)}, s32[]{:T(128)}, f32[32,8,128,128]{3,2,0,1:T(8,128)}, /*index=5*/f...) while((s32[]{:T(128)}, f32[8,128,128]{2,1,0:T(8,128)S(1)}, ...), condition=%wide.region_9.10_spmd, body=%wide.region_8.9_spmd.sunk | while | flops 264198 | bytes 1585343 | solution.py:26
  307.1 1.3 bitcast_add_fusion.18
  319.8 1.3 bitcast_add_fusion.18
  326.2 1.3 bitcast_add_fusion.18
  332.5 1.3 bitcast_add_fusion.18
  335.7 1.3 bitcast_add_fusion.18
  342.0 1.3 bitcast_add_fusion.18
  345.2 1.3 bitcast_add_fusion.18
  348.4 1.3 bitcast_add_fusion.18
  351.6 1.3 bitcast_add_fusion.18
  361.1 1.3 bitcast_add_fusion.18
  367.5 1.3 bitcast_add_fusion.18
  370.7 1.3 bitcast_add_fusion.18
  377.0 1.3 bitcast_add_fusion.18
  380.2 1.3 bitcast_add_fusion.18
  383.3 1.3 bitcast_add_fusion.18
  386.5 1.3 bitcast_add_fusion.18
  389.7 1.3 bitcast_add_fusion.18
  392.9 1.3 bitcast_add_fusion.18
  399.6 2.7 fusion.18
  402.3 3.0 multiply_reduce_fusion
  405.3 3.1 fusion.9
  412.0 1.8 copy.160
  413.8 3.3 convolution_bitcast_fusion.2
  423.2 20.4 %all_gather.51 = f32[32,8,128]{2,1,0:T(8,128)S(1)} all-gather(f32[1,8,128]{2,1,0:T(8,128)S(1)} %bitcast.238), channel_id=1, replica_groups=mesh['grp'=16,'seq'=32] {'seq'}, dimensions={0}, use_global_device_ids=true | all-gather | bytes 135168 | tf_op jit(solution)/shard_map/all_gather | solution.py:17
  443.6 23.6 %all_gather.49 = f32[32,8,128]{2,1,0:T(8,128)S(1)} all-gather(f32[1,8,128]{2,1,0:T(8,128)S(1)} %bitcast.236), channel_id=1, replica_groups=mesh['grp'=16,'seq'=32] {'seq'}, dimensions={0}, use_global_device_ids=true | all-gather | bytes 135168 | tf_op jit(solution)/shard_map/all_gather | solution.py:17
  467.2 29.4 %all-gather.11.cloned.1.call-done = f32[32,8,128,128]{3,2,0,1:T(8,128)} async-done(((f32[1,8,128,128]{3,2,0,1:T(8,128)}), f32[32,8,128,128]{3,2,0,1:T(8,128)}) %all-gather.11.cloned.1.call-update) | async-done | bytes 16777232 | tf_op jit(solution)/shard_map/all_gather | solution.py:17
  496.6 90.6 %all-gather.9.cloned.1.call-done = f32[32,8,128,128]{3,2,0,1:T(8,128)} async-done(((f32[1,8,128,128]{3,2,0,1:T(8,128)}), f32[32,8,128,128]{3,2,0,1:T(8,128)}) %all-gather.9.cloned.1.call-update) | async-done | bytes 16777232 | tf_op jit(solution)/shard_map/all_gather | solution.py:17
  587.3 98.2 %while.62 = (s32[]{:T(128)}, f32[8,128,128]{2,1,0:T(8,128)S(1)}, f32[8,128]{1,0:T(8,128)S(1)}, s32[]{:T(128)}, f32[32,8,128,128]{3,2,0,1:T(8,128)}, /*index=5*/f...) while((s32[]{:T(128)}, f32[8,128,128]{2,1,0:T(8,128)S(1)}, ...), condition=%wide.region_17.18_spmd, body=%wide.region_16.17_spmd.sunk | while | flops 264198 | bytes 1585343 | solution.py:26
  589.2 1.3 bitcast_add_fusion.22
  592.4 1.3 bitcast_add_fusion.22
  595.5 1.3 bitcast_add_fusion.22
  598.7 1.3 bitcast_add_fusion.22
  685.6 2.0 fusion.74
  691.7 2.1 fusion.21
  693.8 2.9 convolution_bitcast_fusion
  696.7 2.6 fusion.98
  700.9 2.4 fusion.38
  (271 shorter events, 162.8 us)
Async XLA Ops:
  7.2 2.7 copy-start
  7.2 244.3 %all-gather.7.cloned.1.call-start = ((), (), s32[]{:S(2)}) async-start(), calls=%async_computation.1 | async-start | bytes 17301504 | tf_op jit(solution)/shard_map/all_gather | solution.py:17
  10.7 105.5 %copy-start.3 = (f32[128,8,128]{0,2,1:T(8,128)}, f32[128,8,128]{0,2,1:T(8,128)S(1)}, u32[]{:S(2)}) copy-start(f32[128,8,128]{0,2,1:T(8,128)S(1)} %get-tuple-element.530) | copy-start | bytes 1572868
  116.2 3.3 copy-start.10
  116.6 12.9 %copy-start.1 = (f32[128,8,128]{2,0,1:T(8,128)}, f32[128,8,128]{2,0,1:T(8,128)S(1)}, u32[]{:S(2)}) copy-start(f32[128,8,128]{2,0,1:T(8,128)S(1)} %copy.121) | copy-start | bytes 1572868
  118.5 78.9 %copy-start.9 = (pred[2,128]{1,0:T(4,128)(4,1)}, pred[2,128]{1,0:T(4,128)(4,1)S(1)}, u32[]{:S(2)}) copy-start(pred[2,128]{1,0:T(4,128)(4,1)S(1)} %get-tuple-element.513) | copy-start | bytes 772
  121.7 174.6 %all-gather.5.cloned.1.call-start = ((), (), s32[]{:S(2)}) async-start(), calls=%async_computation | async-start | bytes 17301504 | tf_op jit(solution)/shard_map/all_gather | solution.py:17
  122.5 374.1 %all-gather.11.cloned.1.call-start = ((), (), s32[]{:S(2)}) async-start(), calls=%async_computation.3 | async-start | bytes 17301504 | tf_op jit(solution)/shard_map/all_gather | solution.py:17
  251.6 0.6 copy-start.13
  394.8 0.5 copy-start.12
  397.8 19.3 %copy-start.7 = (f32[128,8]{0,1:T(8,128)}, f32[128,8]{0,1:T(8,128)S(1)}, u32[]{:S(2)}) copy-start(f32[128,8]{0,1:T(8,128)S(1)} %fusion.40) | copy-start | bytes 12292
  398.5 11.0 %copy-start.8 = (f32[128,8]{0,1:T(8,128)}, f32[128,8]{0,1:T(8,128)S(1)}, u32[]{:S(2)}) copy-start(f32[128,8]{0,1:T(8,128)S(1)} %bitcast_add_fusion.9) | copy-start | bytes 12292
  399.6 2.7 copy-start.5
  399.6 2.7 copy-start.6
  409.5 177.8 %all-gather.9.cloned.1.call-start = ((), (), s32[]{:S(2)}) async-start(), calls=%async_computation.2 | async-start | bytes 17301504 | tf_op jit(solution)/shard_map/all_gather | solution.py:17
  411.0 280.7 %copy-start.2 = (f32[128,8,128]{2,0,1:T(8,128)S(1)}, f32[128,8,128]{2,0,1:T(8,128)}, u32[]{:S(2)}) copy-start(f32[128,8,128]{2,0,1:T(8,128)} %copy-done.1) | copy-start | bytes 1572868
  418.9 2.3 copy-start.4
  418.9 277.8 %copy-start.11 = (f32[8]{0:T(128)S(1)}, f32[8]{0:T(128)}, u32[]{:S(2)}) copy-start(f32[8]{0:T(128)} %copy-done.10) | copy-start | bytes 100
Sparse Core Ops, SparseCore 0:
  121.8 83.5 all-gather.6
  208.6 87.6 all-gather.4
  409.6 86.8 all-gather.10
  499.6 87.6 all-gather.8
where the time goes:
time: 717 us; the launch traced here: 711 us
  blocking collectives  264 us (37%)
  waiting for transfers between devices  165 us (23%)
  other arithmetic  110 us (15%)
  local copies, waits for them, and re-layouts  78.5 us (11%)
  loops' own time  41.5 us (6%)
  matrix products  34.8 us (5%)
  between operations  16.9 us (2%)
    all_gather x4, waiting for transfers between devices, carried_in(): gathered = jax.tree.map(lambda a: lax.all_gather(a, axis), part)  164 us
    pmax x1, blocking collectives, on_device(): peak = lax.pmax(local_peak, ('grp', 'seq'))  106 us
    all_gather x4, blocking collectives, carried_in(): gathered = jax.tree.map(lambda a: lax.all_gather(a, axis), part)  95.3 us
    add x62, other arithmetic, link(): later[1] + keep * earlier[1]  77.6 us
    unnamed x1, blocking collectives  63 us
    dynamic_slice x62, local copies, waits for them, and re-layouts, one(): lax.dynamic_index_in_dim(a, source, 0, False)  56 us
    another operation x4, loops' own time, carried_in(): return lax.fori_loop(0, ahead, one, state)  41.5 us
    add x62, other arithmetic, link(): later[2] + keep * earlier[2]  21.7 us
  transfers between devices with their start and end apart: 4, of which 3 were waited for; matrix products, arithmetic and copies ran while one was open for 4% of the time, Pallas kernels for 0%

commit v1 on v0

v1 whole, which is shorter than its diff:
```python
import functools

import jax
import jax.numpy as jnp
from jax import lax
from jax.experimental import pallas as pl
from jax.experimental.pallas import tpu as pltpu
from jax.sharding import PartitionSpec as P

H = 8
D = 128
M = 128
CHAINS = 4
EPS = 1e-06
SCALE = D ** (-0.25)
RATIO = M ** (-0.5)
F32 = jnp.float32
BF16 = jnp.bfloat16
NN = (((1,), (0,)), ((), ()))
NT = (((1,), (1,)), ((), ()))
TN = (((0,), (0,)), ((), ()))


def dot(a, b, dims):
    return lax.dot_general(a, b, dims, preferred_element_type=F32)


def split(x):
    hi = x.astype(BF16)
    return hi, (x - hi.astype(F32)).astype(BF16)


def split3(x):
    hi = x.astype(BF16)
    rest = x - hi.astype(F32)
    mid = rest.astype(BF16)
    return hi, mid, (rest - mid.astype(F32)).astype(BF16)


def dot3(a, b, dims):
    (ah, al), (bh, bl) = a, b
    return dot(ah, bh, dims) + (dot(ah, bl, dims) + dot(al, bh, dims))


def head(h):
    return slice(h * D, (h + 1) * D)


def logits_of(x, parts):
    f1, f2, f3 = parts
    z = dot(x, f1, NT) + (dot(x, f2, NT) + dot(x, f3, NT))
    wide = x.astype(F32)
    return SCALE * z - (0.5 * SCALE * SCALE) * jnp.sum(wide * wide, axis=1, keepdims=True)


class Chains:
    def __init__(self, lens, place, rows):
        self.rows = rows
        self.first_row = place[0] * rows
        l0, l1, l2 = lens[0, 0], lens[0, 1], lens[0, 2]
        self.starts = (jnp.int32(0), l0, l0 + l1, l0 + l1 + l2)
        self.lens = lens

    def count_ended(self, position):
        c = jnp.int32(0)
        for s in self.starts[1:]:
            c = c + (position >= s).astype(jnp.int32)
        return c

    def present(self):
        return self.count_ended(self.first_row), self.count_ended(self.first_row + self.rows - 1) + 1

    def start_of(self, c):
        s = self.starts
        return jnp.where(c == 0, s[0], jnp.where(c == 1, s[1], jnp.where(c == 2, s[2], s[3])))

    def mask(self, c, axis=0, shape=None):
        shape = (self.rows, D) if shape is None else shape
        low = self.start_of(c) - self.first_row
        at = lax.broadcasted_iota(jnp.int32, shape, axis)
        return (at >= low) & (at < low + self.lens[0, c])


def key_kernel(lens, place, k_ref, f_ref, kl_ref, pay_ref):
    rows = k_ref.shape[0]
    chains = Chains(lens, place, rows)
    parts = split3(f_ref[...])
    masks = [chains.mask(c) for c in range(CHAINS)]
    for h in range(H):
        kl = logits_of(k_ref[:, head(h)], parts)
        kl_ref[:, head(h)] = kl
        peak = jnp.max(kl, axis=(0, 1), keepdims=True)
        raised = jnp.exp(kl - peak)
        for c in range(CHAINS):
            at = c * H + h
            pay_ref[at : at + 1, :] = jnp.sum(
                jnp.where(masks[c], raised, 0.0), axis=0, keepdims=True
            )
        at = CHAINS * H + h
        pay_ref[at : at + 1, :] = jnp.broadcast_to(peak, (1, D))


def state_kernel(lens, place, kl_ref, v_ref, gp_ref, s_ref):
    rows = v_ref.shape[0]
    chains = Chains(lens, place, rows)
    s_ref[...] = jnp.zeros_like(s_ref)
    low, high = chains.present()

    def one(c, carry):
        mask = chains.mask(c)
        for h in range(H):
            raised = jnp.where(mask, jnp.exp(kl_ref[:, head(h)] - gp_ref[h : h + 1, :]), 0.0)
            hi, lo = split(raised)
            v = v_ref[:, head(h)]
            s_ref[c * H + h, :M, :] = dot(hi, v, TN) + dot(lo, v, TN)
        return carry

    lax.fori_loop(low, high, one, 0)
    row = lax.broadcasted_iota(jnp.int32, (8, rows), 0)
    hot = jnp.zeros((8, rows), F32)
    for c in range(CHAINS):
        inside = chains.mask(c, 1, (8, rows)) & (row == c)
        hot = jnp.where(inside, 1.0, hot)
    sums = dot(hot.astype(BF16), v_ref[...], NN)
    for h in range(H):
        for c in range(CHAINS):
            s_ref[c * H + h, M : M + 1, :] = sums[c : c + 1, head(h)]


def query_kernel(q_ref, f_ref, all_ref, gp_ref, qr_ref, te_ref):
    parts = split3(f_ref[...])
    for h in range(H):
        ql = logits_of(q_ref[:, head(h)], parts)
        qr_ref[:, head(h)] = jnp.exp(ql - jnp.max(ql, axis=1, keepdims=True)) * RATIO
    gp = gp_ref[...]

    def one(d, sums):
        share = jnp.exp(all_ref[d, CHAINS * H :, :] - gp)
        return tuple(sums[c] + share * all_ref[d, c * H : (c + 1) * H, :] for c in range(CHAINS))

    zero = jnp.zeros((H, D), F32)
    sums = lax.fori_loop(0, all_ref.shape[0], one, (zero,) * CHAINS)
    for c in range(CHAINS):
        te_ref[c * H : (c + 1) * H, :] = sums[c]


def back_kernel(lens, place, qr_ref, g_ref, te_ref, gp_ref, peak_ref, b_ref, t_ref, inv_ref):
    rows = g_ref.shape[0]
    chains = Chains(lens, place, rows)
    share = jnp.exp(gp_ref[...] - peak_ref[...])
    for c in range(CHAINS):
        count = lens[0, c].astype(F32)
        t_ref[c * H : (c + 1) * H, :] = RATIO * (share * te_ref[c * H : (c + 1) * H, :] + EPS * count)
    b_ref[...] = jnp.zeros_like(b_ref)
    low, high = chains.present()

    def one(c, carry):
        mask = chains.mask(c)
        for h in range(H):
            qf = qr_ref[:, head(h)] + EPS * RATIO
            total = t_ref[pl.ds(c * H + h, 1), :]
            inv = 1.0 / jnp.sum(qf * total, axis=1, keepdims=True)
            hi, lo = split(jnp.where(mask, qf * inv, 0.0))
            g = g_ref[:, head(h)]
            b_ref[c * H + h] = dot(hi, g, TN) + dot(lo, g, TN)
            inv_ref[:, head(h)] = jnp.where(mask, inv, inv_ref[:, head(h)])
        return carry

    lax.fori_loop(low, high, one, 0)


def query_out_kernel(
    lens, place, qr_ref, q_ref, g_ref, f_ref, s_ref, t_ref, inv_ref, gp_ref, peak_ref,
    out_ref, gq_ref, bt_ref, num_ref, gs_ref, tr_ref,
):
    rows = g_ref.shape[0]
    chains = Chains(lens, place, rows)
    share = jnp.exp(gp_ref[...] - peak_ref[...])
    low, high = chains.present()

    def one(c, carry):
        mask = chains.mask(c)
        for h in range(H):
            at = head(h)
            value_sum = s_ref[c * H + h, M : M + 1, :]
            state = RATIO * (share[h : h + 1, :] * s_ref[c * H + h, :M, :] + EPS * value_sum)
            state = split(state)
            num = dot3(split(qr_ref[:, at] + EPS * RATIO), state, NN)
            g = g_ref[:, at]
            gs = dot(g, state[0], NT) + dot(g, state[1], NT)
            num_ref[:, at] = jnp.where(mask, num, num_ref[:, at])
            gs_ref[:, at] = jnp.where(mask, gs, gs_ref[:, at])
            tr_ref[:, at] = jnp.where(mask, t_ref[pl.ds(c * H + h, 1), :], tr_ref[:, at])
        return carry

    lax.fori_loop(low, high, one, 0)
    masks = [chains.mask(c) for c in range(CHAINS)]
    feats = split(f_ref[...])
    for h in range(H):
        at = head(h)
        inv = inv_ref[:, at]
        exact = num_ref[:, at] * inv
        out_ref[:, at] = exact.astype(BF16)
        grad_denom = -jnp.sum(g_ref[:, at].astype(F32) * exact, axis=1, keepdims=True) * inv
        raised = qr_ref[:, at]
        weighted = (raised + EPS * RATIO) * grad_denom
        for c in range(CHAINS):
            bt_ref[c * H + h : c * H + h + 1, :] = jnp.sum(
                jnp.where(masks[c], weighted, 0.0), axis=0, keepdims=True
            )
        grad_logits = (gs_ref[:, at] * inv + grad_denom * tr_ref[:, at]) * raised
        back = dot3(split(grad_logits), feats, NN)
        back = back - jnp.sum(grad_logits, axis=1, keepdims=True) * (SCALE * q_ref[:, at].astype(F32))
        gq_ref[:, at] = (back * SCALE).astype(BF16)


def key_out_kernel(
    lens, place, kl_ref, k_ref, v_ref, f_ref, b_ref, all_ref, peak_ref,
    gk_ref, gv_ref, dk_ref, dv_ref, bt_ref,
):
    rows = v_ref.shape[0]
    chains = Chains(lens, place, rows)
    bt_ref[...] = jnp.sum(all_ref[...], axis=0)
    low, high = chains.present()

    def one(c, carry):
        mask = chains.mask(c)
        for h in range(H):
            at = head(h)
            state = split(b_ref[c * H + h])
            feats = jnp.exp(kl_ref[:, at] - peak_ref[h : h + 1, :]) * RATIO + EPS * RATIO
            dv = dot3(split(feats), state, NN)
            v = v_ref[:, at]
            dk = dot(v, state[0], NT) + dot(v, state[1], NT) + bt_ref[pl.ds(c * H + h, 1), :]
            dv_ref[:, at] = jnp.where(mask, dv, dv_ref[:, at])
            dk_ref[:, at] = jnp.where(mask, dk, dk_ref[:, at])
        return carry

    lax.fori_loop(low, high, one, 0)
    feats = split(f_ref[...])
    for h in range(H):
        at = head(h)
        gv_ref[:, at] = dv_ref[:, at].astype(BF16)
        grad_logits = dk_ref[:, at] * (jnp.exp(kl_ref[:, at] - peak_ref[h : h + 1, :]) * RATIO)
        back = dot3(split(grad_logits), feats, NN)
        back = back - jnp.sum(grad_logits, axis=1, keepdims=True) * (SCALE * k_ref[:, at].astype(F32))
        gk_ref[:, at] = (back * SCALE).astype(BF16)


def call(kernel, shapes, args, scalars=0, scratch=(), flops=10**8):
    vmem = pl.BlockSpec(memory_space=pltpu.VMEM)
    smem = pl.BlockSpec(memory_space=pltpu.SMEM)
    size = sum(a.size * a.dtype.itemsize for a in args)
    return pl.pallas_call(
        kernel,
        out_shape=shapes,
        in_specs=[smem] * scalars + [vmem] * (len(args) - scalars),
        out_specs=[vmem] * len(shapes),
        scratch_shapes=list(scratch),
        compiler_params=pltpu.CompilerParams(vmem_limit_bytes=40 * 2**20),
        cost_estimate=pl.CostEstimate(flops=flops, bytes_accessed=size, transcendentals=10**5),
    )(*args)


def max_over(x, axis):
    count = lax.axis_size(axis)
    span = 1
    while span < count:
        steps = range(span, min(4 * span, count), span)
        others = [
            lax.ppermute(x, axis, [(i, (i + s) % count) for i in range(count)]) for s in steps
        ]
        for other in others:
            x = jnp.maximum(x, other)
        span *= 4
    return x


def on_device(queries, keys, values, grad_attended, features, chain_lengths):
    rows, width = queries.shape[1:]
    q, k, v, g = (a.reshape(rows, width) for a in (queries, keys, values, grad_attended))
    place = lax.axis_index("seq").astype(jnp.int32).reshape(1)
    where = (chain_lengths, place)
    lots = CHAINS * H
    wide = jax.ShapeDtypeStruct((rows, width), F32)
    narrow = jax.ShapeDtypeStruct((rows, width), BF16)
    small = jax.ShapeDtypeStruct((lots, D), F32)
    logits, payload = call(
        key_kernel, [wide, jax.ShapeDtypeStruct((lots + H, D), F32)], (*where, k, features), 2
    )
    gathered = lax.all_gather(payload, "seq")
    group_peak = jnp.max(gathered[:, lots:, :], axis=0)
    (states,) = call(
        state_kernel, [jax.ShapeDtypeStruct((lots, M + 8, D), F32)], (*where, logits, v, group_peak), 2
    )
    states = lax.psum_scatter(states, "seq", scatter_dimension=0, tiled=True)
    states = lax.all_gather(states, "seq", tiled=True)
    peak = max_over(group_peak, "grp")
    raised, sums = call(query_kernel, [wide, small], (q, features, gathered, group_peak))
    backs, totals, inverse = call(
        back_kernel,
        [jax.ShapeDtypeStruct((lots, M, D), F32), small, wide],
        (*where, raised, g, sums, group_peak, peak),
        2,
    )
    backs = lax.psum(backs, "seq")
    scratch = pltpu.VMEM((rows, width), F32)
    attended, grad_queries, back_totals = call(
        query_out_kernel,
        [narrow, narrow, small],
        (*where, raised, q, g, features, states, totals, inverse, group_peak, peak),
        2,
        [scratch] * 3,
    )
    back_totals = lax.all_gather(back_totals, "seq")
    grad_keys, grad_values = call(
        key_out_kernel,
        [narrow, narrow],
        (*where, logits, k, v, features, backs, back_totals, peak),
        2,
        [scratch] * 2 + [pltpu.VMEM((lots, D), F32)],
    )
    return tuple(a.reshape(1, rows, width) for a in (attended, grad_queries, grad_keys, grad_values))


def solution(mesh):
    rows = P("grp", "seq", None)
    return jax.shard_map(
        on_device,
        mesh=mesh,
        in_specs=(rows, rows, rows, rows, P(), P("grp", None)),
        out_specs=(rows, rows, rows, rows),
        check_vma=False,
    )
```

time: 717 us -> 359 us (0.50)
  the two profiles are of different devices: /device:TPU:63 before, /device:TPU:1 now
where the time goes in v1:
time: 359 us; the launch traced here: 358 us
  waiting for transfers between devices  241 us (67%)
  blocking collectives  53.3 us (15%)
  starting transfers between devices  30.1 us (8%)
  between operations  13.9 us (4%)
  Pallas kernels  13.1 us (4%)
  local copies, waits for them, and re-layouts  6.63 us (2%)
    psum x1, waiting for transfers between devices, on_device(): backs = lax.psum(backs, 'seq')  111 us
    unnamed x4, waiting for transfers between devices  99.1 us
    ppermute x6, starting transfers between devices, max_over(): lax.ppermute(x, axis, [(i, (i + s) % count) for i in range(count)])  30 us
    all_gather x1, blocking collectives, on_device(): gathered = lax.all_gather(payload, 'seq')  28.6 us
    all_gather x1, blocking collectives, on_device(): back_totals = lax.all_gather(back_totals, 'seq')  24.7 us
    all_gather x1, waiting for transfers between devices, on_device(): states = lax.all_gather(states, 'seq', tiled=True)  23.8 us
    pallas_call x6, Pallas kernels, call(): pl.pallas_call(kernel, out_shape=shapes, in_specs=[smem] * scalars + [vme...  13.1 us
  transfers between devices with their start and end apart: 9, of which 5 were waited for; matrix products, arithmetic and copies ran while one was open for 0% of the time, Pallas kernels for 2%

profile of v1, /device:TPU:1, one launch (start us, length us, event | category | flops | bytes accessed | tf_op | source)
XLA Modules:
  0.0 357.8 jit_solution(16606948750536476217)
XLA Ops:
  7.2 0.0 reduce-scatter.4.cloned.1.call-start
  7.2 0.0 copy-start.6
  7.2 0.8 copy-done.6
  8.1 0.0 copy-start.8
  8.1 0.9 copy-done.8
  9.0 0.0 copy-start.10
  9.0 0.7 copy-done.10
  9.7 1.5 shard_map.93
  11.2 28.6 %all-gather = f32[1280,128]{1,0:T(8,128)S(1)} all-gather(f32[40,128]{1,0:T(8,128)S(1)} %get-tuple-element.16), channel_id=2, replica_groups=mesh['grp'=16,'seq'=32] {'seq'}, dimensions={0}, use_global_device_ids=true | all-gather | bytes 675840 | tf_op jit(solution)/shard_map/all_gather | solution.py:291
  39.8 0.0 copy-start.4
  39.8 0.9 copy-done.4
  40.7 0.0 copy-start.3
  40.7 0.0 copy-start.7
  40.7 2.6 shard_map.95
  43.3 0.0 copy-start.2
  43.3 0.0 reduce-scatter.4.cloned.1.call-update
  43.3 0.0 all-gather.4.cloned.1.call-start
  43.4 99.1 %reduce-scatter.4.cloned.1.call-done = f32[1,136,128]{2,1,0:T(8,128)} async-done(((f32[32,136,128]{2,1,0:T(8,128)}), f32[1,136,128]{2,1,0:T(8,128)}) %reduce-scatter.4.cloned.1.call-update) | async-done | bytes 69648
  142.5 0.0 all-gather.4.cloned.1.call-update
  142.5 0.0 all-reduce.3.cloned.1.call-start
  142.6 5.1 %collective-permute-start.2 = (f32[8,128]{1,0:T(8,128)S(1)}, f32[8,128]{1,0:T(8,128)S(1)}, u32[]{:S(2)}, u32[]{:S(2)}) collective-permute-start(f32[8,128]{1,0:T(8,128)S(1)} %slice_reduce_fusion.gp_ref), channel_id=1, source_target_pairs={{0,96},{32,128},{64,160},{96,192},{128,224},{160,256},{192,288},{2... | collective-permute-start | bytes 12296 | tf_op jit(solution)/shard_map/ppermute | solution.py:271
  147.7 5.4 %collective-permute-start.1 = (f32[8,128]{1,0:T(8,128)S(1)}, f32[8,128]{1,0:T(8,128)S(1)}, u32[]{:S(2)}, u32[]{:S(2)}) collective-permute-start(f32[8,128]{1,0:T(8,128)S(1)} %slice_reduce_fusion.gp_ref), channel_id=1, source_target_pairs={{0,64},{32,96},{64,128},{96,160},{128,192},{160,224},{192,256},{22... | collective-permute-start | bytes 12296 | tf_op jit(solution)/shard_map/ppermute | solution.py:271
  153.1 3.2 collective-permute-start
  156.3 0.0 collective-permute-done.2
  156.3 0.0 collective-permute-done.1
  156.3 2.4 collective-permute-done
  158.7 2.2 collective-permute-start.5
  160.9 11.3 %collective-permute-start.4 = (f32[8,128]{1,0:T(8,128)S(1)}, f32[8,128]{1,0:T(8,128)S(1)}, u32[]{:S(2)}, u32[]{:S(2)}) collective-permute-start(f32[8,128]{1,0:T(8,128)S(1)} %maximum_maximum_fusion.1), channel_id=1, source_target_pairs={{0,256},{32,288},{64,320},{96,352},{128,384},{160,416},{192,448},{... | collective-permute-start | bytes 12296 | tf_op jit(solution)/shard_map/ppermute | solution.py:271
  172.2 2.8 collective-permute-start.3
  175.0 0.0 copy-done.3
  175.0 0.0 copy-done.7
  175.0 1.1 shard_map.94
  176.2 0.0 collective-permute-done.5
  176.2 0.0 collective-permute-done.4
  176.2 4.2 %collective-permute-done.3 = f32[8,128]{1,0:T(8,128)S(1)} collective-permute-done((f32[8,128]{1,0:T(8,128)S(1)}, f32[8,128]{1,0:T(8,128)S(1)}, u32[]{:S(2)}, u32[]{:S(2)}) %collective-permute-start.3) | collective-permute-done | bytes 4128 | tf_op jit(solution)/shard_map/ppermute | solution.py:271
  180.4 0.0 copy-done.2
  180.4 0.0 copy-done.11
  180.4 2.6 shard_map.96
  183.0 0.0 all-reduce.3.cloned.1.call-update
  183.1 23.8 %all-gather.4.cloned.1.call-done.s_ref = f32[32,136,128]{2,1,0:T(8,128)} async-done(((f32[1,136,128]{2,1,0:T(8,128)}), f32[32,136,128]{2,1,0:T(8,128)}) %all-gather.4.cloned.1.call-update) | async-done | bytes 2228240 | tf_op jit(solution)/shard_map/all_gather | solution.py:297
  206.9 1.6 copy-done
  208.5 2.8 shard_map.97
  211.3 24.7 %all-gather.1 = f32[1024,128]{1,0:T(8,128)S(1)} all-gather(f32[32,128]{1,0:T(8,128)S(1)} %get-tuple-element.25), channel_id=3, replica_groups=mesh['grp'=16,'seq'=32] {'seq'}, dimensions={0}, use_global_device_ids=true | all-gather | bytes 540672 | tf_op jit(solution)/shard_map/all_gather | solution.py:315
  236.0 111.1 %all-reduce.3.cloned.1.call-done.b_ref = f32[32,128,128]{2,1,0:T(8,128)} async-done(((f32[32,128,128]{2,1,0:T(8,128)}), f32[32,128,128]{2,1,0:T(8,128)}) %all-reduce.3.cloned.1.call-update) | async-done | bytes 2097168 | tf_op jit(solution)/shard_map/psum | solution.py:306
  347.2 0.0 copy-done.5
  347.2 0.0 copy-done.9
  347.2 1.6 copy-done.1
  348.8 2.5 shard_map.98
  (8 shorter events, 0.1 us)
Async XLA Ops:
  7.2 135.3 %reduce-scatter.4.cloned.1.call-start = ((), (), s32[]{:S(2)}) async-start(), calls=%async_computation.3 | async-start | bytes 2297856
  7.2 0.8 copy-start.6
  8.1 0.9 copy-start.8
  9.0 0.7 copy-start.10
  39.8 1.0 copy-start.4
  40.7 134.3 %copy-start.3 = (bf16[1,128,1024]{2,1,0:T(8,128)(2,1)S(1)}, bf16[1,128,1024]{2,1,0:T(8,128)(2,1)}, u32[]{:S(2)}) copy-start(bf16[1,128,1024]{2,1,0:T(8,128)(2,1)} %param.6) | copy-start | bytes 786436
  40.7 134.3 %copy-start.7 = (f32[128,128]{1,0:T(8,128)S(1)}, f32[128,128]{1,0:T(8,128)}, u32[]{:S(2)}) copy-start(f32[128,128]{1,0:T(8,128)} %f_ref.7) | copy-start | bytes 196612
  43.3 137.1 %copy-start.2 = (bf16[1,128,1024]{2,1,0:T(8,128)(2,1)S(1)}, bf16[1,128,1024]{2,1,0:T(8,128)(2,1)}, u32[]{:S(2)}) copy-start(bf16[1,128,1024]{2,1,0:T(8,128)(2,1)} %param.9) | copy-start | bytes 786436
  43.3 137.1 %copy-start.11 = (s32[1,4]{1,0:T(1,128)S(1)}, s32[1,4]{1,0:T(1,128)}, u32[]{:S(2)}) copy-start(s32[1,4]{1,0:T(1,128)} %lens.9) | copy-start | bytes 52
  43.3 163.5 %all-gather.4.cloned.1.call-start = ((), (), s32[]{:S(2)}) async-start(), calls=%async_computation.1 | async-start | bytes 2297856 | tf_op jit(solution)/shard_map/all_gather | solution.py:297
  142.5 204.7 %all-reduce.3.cloned.1.call-start = ((), (), s32[]{:S(2)}) async-start(), calls=%async_computation.2 | async-start | bytes 4194304 | tf_op jit(solution)/shard_map/psum | solution.py:306
  142.6 13.8 %collective-permute-start.2 = (f32[8,128]{1,0:T(8,128)S(1)}, f32[8,128]{1,0:T(8,128)S(1)}, u32[]{:S(2)}, u32[]{:S(2)}) collective-permute-start(f32[8,128]{1,0:T(8,128)S(1)} %slice_reduce_fusion.gp_ref), channel_id=1, source_target_pairs={{0,96},{32,128},{64,160},{96,192},{128,224},{160,256},{192,288},{2... | collective-permute-start | bytes 12296 | tf_op jit(solution)/shard_map/ppermute | solution.py:271
  147.7 8.6 %collective-permute-start.1 = (f32[8,128]{1,0:T(8,128)S(1)}, f32[8,128]{1,0:T(8,128)S(1)}, u32[]{:S(2)}, u32[]{:S(2)}) collective-permute-start(f32[8,128]{1,0:T(8,128)S(1)} %slice_reduce_fusion.gp_ref), channel_id=1, source_target_pairs={{0,64},{32,96},{64,128},{96,160},{128,192},{160,224},{192,256},{22... | collective-permute-start | bytes 12296 | tf_op jit(solution)/shard_map/ppermute | solution.py:271
  153.1 5.6 %collective-permute-start = (f32[8,128]{1,0:T(8,128)S(1)}, f32[8,128]{1,0:T(8,128)S(1)}, u32[]{:S(2)}, u32[]{:S(2)}) collective-permute-start(f32[8,128]{1,0:T(8,128)S(1)} %slice_reduce_fusion.gp_ref), channel_id=1, source_target_pairs={{0,32},{32,64},{64,96},{96,128},{128,160},{160,192},{192,224},{224... | collective-permute-start | bytes 12296 | tf_op jit(solution)/shard_map/ppermute | solution.py:271
  158.7 17.5 %collective-permute-start.5 = (f32[8,128]{1,0:T(8,128)S(1)}, f32[8,128]{1,0:T(8,128)S(1)}, u32[]{:S(2)}, u32[]{:S(2)}) collective-permute-start(f32[8,128]{1,0:T(8,128)S(1)} %maximum_maximum_fusion.1), channel_id=1, source_target_pairs={{0,384},{32,416},{64,448},{96,480},{128,0},{160,32},{192,64},{224,... | collective-permute-start | bytes 12296 | tf_op jit(solution)/shard_map/ppermute | solution.py:271
  160.9 15.3 %collective-permute-start.4 = (f32[8,128]{1,0:T(8,128)S(1)}, f32[8,128]{1,0:T(8,128)S(1)}, u32[]{:S(2)}, u32[]{:S(2)}) collective-permute-start(f32[8,128]{1,0:T(8,128)S(1)} %maximum_maximum_fusion.1), channel_id=1, source_target_pairs={{0,256},{32,288},{64,320},{96,352},{128,384},{160,416},{192,448},{... | collective-permute-start | bytes 12296 | tf_op jit(solution)/shard_map/ppermute | solution.py:271
  172.2 8.3 %collective-permute-start.3 = (f32[8,128]{1,0:T(8,128)S(1)}, f32[8,128]{1,0:T(8,128)S(1)}, u32[]{:S(2)}, u32[]{:S(2)}) collective-permute-start(f32[8,128]{1,0:T(8,128)S(1)} %maximum_maximum_fusion.1), channel_id=1, source_target_pairs={{0,128},{32,160},{64,192},{96,224},{128,256},{160,288},{192,320},{... | collective-permute-start | bytes 12296 | tf_op jit(solution)/shard_map/ppermute | solution.py:271
  183.0 164.1 %copy-start.5 = (bf16[1,128,1024]{2,1,0:T(8,128)(2,1)S(1)}, bf16[1,128,1024]{2,1,0:T(8,128)(2,1)}, u32[]{:S(2)}) copy-start(bf16[1,128,1024]{2,1,0:T(8,128)(2,1)} %param.8) | copy-start | bytes 786436
  183.0 164.1 %copy-start.9 = (bf16[1,128,1024]{2,1,0:T(8,128)(2,1)S(1)}, bf16[1,128,1024]{2,1,0:T(8,128)(2,1)}, u32[]{:S(2)}) copy-start(bf16[1,128,1024]{2,1,0:T(8,128)(2,1)} %param.7) | copy-start | bytes 786436
  206.9 1.6 copy-start
  347.2 1.6 copy-start.1
Sparse Core Ops, SparseCore 0:
  43.5 98.9 reduce-scatter.3
  145.7 61.1 all-gather.3
  210.1 136.9 all-reduce.2

commit v2 on v1

v2 whole, which is shorter than its diff:
```python
import jax
import jax.numpy as jnp
from jax import lax
from jax.experimental import pallas as pl
from jax.experimental.pallas import tpu as pltpu
from jax.sharding import Mesh
from jax.sharding import PartitionSpec as P

H = 8
D = 128
M = 128
CHAINS = 4
EPS = 1e-06
SCALE = D ** (-0.25)
RATIO = M ** (-0.5)
F32 = jnp.float32
BF16 = jnp.bfloat16
NN = (((1,), (0,)), ((), ()))
NT = (((1,), (1,)), ((), ()))
TN = (((0,), (0,)), ((), ()))
K, V, Q, G = range(4)
OUT, GQ, GK, GV = range(4)


def dot(a, b, dims):
    return lax.dot_general(a, b, dims, preferred_element_type=F32)


def split(x):
    hi = x.astype(BF16)
    return hi, (x - hi.astype(F32)).astype(BF16)


def split3(x):
    hi = x.astype(BF16)
    rest = x - hi.astype(F32)
    mid = rest.astype(BF16)
    return hi, mid, (rest - mid.astype(F32)).astype(BF16)


def dot3(a, b, dims):
    (ah, al), (bh, bl) = a, b
    return dot(ah, bh, dims) + (dot(ah, bl, dims) + dot(al, bh, dims))


def head(h):
    return slice(h * D, (h + 1) * D)


def logits_of(x, parts):
    f1, f2, f3 = parts
    y = x.astype(BF16)
    z = dot(y, f1, NT) + (dot(y, f2, NT) + dot(y, f3, NT))
    return SCALE * z - (0.5 * SCALE * SCALE) * jnp.sum(x * x, axis=1, keepdims=True)


class Chains:
    def __init__(self, lens, place, blocks, rows):
        self.rows = rows
        self.span = blocks * rows
        self.me = place[0]
        l0, l1, l2 = lens[0, 0], lens[0, 1], lens[0, 2]
        self.starts = (jnp.int32(0), l0, l0 + l1, l0 + l1 + l2)
        self.lens = lens

    def count_ended(self, position):
        c = jnp.int32(0)
        for s in self.starts[1:]:
            c = c + (position >= s).astype(jnp.int32)
        return c

    def ends_of(self, which):
        return self.count_ended(which * self.span), self.count_ended((which + 1) * self.span - 1)

    def start_of(self, c):
        s = self.starts
        return jnp.where(c == 0, s[0], jnp.where(c == 1, s[1], jnp.where(c == 2, s[2], s[3])))

    def mask(self, c, block):
        low = self.start_of(c) - (self.me * self.span + block * self.rows)
        at = lax.broadcasted_iota(jnp.int32, (self.rows, D), 0)
        return (at >= low) & (at < low + self.lens[0, c])


def pack_kernel(k_ref, v_ref, q_ref, g_ref, out_ref):
    for h in range(H):
        for i, ref in enumerate((k_ref, v_ref, q_ref, g_ref)):
            out_ref[h, i] = ref[:, head(h)].astype(F32)


def logit_kernel(lens, place, all_ref, f_ref, kl_ref, qr_ref, pay_ref):
    blocks, _, rows, _ = all_ref.shape
    chains = Chains(lens, place, blocks, rows)
    parts = split3(f_ref[...])
    for b in range(blocks):
        kl_ref[b] = logits_of(all_ref[b, K], parts)
    peak = jnp.max(jnp.max(kl_ref[...], axis=0), axis=(0, 1), keepdims=True)
    pay_ref[...] = jnp.broadcast_to(peak, pay_ref.shape)
    low, high = chains.ends_of(chains.me)

    pay_ref[0:CHAINS, :] = jnp.zeros((CHAINS, M), F32)

    def one(c, carry):
        total = jnp.zeros((rows, M), F32)
        for b in range(blocks):
            total = total + jnp.where(chains.mask(c, b), jnp.exp(kl_ref[b] - peak), 0.0)
        pay_ref[pl.ds(c, 1), :] = jnp.sum(total, axis=0, keepdims=True)
        return carry

    lax.fori_loop(low, high + 1, one, 0)
    for b in range(blocks):
        ql = logits_of(all_ref[b, Q], parts)
        qr_ref[b] = jnp.exp(ql - jnp.max(ql, axis=1, keepdims=True)) * RATIO


def state_kernel(
    lens, place, all_ref, kl_ref, qr_ref, pay_ref,
    kr_ref, inv_ref, t_ref, s_ref, b_ref, s_send, b_send,
):
    blocks, _, rows, _ = all_ref.shape
    chains = Chains(lens, place, blocks, rows)
    lots = pay_ref.shape[1]
    peaks = pay_ref[:, :, CHAINS : CHAINS + 1, :]
    peak = jnp.max(peaks, axis=(0, 1)).reshape(1, M)
    total = jnp.zeros((CHAINS, M), F32)
    for r in range(lots):
        mine = pay_ref[place[1], r]
        total = total + jnp.exp(mine[CHAINS : CHAINS + 1, :] - peak) * mine[:CHAINS, :]
    for c in range(CHAINS):
        count = lens[0, c].astype(F32)
        t_ref[c : c + 1, :] = RATIO * (total[c : c + 1, :] + EPS * count)
    for b in range(blocks):
        kr_ref[b] = jnp.exp(kl_ref[b] - peak) * RATIO
    s_ref[...] = jnp.zeros_like(s_ref)
    b_ref[...] = jnp.zeros_like(b_ref)
    low, high = chains.ends_of(chains.me)

    def one(c, carry):
        state = jnp.zeros((M, D), F32)
        back = jnp.zeros((M, D), F32)
        weights = t_ref[pl.ds(c, 1), :]
        for b in range(blocks):
            mask = chains.mask(c, b)
            hi, lo = split(jnp.where(mask, kr_ref[b] + EPS * RATIO, 0.0))
            v = all_ref[b, V].astype(BF16)
            state = state + (dot(hi, v, TN) + dot(lo, v, TN))
            qf = qr_ref[b] + EPS * RATIO
            inv = 1.0 / jnp.sum(qf * weights, axis=1, keepdims=True)
            hi, lo = split(jnp.where(mask, qf * inv, 0.0))
            g = all_ref[b, G].astype(BF16)
            back = back + (dot(hi, g, TN) + dot(lo, g, TN))
            inv_ref[b] = jnp.where(mask, inv, inv_ref[b])
        s_ref[c] = state
        b_ref[c] = back
        return carry

    lax.fori_loop(low, high + 1, one, 0)
    other = (high != low).astype(F32)
    s_send[0] = s_ref[low]
    b_send[0] = b_ref[low]
    s_send[1] = s_ref[high] * other
    b_send[1] = b_ref[high] * other


def add_rows(chains, full_ref, own_ref, sent_ref):
    full_ref[...] = own_ref[...]
    for r in range(sent_ref.shape[0]):
        low, high = chains.ends_of(r)

        @pl.when(chains.me != r)
        def _():
            full_ref[low] += sent_ref[r, 0]
            full_ref[high] += sent_ref[r, 1]


def middle_kernel(
    lens, place, all_ref, f_ref, qr_ref, kr_ref, inv_ref, t_ref, s_ref, b_ref, s_sent, b_sent,
    res_ref, dk_ref, bt_ref, s_full, b_full, num_ref, gs_ref, tr_ref,
):
    blocks, _, rows, _ = all_ref.shape
    chains = Chains(lens, place, blocks, rows)
    add_rows(chains, s_full, s_ref, s_sent)
    add_rows(chains, b_full, b_ref, b_sent)
    low, high = chains.ends_of(chains.me)

    def one(c, carry):
        state = split(s_full[c])
        back = split(b_full[c])
        for b in range(blocks):
            mask = chains.mask(c, b)
            num = dot3(split(qr_ref[b] + EPS * RATIO), state, NN)
            num_ref[b] = jnp.where(mask, num, num_ref[b])
            g = all_ref[b, G].astype(BF16)
            gs = dot(g, state[0], NT) + dot(g, state[1], NT)
            gs_ref[b] = jnp.where(mask, gs, gs_ref[b])
            tr_ref[b] = jnp.where(mask, t_ref[pl.ds(c, 1), :], tr_ref[b])
            dv = dot3(split(kr_ref[b] + EPS * RATIO), back, NN)
            res_ref[b, GV] = jnp.where(mask, dv, res_ref[b, GV])
            v = all_ref[b, V].astype(BF16)
            dk = dot(v, back[0], NT) + dot(v, back[1], NT)
            dk_ref[b] = jnp.where(mask, dk, dk_ref[b])
        return carry

    lax.fori_loop(low, high + 1, one, 0)
    feats = split(f_ref[...])
    for b in range(blocks):
        inv = inv_ref[b]
        exact = num_ref[b] * inv
        res_ref[b, OUT] = exact
        res_ref[b, GK] = exact
        grad_denom = -jnp.sum(all_ref[b, G] * exact, axis=1, keepdims=True) * inv
        raised = qr_ref[b]
        num_ref[b] = (raised + EPS * RATIO) * grad_denom
        grad_logits = (gs_ref[b] * inv + grad_denom * tr_ref[b]) * raised
        back = dot3(split(grad_logits), feats, NN)
        back = back - jnp.sum(grad_logits, axis=1, keepdims=True) * (SCALE * all_ref[b, Q])
        res_ref[b, GQ] = back * SCALE
    bt_ref[...] = jnp.zeros_like(bt_ref)

    def two(c, carry):
        total = jnp.zeros((rows, M), F32)
        for b in range(blocks):
            total = total + jnp.where(chains.mask(c, b), num_ref[b], 0.0)
        bt_ref[pl.ds(c, 1), :] = jnp.sum(total, axis=0, keepdims=True)
        return carry

    lax.fori_loop(low, high + 1, two, 0)


def key_kernel(lens, place, all_ref, f_ref, kr_ref, dk_ref, res_in, bt_ref, res_ref, sum_ref, add_ref):
    blocks, _, rows, _ = all_ref.shape
    chains = Chains(lens, place, blocks, rows)
    sum_ref[...] = jnp.sum(bt_ref[...], axis=0)
    low, high = chains.ends_of(chains.me)

    def one(c, carry):
        for b in range(blocks):
            add_ref[b] = jnp.where(chains.mask(c, b), sum_ref[pl.ds(c, 1), :], add_ref[b])
        return carry

    lax.fori_loop(low, high + 1, one, 0)
    feats = split(f_ref[...])
    for b in range(blocks):
        for i in (OUT, GQ, GV):
            res_ref[b, i] = res_in[b, i]
        grad_logits = (dk_ref[b] + add_ref[b]) * kr_ref[b]
        back = dot3(split(grad_logits), feats, NN)
        back = back - jnp.sum(grad_logits, axis=1, keepdims=True) * (SCALE * all_ref[b, K])
        res_ref[b, GK] = back * SCALE


def unpack_kernel(res_ref, out_ref, gq_ref, gk_ref, gv_ref):
    for h in range(H):
        for i, ref in ((OUT, out_ref), (GQ, gq_ref), (GK, gk_ref), (GV, gv_ref)):
            ref[:, head(h)] = res_ref[h, i].astype(BF16)


def call(kernel, shapes, args, scalars=0, scratch=()):
    vmem = pl.BlockSpec(memory_space=pltpu.VMEM)
    smem = pl.BlockSpec(memory_space=pltpu.SMEM)
    return pl.pallas_call(
        kernel,
        out_shape=shapes,
        in_specs=[smem] * scalars + [vmem] * (len(args) - scalars),
        out_specs=[vmem] * len(shapes),
        scratch_shapes=list(scratch),
        compiler_params=pltpu.CompilerParams(vmem_limit_bytes=40 * 2**20),
    )(*args)


def f32(*shape):
    return jax.ShapeDtypeStruct(shape, F32)


def on_device(queries, keys, values, grad_attended, features, chain_lengths):
    rows, width = queries.shape[1:]
    q, k, v, g = (a.reshape(rows, width) for a in (queries, keys, values, grad_attended))
    place = jnp.stack([lax.axis_index("row"), lax.axis_index("grp")]).astype(jnp.int32)
    where = (chain_lengths, place)
    blocks = lax.axis_size("col")
    wide = (blocks, rows, D)
    (packed,) = call(pack_kernel, [f32(H, 4, rows, D)], (k, v, q, g))
    own = lax.all_to_all(packed, "col", 0, 0, tiled=True)
    logits, raised, payload = call(
        logit_kernel, [f32(*wide), f32(*wide), f32(2 * CHAINS, M)], (*where, own, features), 2
    )
    payload = lax.all_gather(payload, ("grp", "row"))
    payload = payload.reshape(lax.axis_size("grp"), lax.axis_size("row"), 2 * CHAINS, M)
    lots = (CHAINS, M, D)
    key_raised, inverse, totals, states, backs, state_ends, back_ends = call(
        state_kernel,
        [f32(*wide), f32(*wide), f32(CHAINS, M), f32(*lots), f32(*lots), f32(2, M, D), f32(2, M, D)],
        (*where, own, logits, raised, payload),
        2,
    )
    state_ends = lax.all_gather(state_ends, "row")
    back_ends = lax.all_gather(back_ends, "row")
    results, grad_feats, back_totals = call(
        middle_kernel,
        [f32(blocks, 4, rows, D), f32(*wide), f32(2 * CHAINS, M)],
        (*where, own, features, raised, key_raised, inverse, totals, states, backs, state_ends, back_ends),
        2,
        [pltpu.VMEM(lots, F32)] * 2 + [pltpu.VMEM(wide, F32)] * 3,
    )
    back_totals = lax.all_gather(back_totals, "row")
    (results,) = call(
        key_kernel,
        [f32(blocks, 4, rows, D)],
        (*where, own, features, key_raised, grad_feats, results, back_totals),
        2,
        [pltpu.VMEM((2 * CHAINS, M), F32), pltpu.VMEM(wide, F32)],
    )
    results = lax.all_to_all(results, "col", 0, 0, tiled=True)
    outs = call(unpack_kernel, [jax.ShapeDtypeStruct((rows, width), BF16)] * 4, (results,))
    return tuple(a.reshape(1, rows, width) for a in outs)


def solution(mesh):
    groups, seq = mesh.devices.shape
    fine = Mesh(mesh.devices.reshape(groups, seq // H, H), ("grp", "row", "col"))
    rows = P("grp", ("row", "col"), None)
    return jax.shard_map(
        on_device,
        mesh=fine,
        in_specs=(rows, rows, rows, rows, P(), P("grp", None)),
        out_specs=(rows, rows, rows, rows),
        check_vma=False,
    )
```

time: 359 us -> 206 us (0.57)
  waiting for transfers between devices: 241 us -> 26.3 us
  blocking collectives: 53.3 us -> 152 us
  starting transfers between devices: 30.1 us -> 10.5 us
  between operations: 13.9 us -> 0.69 us
    psum x1 -> x0, waiting for transfers between devices: 111 us -> none  [on_device(): backs = lax.psum(backs, 'seq')]
    unnamed x4 -> x0, waiting for transfers between devices: 99.1 us -> none
    all_to_all x0 -> x1, blocking collectives: none -> 56.4 us  [on_device(): results = lax.all_to_all(results, 'col', 0, 0, tiled=True)]
    all_gather x2 -> x4, blocking collectives: 53.3 us -> 95.2 us  [the longest x1 65.2 us: on_device(): payload = lax.all_gather(payload, ('grp', 'row'))]
    ppermute x6 -> x0, starting transfers between devices: 30 us -> none  [max_over(): lax.ppermute(x, axis, [(i, (i + s) % count) for i in range(count)])]
    all_to_all x0 -> x1, waiting for transfers between devices: none -> 26.3 us  [on_device(): own = lax.all_to_all(packed, 'col', 0, 0, tiled=True)]
    all_gather x1 -> x0, waiting for transfers between devices: 23.8 us -> none  [on_device(): states = lax.all_gather(states, 'seq', tiled=True)]
    all_to_all x0 -> x1, starting transfers between devices: none -> 10.5 us  [on_device(): own = lax.all_to_all(packed, 'col', 0, 0, tiled=True)]
  transfers between devices with their start and end apart: 9 -> 1, of which waited for: 5 -> 1; matrix products, arithmetic and copies ran while one was open for 0% -> 0% of each run, Pallas kernels for 2% -> 0%
where the time goes in v2:
time: 206 us
  blocking collectives  152 us (74%)
  waiting for transfers between devices  26.3 us (13%)
  Pallas kernels  11.4 us (6%)
  starting transfers between devices  10.5 us (5%)
  local copies, waits for them, and re-layouts  5.12 us (2%)
    all_gather x1, blocking collectives, on_device(): payload = lax.all_gather(payload, ('grp', 'row'))  65.2 us
    all_to_all x1, blocking collectives, on_device(): results = lax.all_to_all(results, 'col', 0, 0, tiled=True)  56.4 us
    all_to_all x1, waiting for transfers between devices, on_device(): own = lax.all_to_all(packed, 'col', 0, 0, tiled=True)  26.3 us
    pallas_call x6, Pallas kernels, call(): pl.pallas_call(kernel, out_shape=shapes, in_specs=[smem] * scalars + [vme...  11.4 us
    all_to_all x1, starting transfers between devices, on_device(): own = lax.all_to_all(packed, 'col', 0, 0, tiled=True)  10.5 us
    all_gather x1, blocking collectives, on_device(): state_ends = lax.all_gather(state_ends, 'row')  10.5 us
    all_gather x1, blocking collectives, on_device(): back_ends = lax.all_gather(back_ends, 'row')  10.2 us
    all_gather x1, blocking collectives, on_device(): back_totals = lax.all_gather(back_totals, 'row')  9.27 us
  transfers between devices with their start and end apart: 1, of which 1 were waited for; matrix products, arithmetic and copies ran while one was open for 0% of the time, Pallas kernels for 0%

profile of v2, /device:TPU:1, one launch (start us, length us, event | category | flops | bytes accessed | tf_op | source)
XLA Modules:
  0.0 205.7 jit_solution(10958442334933433106)
XLA Ops:
  0.6 0.0 copy-start.2
  0.6 0.9 copy-done.2
  1.6 0.0 copy-start.3
  1.6 0.9 copy-done.3
  2.5 0.0 copy-start.4
  2.5 0.9 copy-done.4
  3.5 0.0 copy-start.5
  3.5 0.9 copy-done.5
  4.4 0.2 shard_map.93
  4.6 0.0 copy-start
  4.6 1.3 copy-done
  5.9 0.0 copy-start.1
  5.9 0.0 copy-start.6
  5.9 10.5 %all-to-all-start = ((f32[8,4,128,128]{3,2,1,0:T(8,128)}), f32[8,4,128,128]{3,2,1,0:T(8,128)S(1)}, u32[]{:S(2)}, u32[]{:S(2)}) async-start(f32[8,4,128,128]{3,2,1,0:T(8,128)} %copy-done), calls=%async_computation | async-start | bytes 4194304 | tf_op jit(solution)/shard_map/all_to_all | solution.py:283
  16.4 0.1 pad_add_fusion.place
  16.5 26.3 %all-to-all-done.all_ref = f32[8,4,128,128]{3,2,1,0:T(8,128)S(1)} async-done(((f32[8,4,128,128]{3,2,1,0:T(8,128)}), f32[8,4,128,128]{3,2,1,0:T(8,128)S(1)}, u32[]{:S(2)}, u32[]{:S(2)}) %all-to-all-start) | async-done | bytes 2097184 | tf_op jit(solution)/shard_map/all_to_all | solution.py:283
  42.8 0.0 copy-done.1
  42.8 0.0 copy-done.6
  42.8 2.6 %shard_map.94 = (f32[8,128,128]{2,1,0:T(8,128)S(1)}, f32[8,128,128]{2,1,0:T(8,128)S(1)}, f32[8,128]{1,0:T(8,128)S(1)}) custom-call(s32[1,4]{1,0:T(1,128)S(1)} %copy-done.6, s32[2]{0:T(128)S(1)} %pad_add_fusion.place, f32[8,4,128,128]{3,2,1,0:T(8,128)S(1)} %all-to-all-done.all_ref, f32[128,128]{1,0:T(8,128)S(1)} %copy-done.1), custom_call_target="tpu_custom_call" | custom-call | tf_op jit(solution)/shard_map/pallas_call | solution.py:261
  45.4 65.2 %all-gather = f32[512,128]{1,0:T(8,128)S(1)} all-gather(f32[8,128]{1,0:T(8,128)S(1)} %get-tuple-element.23), channel_id=2, replica_groups=mesh['grp'=16,'row'=4,'col'=8] {'grp','row'}, dimensions={0}, use_global_device_ids=true | all-gather | bytes 266240 | tf_op jit(solution)/shard_map/all_gather | solution.py:287
  110.6 2.1 %shard_map.95 = (f32[8,128,128]{2,1,0:T(8,128)S(1)}, f32[8,128,128]{2,1,0:T(8,128)S(1)}, f32[4,128]{1,0:T(4,128)S(1)}, f32[4,128,128]{2,1,0:T(8,128)S(1)}, f32[4...) custom-call(s32[1,4]{1,0:T(1,128)S(1)} %copy-done.6, s32[2]{0:T(128)S(1)} %pad_add_fusion.place, ...), custom_call_target="tpu_custom_call" | custom-call | tf_op jit(solution)/shard_map/pallas_call | solution.py:261
  112.7 10.5 %all-gather.1 = f32[8,128,128]{2,1,0:T(8,128)S(1)} all-gather(f32[2,128,128]{2,1,0:T(8,128)S(1)} %get-tuple-element.29), channel_id=3, replica_groups=mesh['grp'=16,'row'=4,'col'=8] {'row'}, dimensions={0}, use_global_device_ids=true | all-gather | bytes 655360 | tf_op jit(solution)/shard_map/all_gather | solution.py:296
  123.2 10.2 %all-gather.2 = f32[8,128,128]{2,1,0:T(8,128)S(1)} all-gather(f32[2,128,128]{2,1,0:T(8,128)S(1)} %get-tuple-element.30), channel_id=4, replica_groups=mesh['grp'=16,'row'=4,'col'=8] {'row'}, dimensions={0}, use_global_device_ids=true | all-gather | bytes 655360 | tf_op jit(solution)/shard_map/all_gather | solution.py:297
  133.4 4.3 %shard_map.96 = (f32[8,4,128,128]{3,2,1,0:T(8,128)S(1)}, f32[8,128,128]{2,1,0:T(8,128)S(1)}, f32[8,128]{1,0:T(8,128)S(1)}) custom-call(s32[1,4]{1,0:T(1,128)S(1)} %copy-done.6, s32[2]{0:T(128)S(1)} %pad_add_fusion.place, f32[8,4,128,128]{3,2,1,0:T(8,128)S(1)} %all-to-all-done.all_ref, f32[128,128]{1,0:T(8,128)S(1)} %copy-done.1, ...), custom_call_target="tpu_custom_call" | custom-call | tf_op jit(solution)/shard_map/pallas_call | solution.py:261
  137.7 9.3 %all-gather.3 = f32[32,128]{1,0:T(8,128)S(1)} all-gather(f32[8,128]{1,0:T(8,128)S(1)} %get-tuple-element.33), channel_id=5, replica_groups=mesh['grp'=16,'row'=4,'col'=8] {'row'}, dimensions={0}, use_global_device_ids=true | all-gather | bytes 20480 | tf_op jit(solution)/shard_map/all_gather | solution.py:305
  146.9 1.1 shard_map.97
  148.1 56.4 %all_to_all.10.res_ref = f32[8,4,128,128]{3,2,1,0:T(8,128)S(1)} all-to-all(f32[8,4,128,128]{3,2,1,0:T(8,128)S(1)} %shard_map.97), channel_id=1, replica_groups=mesh['grp'=16,'row'=4,'col'=8] {'col'}, dimensions={0} | all-to-all | bytes 4194304 | tf_op jit(solution)/shard_map/all_to_all | solution.py:313
  204.5 1.2 shard_map.98
Async XLA Ops:
  0.6 1.0 copy-start.2
  1.6 0.9 copy-start.3
  2.5 0.9 copy-start.4
  3.5 0.9 copy-start.5
  4.6 1.3 copy-start
  5.9 36.9 %copy-start.1 = (f32[128,128]{1,0:T(8,128)S(1)}, f32[128,128]{1,0:T(8,128)}, u32[]{:S(2)}) copy-start(f32[128,128]{1,0:T(8,128)} %f_ref.5) | copy-start | bytes 196612
  5.9 36.9 %copy-start.6 = (s32[1,4]{1,0:T(1,128)S(1)}, s32[1,4]{1,0:T(1,128)}, u32[]{:S(2)}) copy-start(s32[1,4]{1,0:T(1,128)} %lens.7) | copy-start | bytes 52
  5.9 36.9 %all-to-all-start = ((f32[8,4,128,128]{3,2,1,0:T(8,128)}), f32[8,4,128,128]{3,2,1,0:T(8,128)S(1)}, u32[]{:S(2)}, u32[]{:S(2)}) async-start(f32[8,4,128,128]{3,2,1,0:T(8,128)} %copy-done), calls=%async_computation | async-start | bytes 4194304 | tf_op jit(solution)/shard_map/all_to_all | solution.py:283

commit v3 on v2

--- a/solution.py
+++ b/solution.py
@@ -19,7 +19,7 @@
 NT = (((1,), (1,)), ((), ()))
 TN = (((0,), (0,)), ((), ()))
 K, V, Q, G = range(4)
-OUT, GQ, GK, GV = range(4)
+OUT, GQ, GV = range(3)
 
 
 def dot(a, b, dims):
@@ -82,32 +82,54 @@
         return (at >= low) & (at < low + self.lens[0, c])
 
 
-def pack_kernel(k_ref, v_ref, q_ref, g_ref, out_ref):
+def pack_kernel(f_ref, k_hbm, v_hbm, q_hbm, g_hbm, out_hbm, peak_ref, rows_ref, wide_ref, in_sem, out_sem):
+    sources = (k_hbm, v_hbm, q_hbm, g_hbm)
+    loads = [pltpu.make_async_copy(r, rows_ref.at[i], in_sem.at[i]) for i, r in enumerate(sources)]
+    for load in loads:
+        load.start()
+    for load in loads:
+        load.wait()
+    stores = [pltpu.make_async_copy(wide_ref.at[h], out_hbm.at[h], out_sem.at[h]) for h in range(H)]
     for h in range(H):
-        for i, ref in enumerate((k_ref, v_ref, q_ref, g_ref)):
-            out_ref[h, i] = ref[:, head(h)].astype(F32)
-
-
-def logit_kernel(lens, place, all_ref, f_ref, kl_ref, qr_ref, pay_ref):
+        for i in range(4):
+            wide_ref[h, i] = rows_ref[i, :, head(h)].astype(F32)
+        stores[h].start()
+    parts = split3(f_ref[...])
+    for h in range(H):
+        logits = logits_of(rows_ref[K, :, head(h)].astype(F32), parts)
+        peak = jnp.broadcast_to(jnp.max(logits, axis=(0, 1), keepdims=True), (1, M))
+        peak_ref[0, h : h + 1, :] = peak
+    for r in range(1, peak_ref.shape[0]):
+        peak_ref[r] = peak_ref[0]
+    for store in stores:
+        store.wait()
+
+
+def logit_kernel(lens, place, all_ref, f_ref, z_ref, kl_ref, qr_ref, pay_ref):
     blocks, _, rows, _ = all_ref.shape
     chains = Chains(lens, place, blocks, rows)
     parts = split3(f_ref[...])
     for b in range(blocks):
         kl_ref[b] = logits_of(all_ref[b, K], parts)
     peak = jnp.max(jnp.max(kl_ref[...], axis=0), axis=(0, 1), keepdims=True)
-    pay_ref[...] = jnp.broadcast_to(peak, pay_ref.shape)
     low, high = chains.ends_of(chains.me)
-
-    pay_ref[0:CHAINS, :] = jnp.zeros((CHAINS, M), F32)
+    pay_ref[0] = jnp.zeros((2 * CHAINS, M), F32)
+    pay_ref[0, CHAINS : CHAINS + 1, :] = jnp.broadcast_to(peak, (1, M))
 
     def one(c, carry):
         total = jnp.zeros((rows, M), F32)
         for b in range(blocks):
             total = total + jnp.where(chains.mask(c, b), jnp.exp(kl_ref[b] - peak), 0.0)
-        pay_ref[pl.ds(c, 1), :] = jnp.sum(total, axis=0, keepdims=True)
+        pay_ref[0, pl.ds(c, 1), :] = jnp.sum(total, axis=0, keepdims=True)
         return carry
 
     lax.fori_loop(low, high + 1, one, 0)
+    peaks = jnp.max(z_ref[...], axis=0)
+    for i in range(1, pay_ref.shape[0]):
+        h = i % H
+        pay_ref[i] = pay_ref[0]
+        pay_ref[i, CHAINS + 1 : CHAINS + 2, :] = peaks[h : h + 1, :]
+    pay_ref[0, CHAINS + 1 : CHAINS + 2, :] = peaks[0:1, :]
     for b in range(blocks):
         ql = logits_of(all_ref[b, Q], parts)
         qr_ref[b] = jnp.exp(ql - jnp.max(ql, axis=1, keepdims=True)) * RATIO
@@ -115,16 +137,15 @@
 
 def state_kernel(
     lens, place, all_ref, kl_ref, qr_ref, pay_ref,
-    kr_ref, inv_ref, t_ref, s_ref, b_ref, s_send, b_send,
+    kr_ref, inv_ref, t_ref, s_ref, b_ref, send_ref,
 ):
     blocks, _, rows, _ = all_ref.shape
     chains = Chains(lens, place, blocks, rows)
-    lots = pay_ref.shape[1]
-    peaks = pay_ref[:, :, CHAINS : CHAINS + 1, :]
-    peak = jnp.max(peaks, axis=(0, 1)).reshape(1, M)
+    everyone = pay_ref.shape[0]
+    peak = jnp.max(pay_ref[...], axis=0)[CHAINS + 1 : CHAINS + 2, :]
     total = jnp.zeros((CHAINS, M), F32)
-    for r in range(lots):
-        mine = pay_ref[place[1], r]
+    for r in range(everyone // H):
+        mine = pay_ref[r * H + place[1]]
         total = total + jnp.exp(mine[CHAINS : CHAINS + 1, :] - peak) * mine[:CHAINS, :]
     for c in range(CHAINS):
         count = lens[0, c].astype(F32)
@@ -156,31 +177,31 @@
 
     lax.fori_loop(low, high + 1, one, 0)
     other = (high != low).astype(F32)
-    s_send[0] = s_ref[low]
-    b_send[0] = b_ref[low]
-    s_send[1] = s_ref[high] * other
-    b_send[1] = b_ref[high] * other
-
-
-def add_rows(chains, full_ref, own_ref, sent_ref):
+    for r in range(send_ref.shape[0]):
+        for i, ref in ((0, s_ref), (1, b_ref)):
+            send_ref[r, i, 0] = ref[low]
+            send_ref[r, i, 1] = ref[high] * other
+
+
+def add_rows(chains, full_ref, own_ref, sent_ref, which):
     full_ref[...] = own_ref[...]
     for r in range(sent_ref.shape[0]):
         low, high = chains.ends_of(r)
 
         @pl.when(chains.me != r)
         def _():
-            full_ref[low] += sent_ref[r, 0]
-            full_ref[high] += sent_ref[r, 1]
+            full_ref[low] += sent_ref[r, which, 0]
+            full_ref[high] += sent_ref[r, which, 1]
 
 
 def middle_kernel(
-    lens, place, all_ref, f_ref, qr_ref, kr_ref, inv_ref, t_ref, s_ref, b_ref, s_sent, b_sent,
+    lens, place, all_ref, f_ref, qr_ref, kr_ref, inv_ref, t_ref, s_ref, b_ref, sent_ref,
     res_ref, dk_ref, bt_ref, s_full, b_full, num_ref, gs_ref, tr_ref,
 ):
     blocks, _, rows, _ = all_ref.shape
     chains = Chains(lens, place, blocks, rows)
-    add_rows(chains, s_full, s_ref, s_sent)
-    add_rows(chains, b_full, b_ref, b_sent)
+    add_rows(chains, s_full, s_ref, sent_ref, 0)
+    add_rows(chains, b_full, b_ref, sent_ref, 1)
     low, high = chains.ends_of(chains.me)
 
     def one(c, carry):
@@ -207,7 +228,6 @@
         inv = inv_ref[b]
         exact = num_ref[b] * inv
         res_ref[b, OUT] = exact
-        res_ref[b, GK] = exact
         grad_denom = -jnp.sum(all_ref[b, G] * exact, axis=1, keepdims=True) * inv
         raised = qr_ref[b]
         num_ref[b] = (raised + EPS * RATIO) * grad_denom
@@ -215,19 +235,21 @@
         back = dot3(split(grad_logits), feats, NN)
         back = back - jnp.sum(grad_logits, axis=1, keepdims=True) * (SCALE * all_ref[b, Q])
         res_ref[b, GQ] = back * SCALE
-    bt_ref[...] = jnp.zeros_like(bt_ref)
+    bt_ref[0] = jnp.zeros(bt_ref.shape[1:], F32)
 
     def two(c, carry):
         total = jnp.zeros((rows, M), F32)
         for b in range(blocks):
             total = total + jnp.where(chains.mask(c, b), num_ref[b], 0.0)
-        bt_ref[pl.ds(c, 1), :] = jnp.sum(total, axis=0, keepdims=True)
+        bt_ref[0, pl.ds(c, 1), :] = jnp.sum(total, axis=0, keepdims=True)
         return carry
 
     lax.fori_loop(low, high + 1, two, 0)
-
-
-def key_kernel(lens, place, all_ref, f_ref, kr_ref, dk_ref, res_in, bt_ref, res_ref, sum_ref, add_ref):
+    for r in range(1, bt_ref.shape[0]):
+        bt_ref[r] = bt_ref[0]
+
+
+def key_kernel(lens, place, all_ref, f_ref, kr_ref, dk_ref, bt_ref, res_ref, sum_ref, add_ref):
     blocks, _, rows, _ = all_ref.shape
     chains = Chains(lens, place, blocks, rows)
     sum_ref[...] = jnp.sum(bt_ref[...], axis=0)
@@ -241,18 +263,17 @@
     lax.fori_loop(low, high + 1, one, 0)
     feats = split(f_ref[...])
     for b in range(blocks):
-        for i in (OUT, GQ, GV):
-            res_ref[b, i] = res_in[b, i]
         grad_logits = (dk_ref[b] + add_ref[b]) * kr_ref[b]
         back = dot3(split(grad_logits), feats, NN)
         back = back - jnp.sum(grad_logits, axis=1, keepdims=True) * (SCALE * all_ref[b, K])
-        res_ref[b, GK] = back * SCALE
-
-
-def unpack_kernel(res_ref, out_ref, gq_ref, gk_ref, gv_ref):
+        res_ref[b] = back * SCALE
+
+
+def unpack_kernel(res_ref, key_ref, out_ref, gq_ref, gk_ref, gv_ref):
     for h in range(H):
-        for i, ref in ((OUT, out_ref), (GQ, gq_ref), (GK, gk_ref), (GV, gv_ref)):
+        for i, ref in ((OUT, out_ref), (GQ, gq_ref), (GV, gv_ref)):
             ref[:, head(h)] = res_ref[h, i].astype(BF16)
+        gk_ref[:, head(h)] = key_ref[h].astype(BF16)
 
 
 def call(kernel, shapes, args, scalars=0, scratch=()):
@@ -275,43 +296,62 @@
 def on_device(queries, keys, values, grad_attended, features, chain_lengths):
     rows, width = queries.shape[1:]
     q, k, v, g = (a.reshape(rows, width) for a in (queries, keys, values, grad_attended))
-    place = jnp.stack([lax.axis_index("row"), lax.axis_index("grp")]).astype(jnp.int32)
+    place = jnp.stack([lax.axis_index("row"), lax.axis_index("col")]).astype(jnp.int32)
     where = (chain_lengths, place)
-    blocks = lax.axis_size("col")
+    groups, lines, blocks = (lax.axis_size(a) for a in ("grp", "row", "col"))
     wide = (blocks, rows, D)
-    (packed,) = call(pack_kernel, [f32(H, 4, rows, D)], (k, v, q, g))
+    hbm = pl.BlockSpec(memory_space=pltpu.HBM)
+    vmem = pl.BlockSpec(memory_space=pltpu.VMEM)
+    packed, peaks = pl.pallas_call(
+        pack_kernel,
+        out_shape=[f32(H, 4, rows, D), f32(groups, H, M)],
+        in_specs=[vmem] + [hbm] * 4,
+        out_specs=[hbm, vmem],
+        scratch_shapes=[
+            pltpu.VMEM((4, rows, width), BF16),
+            pltpu.VMEM((H, 4, rows, D), F32),
+            pltpu.SemaphoreType.DMA((4,)),
+            pltpu.SemaphoreType.DMA((H,)),
+        ],
+        compiler_params=pltpu.CompilerParams(vmem_limit_bytes=40 * 2**20),
+    )(features, k, v, q, g)
     own = lax.all_to_all(packed, "col", 0, 0, tiled=True)
+    peaks = lax.all_to_all(peaks, "grp", 0, 0, tiled=True)
     logits, raised, payload = call(
-        logit_kernel, [f32(*wide), f32(*wide), f32(2 * CHAINS, M)], (*where, own, features), 2
-    )
-    payload = lax.all_gather(payload, ("grp", "row"))
-    payload = payload.reshape(lax.axis_size("grp"), lax.axis_size("row"), 2 * CHAINS, M)
+        logit_kernel,
+        [f32(*wide), f32(*wide), f32(lines * blocks, 2 * CHAINS, M)],
+        (*where, own, features, peaks),
+        2,
+    )
+    payload = lax.all_to_all(payload, ("row", "col"), 0, 0, tiled=True)
     lots = (CHAINS, M, D)
-    key_raised, inverse, totals, states, backs, state_ends, back_ends = call(
+    key_raised, inverse, totals, states, backs, ends = call(
         state_kernel,
-        [f32(*wide), f32(*wide), f32(CHAINS, M), f32(*lots), f32(*lots), f32(2, M, D), f32(2, M, D)],
+        [f32(*wide), f32(*wide), f32(CHAINS, M), f32(*lots), f32(*lots), f32(lines, 2, 2, M, D)],
         (*where, own, logits, raised, payload),
         2,
     )
-    state_ends = lax.all_gather(state_ends, "row")
-    back_ends = lax.all_gather(back_ends, "row")
+    ends = lax.all_to_all(ends, "row", 0, 0, tiled=True)
     results, grad_feats, back_totals = call(
         middle_kernel,
-        [f32(blocks, 4, rows, D), f32(*wide), f32(2 * CHAINS, M)],
-        (*where, own, features, raised, key_raised, inverse, totals, states, backs, state_ends, back_ends),
+        [f32(blocks, 3, rows, D), f32(*wide), f32(lines, 2 * CHAINS, M)],
+        (*where, own, features, raised, key_raised, inverse, totals, states, backs, ends),
         2,
         [pltpu.VMEM(lots, F32)] * 2 + [pltpu.VMEM(wide, F32)] * 3,
     )
-    back_totals = lax.all_gather(back_totals, "row")
-    (results,) = call(
+    results = lax.all_to_all(results, "col", 0, 0, tiled=True)
+    back_totals = lax.all_to_all(back_totals, "row", 0, 0, tiled=True)
+    (grad_keys,) = call(
         key_kernel,
-        [f32(blocks, 4, rows, D)],
-        (*where, own, features, key_raised, grad_feats, results, back_totals),
+        [f32(*wide)],
+        (*where, own, features, key_raised, grad_feats, back_totals),
         2,
         [pltpu.VMEM((2 * CHAINS, M), F32), pltpu.VMEM(wide, F32)],
     )
-    results = lax.all_to_all(results, "col", 0, 0, tiled=True)
-    outs = call(unpack_kernel, [jax.ShapeDtypeStruct((rows, width), BF16)] * 4, (results,))
+    grad_keys = lax.all_to_all(grad_keys, "col", 0, 0, tiled=True)
+    outs = call(
+        unpack_kernel, [jax.ShapeDtypeStruct((rows, width), BF16)] * 4, (results, grad_keys)
+    )
     return tuple(a.reshape(1, rows, width) for a in outs)
 
 

time: 206 us -> 156 us (0.76)
  blocking collectives: 152 us -> 103 us
  starting transfers between devices: 10.5 us -> 6.55 us
    all_gather x4 -> x0, blocking collectives: 95.2 us -> none  [the longest x1 65.2 us: on_device(): payload = lax.all_gather(payload, ('grp', 'row'))]
    all_to_all x0 -> x5, blocking collectives: none -> 78.4 us  [the longest x1 27.1 us: on_device(): peaks = lax.all_to_all(peaks, 'grp', 0, 0, tiled=True)]
    all_to_all x1, blocking collectives: 56.4 us -> 24.2 us  [on_device(): results = lax.all_to_all(results, 'col', 0, 0, tiled=True)]
    all_to_all x1, starting transfers between devices: 10.5 us -> 6.55 us  [on_device(): own = lax.all_to_all(packed, 'col', 0, 0, tiled=True)]
    unnamed x14 -> x16, local copies, waits for them, and re-layouts: 5.12 us -> 5.97 us
    pallas_call x6 -> x5, Pallas kernels: 11.4 us -> 11.4 us  [call(): pl.pallas_call(kernel, out_shape=shapes, in_specs=[smem] * scalars + [vme...]
where the time goes in v3:
time: 156 us; the launch traced here: 155 us
  blocking collectives  103 us (66%)
  waiting for transfers between devices  26.3 us (17%)
  Pallas kernels  12.8 us (8%)
  starting transfers between devices  6.55 us (4%)
  local copies, waits for them, and re-layouts  5.97 us (4%)
    all_to_all x1, blocking collectives, on_device(): peaks = lax.all_to_all(peaks, 'grp', 0, 0, tiled=True)  27.1 us
    all_to_all x1, waiting for transfers between devices, on_device(): own = lax.all_to_all(packed, 'col', 0, 0, tiled=True)  26.3 us
    all_to_all x1, blocking collectives, on_device(): results = lax.all_to_all(results, 'col', 0, 0, tiled=True)  24.2 us
    all_to_all x1, blocking collectives, on_device(): ends = lax.all_to_all(ends, 'row', 0, 0, tiled=True)  17.2 us
    all_to_all x1, blocking collectives, on_device(): grad_keys = lax.all_to_all(grad_keys, 'col', 0, 0, tiled=True)  14.2 us
    all_to_all x1, blocking collectives, on_device(): payload = lax.all_to_all(payload, ('row', 'col'), 0, 0, tiled=True)  13.4 us
    pallas_call x5, Pallas kernels, call(): pl.pallas_call(kernel, out_shape=shapes, in_specs=[smem] * scalars + [vme...  11.4 us
    all_to_all x1, blocking collectives, on_device(): back_totals = lax.all_to_all(back_totals, 'row', 0, 0, tiled=True)  6.56 us
  transfers between devices with their start and end apart: 1, of which 1 were waited for; matrix products, arithmetic and copies ran while one was open for 0% of the time, Pallas kernels for 0%

profile of v3, /device:TPU:1, one launch (start us, length us, event | category | flops | bytes accessed | tf_op | source)
XLA Modules:
  0.0 155.0 jit_solution(6207480375418816480)
XLA Ops:
  0.6 0.0 copy-start.1
  0.6 0.8 copy-done.1
  1.5 0.0 copy-start.3
  1.5 0.9 copy-done.3
  2.4 0.0 copy-start.4
  2.4 0.9 copy-done.4
  3.4 0.0 copy-start.5
  3.4 0.9 copy-done.5
  4.3 0.0 copy-start.6
  4.3 0.9 copy-done.6
  5.3 1.5 shard_map.93
  6.7 0.0 copy-start
  6.7 1.3 copy-done
  8.1 27.1 %all_to_all.35.z_ref = f32[16,8,128]{2,1,0:T(8,128)S(1)} all-to-all(f32[16,8,128]{2,1,0:T(8,128)S(1)} %get-tuple-element.23), channel_id=1, replica_groups=mesh['grp'=16,'row'=4,'col'=8] {'grp'}, dimensions={0} | all-to-all | bytes 131072 | tf_op jit(solution)/shard_map/all_to_all | solution.py:319
  35.2 0.0 copy-start.2
  35.2 0.0 copy-start.7
  35.2 6.6 %all-to-all-start = ((f32[8,4,128,128]{3,2,1,0:T(8,128)}), f32[8,4,128,128]{3,2,1,0:T(8,128)S(1)}, u32[]{:S(2)}, u32[]{:S(2)}) async-start(f32[8,4,128,128]{3,2,1,0:T(8,128)} %copy-done), calls=%async_computation | async-start | bytes 4194304 | tf_op jit(solution)/shard_map/all_to_all | solution.py:318
  41.7 0.1 pad_add_fusion.place
  41.8 26.3 %all-to-all-done.all_ref = f32[8,4,128,128]{3,2,1,0:T(8,128)S(1)} async-done(((f32[8,4,128,128]{3,2,1,0:T(8,128)}), f32[8,4,128,128]{3,2,1,0:T(8,128)S(1)}, u32[]{:S(2)}, u32[]{:S(2)}) %all-to-all-start) | async-done | bytes 2097184 | tf_op jit(solution)/shard_map/all_to_all | solution.py:318
  68.1 0.0 copy-done.2
  68.1 0.0 copy-done.7
  68.1 2.6 %shard_map.94 = (f32[8,128,128]{2,1,0:T(8,128)S(1)}, f32[8,128,128]{2,1,0:T(8,128)S(1)}, f32[32,8,128]{2,1,0:T(8,128)S(1)}) custom-call(s32[1,4]{1,0:T(1,128)S(1)} %copy-done.7, s32[2]{0:T(128)S(1)} %pad_add_fusion.place, f32[8,4,128,128]{3,2,1,0:T(8,128)S(1)} %all-to-all-done.all_ref, f32[128,128]{1,0:T(8,128)S(1)} %copy-done.2, ...), custom_call_target="tpu_custom_call" | custom-call | tf_op jit(solution)/shard_map/pallas_call | solution.py:282
  70.6 13.4 %all_to_all.36.pay_ref = f32[32,8,128]{2,1,0:T(8,128)S(1)} all-to-all(f32[32,8,128]{2,1,0:T(8,128)S(1)} %get-tuple-element.26), channel_id=1, replica_groups=mesh['grp'=16,'row'=4,'col'=8] {'row','col'}, dimensions={0} | all-to-all | bytes 262144 | tf_op jit(solution)/shard_map/all_to_all | solution.py:326
  84.0 2.2 %shard_map.95 = (f32[8,128,128]{2,1,0:T(8,128)S(1)}, f32[8,128,128]{2,1,0:T(8,128)S(1)}, f32[4,128]{1,0:T(4,128)S(1)}, f32[4,128,128]{2,1,0:T(8,128)S(1)}, f32[4...) custom-call(s32[1,4]{1,0:T(1,128)S(1)} %copy-done.7, s32[2]{0:T(128)S(1)} %pad_add_fusion.place, ...), custom_call_target="tpu_custom_call" | custom-call | tf_op jit(solution)/shard_map/pallas_call | solution.py:282
  86.2 17.2 %all_to_all.37.sent_ref = f32[4,2,2,128,128]{4,3,2,1,0:T(8,128)S(1)} all-to-all(f32[4,2,2,128,128]{4,3,2,1,0:T(8,128)S(1)} %get-tuple-element.32), channel_id=1, replica_groups=mesh['grp'=16,'row'=4,'col'=8] {'row'}, dimensions={0} | all-to-all | bytes 2097152 | tf_op jit(solution)/shard_map/all_to_all | solution.py:334
  103.4 4.3 %shard_map.96 = (f32[8,3,128,128]{3,2,1,0:T(8,128)S(1)}, f32[8,128,128]{2,1,0:T(8,128)S(1)}, f32[4,8,128]{2,1,0:T(8,128)S(1)}) custom-call(s32[1,4]{1,0:T(1,128)S(1)} %copy-done.7, s32[2]{0:T(128)S(1)} %pad_add_fusion.place, f32[8,4,128,128]{3,2,1,0:T(8,128)S(1)} %all-to-all-done.all_ref, f32[128,128]{1,0:T(8,128)S(1)} %copy-done.2, ...), custom_call_target="tpu_custom_call" | custom-call | tf_op jit(solution)/shard_map/pallas_call | solution.py:282
  107.7 6.6 %all_to_all.38.bt_ref = f32[4,8,128]{2,1,0:T(8,128)S(1)} all-to-all(f32[4,8,128]{2,1,0:T(8,128)S(1)} %get-tuple-element.35), channel_id=1, replica_groups=mesh['grp'=16,'row'=4,'col'=8] {'row'}, dimensions={0} | all-to-all | bytes 32768 | tf_op jit(solution)/shard_map/all_to_all | solution.py:343
  114.3 1.1 shard_map.97
  115.4 14.2 %all_to_all.39.key_ref = f32[8,128,128]{2,1,0:T(8,128)S(1)} all-to-all(f32[8,128,128]{2,1,0:T(8,128)S(1)} %shard_map.97), channel_id=1, replica_groups=mesh['grp'=16,'row'=4,'col'=8] {'col'}, dimensions={0} | all-to-all | bytes 1048576 | tf_op jit(solution)/shard_map/all_to_all | solution.py:351
  129.5 24.2 %all_to_all.40.res_ref = f32[8,3,128,128]{3,2,1,0:T(8,128)S(1)} all-to-all(f32[8,3,128,128]{3,2,1,0:T(8,128)S(1)} %get-tuple-element.33), channel_id=1, replica_groups=mesh['grp'=16,'row'=4,'col'=8] {'col'}, dimensions={0} | all-to-all | bytes 3145728 | tf_op jit(solution)/shard_map/all_to_all | solution.py:342
  153.8 1.2 shard_map.98
Async XLA Ops:
  0.6 0.8 copy-start.1
  1.5 0.9 copy-start.3
  2.4 0.9 copy-start.4
  3.4 0.9 copy-start.5
  4.3 0.9 copy-start.6
  6.7 1.3 copy-start
  35.2 32.9 %copy-start.2 = (f32[128,128]{1,0:T(8,128)S(1)}, f32[128,128]{1,0:T(8,128)}, u32[]{:S(2)}) copy-start(f32[128,128]{1,0:T(8,128)} %f_ref.7) | copy-start | bytes 196612
  35.2 32.9 %copy-start.7 = (s32[1,4]{1,0:T(1,128)S(1)}, s32[1,4]{1,0:T(1,128)}, u32[]{:S(2)}) copy-start(s32[1,4]{1,0:T(1,128)} %lens.7) | copy-start | bytes 52
  35.2 32.9 %all-to-all-start = ((f32[8,4,128,128]{3,2,1,0:T(8,128)}), f32[8,4,128,128]{3,2,1,0:T(8,128)S(1)}, u32[]{:S(2)}, u32[]{:S(2)}) async-start(f32[8,4,128,128]{3,2,1,0:T(8,128)} %copy-done), calls=%async_computation | async-start | bytes 4194304 | tf_op jit(solution)/shard_map/all_to_all | solution.py:318

commit v4 on v3

--- a/solution.py
+++ b/solution.py
@@ -19,7 +19,8 @@
 NT = (((1,), (1,)), ((), ()))
 TN = (((0,), (0,)), ((), ()))
 K, V, Q, G = range(4)
-OUT, GQ, GV = range(3)
+OUT, GQ = range(2)
+GK, GV = range(2)
 
 
 def dot(a, b, dims):
@@ -98,14 +99,12 @@
     for h in range(H):
         logits = logits_of(rows_ref[K, :, head(h)].astype(F32), parts)
         peak = jnp.broadcast_to(jnp.max(logits, axis=(0, 1), keepdims=True), (1, M))
-        peak_ref[0, h : h + 1, :] = peak
-    for r in range(1, peak_ref.shape[0]):
-        peak_ref[r] = peak_ref[0]
+        peak_ref[h : h + 1, :] = peak
     for store in stores:
         store.wait()
 
 
-def logit_kernel(lens, place, all_ref, f_ref, z_ref, kl_ref, qr_ref, pay_ref):
+def logit_kernel(lens, place, all_ref, f_ref, kl_ref, qr_ref, base_ref):
     blocks, _, rows, _ = all_ref.shape
     chains = Chains(lens, place, blocks, rows)
     parts = split3(f_ref[...])
@@ -113,31 +112,32 @@
         kl_ref[b] = logits_of(all_ref[b, K], parts)
     peak = jnp.max(jnp.max(kl_ref[...], axis=0), axis=(0, 1), keepdims=True)
     low, high = chains.ends_of(chains.me)
-    pay_ref[0] = jnp.zeros((2 * CHAINS, M), F32)
-    pay_ref[0, CHAINS : CHAINS + 1, :] = jnp.broadcast_to(peak, (1, M))
+    base_ref[...] = jnp.zeros_like(base_ref)
+    base_ref[CHAINS : CHAINS + 1, :] = jnp.broadcast_to(peak, (1, M))
 
     def one(c, carry):
         total = jnp.zeros((rows, M), F32)
         for b in range(blocks):
             total = total + jnp.where(chains.mask(c, b), jnp.exp(kl_ref[b] - peak), 0.0)
-        pay_ref[0, pl.ds(c, 1), :] = jnp.sum(total, axis=0, keepdims=True)
+        base_ref[pl.ds(c, 1), :] = jnp.sum(total, axis=0, keepdims=True)
         return carry
 
     lax.fori_loop(low, high + 1, one, 0)
-    peaks = jnp.max(z_ref[...], axis=0)
-    for i in range(1, pay_ref.shape[0]):
-        h = i % H
-        pay_ref[i] = pay_ref[0]
-        pay_ref[i, CHAINS + 1 : CHAINS + 2, :] = peaks[h : h + 1, :]
-    pay_ref[0, CHAINS + 1 : CHAINS + 2, :] = peaks[0:1, :]
     for b in range(blocks):
         ql = logits_of(all_ref[b, Q], parts)
         qr_ref[b] = jnp.exp(ql - jnp.max(ql, axis=1, keepdims=True)) * RATIO
 
 
+def payload_kernel(base_ref, peak_ref, pay_ref):
+    row = lax.broadcasted_iota(jnp.int32, base_ref.shape, 0)
+    for i in range(pay_ref.shape[0]):
+        h = i % H
+        pay_ref[i] = jnp.where(row == CHAINS + 1, peak_ref[h : h + 1, :], base_ref[...])
+
+
 def state_kernel(
     lens, place, all_ref, kl_ref, qr_ref, pay_ref,
-    kr_ref, inv_ref, t_ref, s_ref, b_ref, send_ref,
+    kr_ref, inv_ref, t_ref, s_ref, b_ref, s_send, b_send,
 ):
     blocks, _, rows, _ = all_ref.shape
     chains = Chains(lens, place, blocks, rows)
@@ -177,36 +177,33 @@
 
     lax.fori_loop(low, high + 1, one, 0)
     other = (high != low).astype(F32)
-    for r in range(send_ref.shape[0]):
-        for i, ref in ((0, s_ref), (1, b_ref)):
-            send_ref[r, i, 0] = ref[low]
-            send_ref[r, i, 1] = ref[high] * other
-
-
-def add_rows(chains, full_ref, own_ref, sent_ref, which):
+    for ref, send in ((s_ref, s_send), (b_ref, b_send)):
+        send[0] = ref[low]
+        send[1] = ref[high] * other
+
+
+def add_rows(chains, full_ref, own_ref, sent_ref):
     full_ref[...] = own_ref[...]
     for r in range(sent_ref.shape[0]):
         low, high = chains.ends_of(r)
 
         @pl.when(chains.me != r)
         def _():
-            full_ref[low] += sent_ref[r, which, 0]
-            full_ref[high] += sent_ref[r, which, 1]
-
-
-def middle_kernel(
-    lens, place, all_ref, f_ref, qr_ref, kr_ref, inv_ref, t_ref, s_ref, b_ref, sent_ref,
-    res_ref, dk_ref, bt_ref, s_full, b_full, num_ref, gs_ref, tr_ref,
+            full_ref[low] += sent_ref[r, :M, :]
+            full_ref[high] += sent_ref[r, M : 2 * M, :]
+
+
+def query_kernel(
+    lens, place, all_ref, f_ref, qr_ref, inv_ref, t_ref, s_ref, s_sent, b_send,
+    res_ref, back_ref, full_ref, num_ref, gs_ref, tr_ref,
 ):
     blocks, _, rows, _ = all_ref.shape
     chains = Chains(lens, place, blocks, rows)
-    add_rows(chains, s_full, s_ref, sent_ref, 0)
-    add_rows(chains, b_full, b_ref, sent_ref, 1)
+    add_rows(chains, full_ref, s_ref, s_sent)
     low, high = chains.ends_of(chains.me)
 
     def one(c, carry):
-        state = split(s_full[c])
-        back = split(b_full[c])
+        state = split(full_ref[c])
         for b in range(blocks):
             mask = chains.mask(c, b)
             num = dot3(split(qr_ref[b] + EPS * RATIO), state, NN)
@@ -215,11 +212,6 @@
             gs = dot(g, state[0], NT) + dot(g, state[1], NT)
             gs_ref[b] = jnp.where(mask, gs, gs_ref[b])
             tr_ref[b] = jnp.where(mask, t_ref[pl.ds(c, 1), :], tr_ref[b])
-            dv = dot3(split(kr_ref[b] + EPS * RATIO), back, NN)
-            res_ref[b, GV] = jnp.where(mask, dv, res_ref[b, GV])
-            v = all_ref[b, V].astype(BF16)
-            dk = dot(v, back[0], NT) + dot(v, back[1], NT)
-            dk_ref[b] = jnp.where(mask, dk, dk_ref[b])
         return carry
 
     lax.fori_loop(low, high + 1, one, 0)
@@ -235,45 +227,56 @@
         back = dot3(split(grad_logits), feats, NN)
         back = back - jnp.sum(grad_logits, axis=1, keepdims=True) * (SCALE * all_ref[b, Q])
         res_ref[b, GQ] = back * SCALE
-    bt_ref[0] = jnp.zeros(bt_ref.shape[1:], F32)
+    back_ref[0:M, :] = b_send[0]
+    back_ref[M : 2 * M, :] = b_send[1]
+    back_ref[2 * M :, :] = jnp.zeros((2 * CHAINS, M), F32)
 
     def two(c, carry):
         total = jnp.zeros((rows, M), F32)
         for b in range(blocks):
             total = total + jnp.where(chains.mask(c, b), num_ref[b], 0.0)
-        bt_ref[0, pl.ds(c, 1), :] = jnp.sum(total, axis=0, keepdims=True)
+        back_ref[pl.ds(2 * M + c, 1), :] = jnp.sum(total, axis=0, keepdims=True)
         return carry
 
     lax.fori_loop(low, high + 1, two, 0)
-    for r in range(1, bt_ref.shape[0]):
-        bt_ref[r] = bt_ref[0]
-
-
-def key_kernel(lens, place, all_ref, f_ref, kr_ref, dk_ref, bt_ref, res_ref, sum_ref, add_ref):
+
+
+def key_kernel(
+    lens, place, all_ref, f_ref, kr_ref, b_ref, sent_ref, res_ref, full_ref, sum_ref, dk_ref,
+):
     blocks, _, rows, _ = all_ref.shape
     chains = Chains(lens, place, blocks, rows)
-    sum_ref[...] = jnp.sum(bt_ref[...], axis=0)
+    add_rows(chains, full_ref, b_ref, sent_ref)
+    sum_ref[...] = jnp.sum(sent_ref[:, 2 * M :, :], axis=0)
     low, high = chains.ends_of(chains.me)
 
     def one(c, carry):
-        for b in range(blocks):
-            add_ref[b] = jnp.where(chains.mask(c, b), sum_ref[pl.ds(c, 1), :], add_ref[b])
+        back = split(full_ref[c])
+        total = sum_ref[pl.ds(c, 1), :]
+        for b in range(blocks):
+            mask = chains.mask(c, b)
+            dv = dot3(split(kr_ref[b] + EPS * RATIO), back, NN)
+            res_ref[b, GV] = jnp.where(mask, dv, res_ref[b, GV])
+            v = all_ref[b, V].astype(BF16)
+            dk = dot(v, back[0], NT) + dot(v, back[1], NT) + total
+            dk_ref[b] = jnp.where(mask, dk, dk_ref[b])
         return carry
 
     lax.fori_loop(low, high + 1, one, 0)
     feats = split(f_ref[...])
     for b in range(blocks):
-        grad_logits = (dk_ref[b] + add_ref[b]) * kr_ref[b]
+        grad_logits = dk_ref[b] * kr_ref[b]
         back = dot3(split(grad_logits), feats, NN)
         back = back - jnp.sum(grad_logits, axis=1, keepdims=True) * (SCALE * all_ref[b, K])
-        res_ref[b] = back * SCALE
-
-
-def unpack_kernel(res_ref, key_ref, out_ref, gq_ref, gk_ref, gv_ref):
+        res_ref[b, GK] = back * SCALE
+
+
+def unpack_kernel(first_ref, second_ref, out_ref, gq_ref, gk_ref, gv_ref):
     for h in range(H):
-        for i, ref in ((OUT, out_ref), (GQ, gq_ref), (GV, gv_ref)):
-            ref[:, head(h)] = res_ref[h, i].astype(BF16)
-        gk_ref[:, head(h)] = key_ref[h].astype(BF16)
+        out_ref[:, head(h)] = first_ref[h, OUT].astype(BF16)
+        gq_ref[:, head(h)] = first_ref[h, GQ].astype(BF16)
+        gk_ref[:, head(h)] = second_ref[h, GK].astype(BF16)
+        gv_ref[:, head(h)] = second_ref[h, GV].astype(BF16)
 
 
 def call(kernel, shapes, args, scalars=0, scratch=()):
@@ -293,18 +296,30 @@
     return jax.ShapeDtypeStruct(shape, F32)
 
 
+def max_over(x, axis):
+    count = lax.axis_size(axis)
+    reach = 0
+    while 2 * reach + 1 < count:
+        step = min(2 * reach + 1, count // 2 - reach)
+        up = lax.ppermute(x, axis, [(i, (i + step) % count) for i in range(count)])
+        down = lax.ppermute(x, axis, [(i, (i - step) % count) for i in range(count)])
+        x = jnp.maximum(x, jnp.maximum(up, down))
+        reach += step
+    return x
+
+
 def on_device(queries, keys, values, grad_attended, features, chain_lengths):
     rows, width = queries.shape[1:]
     q, k, v, g = (a.reshape(rows, width) for a in (queries, keys, values, grad_attended))
     place = jnp.stack([lax.axis_index("row"), lax.axis_index("col")]).astype(jnp.int32)
     where = (chain_lengths, place)
-    groups, lines, blocks = (lax.axis_size(a) for a in ("grp", "row", "col"))
+    lines, blocks = (lax.axis_size(a) for a in ("row", "col"))
     wide = (blocks, rows, D)
     hbm = pl.BlockSpec(memory_space=pltpu.HBM)
     vmem = pl.BlockSpec(memory_space=pltpu.VMEM)
     packed, peaks = pl.pallas_call(
         pack_kernel,
-        out_shape=[f32(H, 4, rows, D), f32(groups, H, M)],
+        out_shape=[f32(H, 4, rows, D), f32(H, M)],
         in_specs=[vmem] + [hbm] * 4,
         out_specs=[hbm, vmem],
         scratch_shapes=[
@@ -313,45 +328,41 @@
             pltpu.SemaphoreType.DMA((4,)),
             pltpu.SemaphoreType.DMA((H,)),
         ],
-        compiler_params=pltpu.CompilerParams(vmem_limit_bytes=40 * 2**20),
+        compiler_params=pltpu.CompilerParams(vmem_limit_bytes=60 * 2**20),
     )(features, k, v, q, g)
     own = lax.all_to_all(packed, "col", 0, 0, tiled=True)
-    peaks = lax.all_to_all(peaks, "grp", 0, 0, tiled=True)
-    logits, raised, payload = call(
-        logit_kernel,
-        [f32(*wide), f32(*wide), f32(lines * blocks, 2 * CHAINS, M)],
-        (*where, own, features, peaks),
-        2,
-    )
+    peaks = max_over(peaks, "grp")
+    logits, raised, base = call(
+        logit_kernel, [f32(*wide), f32(*wide), f32(2 * CHAINS, M)], (*where, own, features), 2
+    )
+    (payload,) = call(payload_kernel, [f32(lines * blocks, 2 * CHAINS, M)], (base, peaks))
     payload = lax.all_to_all(payload, ("row", "col"), 0, 0, tiled=True)
     lots = (CHAINS, M, D)
-    key_raised, inverse, totals, states, backs, ends = call(
+    key_raised, inverse, totals, states, backs, state_ends, back_ends = call(
         state_kernel,
-        [f32(*wide), f32(*wide), f32(CHAINS, M), f32(*lots), f32(*lots), f32(lines, 2, 2, M, D)],
+        [f32(*wide), f32(*wide), f32(CHAINS, M), f32(*lots), f32(*lots), f32(2, M, D), f32(2, M, D)],
         (*where, own, logits, raised, payload),
         2,
     )
-    ends = lax.all_to_all(ends, "row", 0, 0, tiled=True)
-    results, grad_feats, back_totals = call(
-        middle_kernel,
-        [f32(blocks, 3, rows, D), f32(*wide), f32(lines, 2 * CHAINS, M)],
-        (*where, own, features, raised, key_raised, inverse, totals, states, backs, ends),
+    state_ends = lax.all_gather(state_ends.reshape(2 * M, D), "row")
+    first, back_ends = call(
+        query_kernel,
+        [f32(blocks, 2, rows, D), f32(2 * M + 2 * CHAINS, D)],
+        (*where, own, features, raised, inverse, totals, states, state_ends, back_ends),
         2,
-        [pltpu.VMEM(lots, F32)] * 2 + [pltpu.VMEM(wide, F32)] * 3,
-    )
-    results = lax.all_to_all(results, "col", 0, 0, tiled=True)
-    back_totals = lax.all_to_all(back_totals, "row", 0, 0, tiled=True)
-    (grad_keys,) = call(
+        [pltpu.VMEM(lots, F32)] + [pltpu.VMEM(wide, F32)] * 3,
+    )
+    first = lax.all_to_all(first, "col", 0, 0, tiled=True)
+    back_ends = lax.all_gather(back_ends, "row")
+    (second,) = call(
         key_kernel,
-        [f32(*wide)],
-        (*where, own, features, key_raised, grad_feats, back_totals),
+        [f32(blocks, 2, rows, D)],
+        (*where, own, features, key_raised, backs, back_ends),
         2,
-        [pltpu.VMEM((2 * CHAINS, M), F32), pltpu.VMEM(wide, F32)],
-    )
-    grad_keys = lax.all_to_all(grad_keys, "col", 0, 0, tiled=True)
-    outs = call(
-        unpack_kernel, [jax.ShapeDtypeStruct((rows, width), BF16)] * 4, (results, grad_keys)
-    )
+        [pltpu.VMEM(lots, F32), pltpu.VMEM((2 * CHAINS, M), F32), pltpu.VMEM(wide, F32)],
+    )
+    second = lax.all_to_all(second, "col", 0, 0, tiled=True)
+    outs = call(unpack_kernel, [jax.ShapeDtypeStruct((rows, width), BF16)] * 4, (first, second))
     return tuple(a.reshape(1, rows, width) for a in outs)
 
 

time: 156 us -> 138 us (0.88)
  blocking collectives: 103 us -> 61.5 us
  starting transfers between devices: 6.55 us -> 43.2 us
  waiting for transfers between devices: 26.3 us -> 11.1 us
  Pallas kernels: 12.8 us -> 18.4 us
  local copies, waits for them, and re-layouts: 5.97 us -> 1.85 us
    all_to_all x5 -> x1, blocking collectives: 89.3 us -> 21.5 us  [on_device(): second = lax.all_to_all(second, 'col', 0, 0, tiled=True)]
    all_to_all x1, waiting for transfers between devices: 26.3 us -> 0.01 us  [on_device(): own = lax.all_to_all(packed, 'col', 0, 0, tiled=True)]
    ppermute x0 -> x6, starting transfers between devices: none -> 24.7 us  [the longest x3 14 us: max_over(): lax.ppermute(x, axis, [(i, (i - step) % count) for i in range(count)])]
    all_gather x0 -> x2, blocking collectives: none -> 21.2 us  [the longest x1 11.3 us: on_device(): back_ends = lax.all_gather(back_ends, 'row')]
    ppermute x0 -> x6, waiting for transfers between devices: none -> 10.7 us  [the longest x3 10.6 us: max_over(): up = lax.ppermute(x, axis, [(i, (i + step) % count) for i in range(count)])]
    all_to_all x0 -> x1, starting transfers between devices: none -> 7.99 us  [on_device(): first = lax.all_to_all(first, 'col', 0, 0, tiled=True)]
    all_to_all x1, blocking collectives: 13.4 us -> 18.8 us  [on_device(): payload = lax.all_to_all(payload, ('row', 'col'), 0, 0, tiled=True)]
    unnamed x16 -> x10, local copies, waits for them, and re-layouts: 5.97 us -> 1.85 us
  transfers between devices with their start and end apart: 1 -> 8, of which waited for: 1 -> 4; matrix products, arithmetic and copies ran while one was open for 0% -> 0% of each run, Pallas kernels for 0% -> 2%
where the time goes in v4:
time: 138 us; the launch traced here: 137 us
  blocking collectives  61.5 us (45%)
  starting transfers between devices  43.2 us (31%)
  Pallas kernels  18.4 us (13%)
  waiting for transfers between devices  11.1 us (8%)
  local copies, waits for them, and re-layouts  1.85 us (1%)
    all_to_all x1, blocking collectives, on_device(): second = lax.all_to_all(second, 'col', 0, 0, tiled=True)  21.5 us
    all_to_all x1, blocking collectives, on_device(): payload = lax.all_to_all(payload, ('row', 'col'), 0, 0, tiled=True)  18.8 us
    ppermute x3, starting transfers between devices, max_over(): lax.ppermute(x, axis, [(i, (i - step) % count) for i in range(count)])  14 us
    pallas_call x6, Pallas kernels, call(): pl.pallas_call(kernel, out_shape=shapes, in_specs=[smem] * scalars + [vme...  13.6 us
    all_gather x1, blocking collectives, on_device(): back_ends = lax.all_gather(back_ends, 'row')  11.3 us
    ppermute x3, starting transfers between devices, max_over(): up = lax.ppermute(x, axis, [(i, (i + step) % count) for i in range(count)])  10.7 us
    ppermute x3, waiting for transfers between devices, max_over(): up = lax.ppermute(x, axis, [(i, (i + step) % count) for i in range(count)])  10.6 us
    all_to_all x1, starting transfers between devices, on_device(): own = lax.all_to_all(packed, 'col', 0, 0, tiled=True)  10.5 us
  transfers between devices with their start and end apart: 8, of which 4 were waited for; matrix products, arithmetic and copies ran while one was open for 0% of the time, Pallas kernels for 2%

profile of v4, /device:TPU:1, one launch (start us, length us, event | category | flops | bytes accessed | tf_op | source)
XLA Modules:
  0.0 136.9 jit_solution(17490636795397547346)
XLA Ops:
  0.6 4.8 %shard_map.93 = (f32[8,4,128,128]{3,2,1,0:T(8,128)}, f32[8,128]{1,0:T(8,128)}) custom-call(f32[128,128]{1,0:T(8,128)} %f_ref.7, bf16[128,1024]{1,0:T(8,128)(2,1)} %bitcast.14, bf16[128,1024]{1,0:T(8,128)(2,1)} %bitcast.15, bf16[128,1024]{1,0:T(8,128)(2,1)} %bitcast.16, bf16[128,1024]{1,0:T(8,128)(2,1)} %bitcast.17), custom_call_target="tpu_custom_call" | custom-call | tf_op jit(solution)/shard_map/pallas_call | solution.py:320
  5.4 0.0 copy-start.4
  5.4 0.0 copy-start
  5.4 0.0 copy-start.3
  5.5 10.5 %all-to-all-start = ((f32[8,4,128,128]{3,2,1,0:T(8,128)}), f32[8,4,128,128]{3,2,1,0:T(8,128)S(1)}, u32[]{:S(2)}, u32[]{:S(2)}) async-start(f32[8,4,128,128]{3,2,1,0:T(8,128)} %get-tuple-element.22), calls=%async_computation | async-start | bytes 4194304 | tf_op jit(solution)/shard_map/all_to_all | solution.py:333
  16.0 0.0 copy-done.4
  16.0 6.5 %collective-permute-start.1 = (f32[8,128]{1,0:T(8,128)S(1)}, f32[8,128]{1,0:T(8,128)S(1)}, u32[]{:S(2)}, u32[]{:S(2)}) collective-permute-start(f32[8,128]{1,0:T(8,128)S(1)} %copy-done.4), channel_id=1, source_target_pairs={{0,480},{32,0},{64,32},{96,64},{128,96},{160,128},{192,160},{224,1... | collective-permute-start | bytes 12296 | tf_op jit(solution)/shard_map/ppermute | solution.py:305
  22.5 1.9 %collective-permute-start = (f32[8,128]{1,0:T(8,128)S(1)}, f32[8,128]{1,0:T(8,128)S(1)}, u32[]{:S(2)}, u32[]{:S(2)}) collective-permute-start(f32[8,128]{1,0:T(8,128)S(1)} %copy-done.4), channel_id=1, source_target_pairs={{0,32},{32,64},{64,96},{96,128},{128,160},{160,192},{192,224},{224... | collective-permute-start | bytes 12296 | tf_op jit(solution)/shard_map/ppermute | solution.py:304
  24.5 0.0 collective-permute-done.1
  24.5 3.9 %collective-permute-done = f32[8,128]{1,0:T(8,128)S(1)} collective-permute-done((f32[8,128]{1,0:T(8,128)S(1)}, f32[8,128]{1,0:T(8,128)S(1)}, u32[]{:S(2)}, u32[]{:S(2)}) %collective-permute-start) | collective-permute-done | bytes 4128 | tf_op jit(solution)/shard_map/ppermute | solution.py:304
  28.4 2.8 %collective-permute-start.3 = (f32[8,128]{1,0:T(8,128)S(1)}, f32[8,128]{1,0:T(8,128)S(1)}, u32[]{:S(2)}, u32[]{:S(2)}) collective-permute-start(f32[8,128]{1,0:T(8,128)S(1)} %maximum_maximum_fusion.2), channel_id=1, source_target_pairs={{0,416},{32,448},{64,480},{96,0},{128,32},{160,64},{192,96},{224,1... | collective-permute-start | bytes 12296 | tf_op jit(solution)/shard_map/ppermute | solution.py:305
  31.2 4.3 %collective-permute-start.2 = (f32[8,128]{1,0:T(8,128)S(1)}, f32[8,128]{1,0:T(8,128)S(1)}, u32[]{:S(2)}, u32[]{:S(2)}) collective-permute-start(f32[8,128]{1,0:T(8,128)S(1)} %maximum_maximum_fusion.2), channel_id=1, source_target_pairs={{0,96},{32,128},{64,160},{96,192},{128,224},{160,256},{192,288},{2... | collective-permute-start | bytes 12296 | tf_op jit(solution)/shard_map/ppermute | solution.py:304
  35.5 0.0 collective-permute-done.3
  35.5 3.1 %collective-permute-done.2 = f32[8,128]{1,0:T(8,128)S(1)} collective-permute-done((f32[8,128]{1,0:T(8,128)S(1)}, f32[8,128]{1,0:T(8,128)S(1)}, u32[]{:S(2)}, u32[]{:S(2)}) %collective-permute-start.2) | collective-permute-done | bytes 4128 | tf_op jit(solution)/shard_map/ppermute | solution.py:304
  38.5 4.7 %collective-permute-start.5 = (f32[8,128]{1,0:T(8,128)S(1)}, f32[8,128]{1,0:T(8,128)S(1)}, u32[]{:S(2)}, u32[]{:S(2)}) collective-permute-start(f32[8,128]{1,0:T(8,128)S(1)} %maximum_maximum_fusion.1), channel_id=1, source_target_pairs={{0,384},{32,416},{64,448},{96,480},{128,0},{160,32},{192,64},{224,... | collective-permute-start | bytes 12296 | tf_op jit(solution)/shard_map/ppermute | solution.py:305
  43.2 4.5 %collective-permute-start.4 = (f32[8,128]{1,0:T(8,128)S(1)}, f32[8,128]{1,0:T(8,128)S(1)}, u32[]{:S(2)}, u32[]{:S(2)}) collective-permute-start(f32[8,128]{1,0:T(8,128)S(1)} %maximum_maximum_fusion.1), channel_id=1, source_target_pairs={{0,128},{32,160},{64,192},{96,224},{128,256},{160,288},{192,320},{... | collective-permute-start | bytes 12296 | tf_op jit(solution)/shard_map/ppermute | solution.py:304
  47.7 0.1 pad_add_fusion.place
  47.8 0.0 collective-permute-done.5
  47.8 3.7 %collective-permute-done.4 = f32[8,128]{1,0:T(8,128)S(1)} collective-permute-done((f32[8,128]{1,0:T(8,128)S(1)}, f32[8,128]{1,0:T(8,128)S(1)}, u32[]{:S(2)}, u32[]{:S(2)}) %collective-permute-start.4) | collective-permute-done | bytes 4128 | tf_op jit(solution)/shard_map/ppermute | solution.py:304
  51.5 0.0 all-to-all-done.all_ref
  51.5 0.0 copy-done
  51.5 0.0 copy-done.3
  51.5 2.6 %shard_map.94 = (f32[8,128,128]{2,1,0:T(8,128)S(1)}, f32[8,128,128]{2,1,0:T(8,128)S(1)}, f32[8,128]{1,0:T(8,128)S(1)}) custom-call(s32[1,4]{1,0:T(1,128)S(1)} %copy-done.3, s32[2]{0:T(128)S(1)} %pad_add_fusion.place, f32[8,4,128,128]{3,2,1,0:T(8,128)S(1)} %all-to-all-done.all_ref, f32[128,128]{1,0:T(8,128)S(1)} %copy-done), custom_call_target="tpu_custom_call" | custom-call | tf_op jit(solution)/shard_map/pallas_call | solution.py:285
  54.1 18.8 %all_to_all.20.pay_ref = f32[32,8,128]{2,1,0:T(8,128)S(1)} all-to-all(f32[32,8,128]{2,1,0:T(8,128)S(1)} %shard_map.95), channel_id=1, replica_groups=mesh['grp'=16,'row'=4,'col'=8] {'row','col'}, dimensions={0} | all-to-all | bytes 262144 | tf_op jit(solution)/shard_map/all_to_all | solution.py:339
  73.0 2.2 %shard_map.96 = (f32[8,128,128]{2,1,0:T(8,128)S(1)}, f32[8,128,128]{2,1,0:T(8,128)S(1)}, f32[4,128]{1,0:T(4,128)S(1)}, f32[4,128,128]{2,1,0:T(8,128)S(1)}, f32[4...) custom-call(s32[1,4]{1,0:T(1,128)S(1)} %copy-done.3, s32[2]{0:T(128)S(1)} %pad_add_fusion.place, ...), custom_call_target="tpu_custom_call" | custom-call | tf_op jit(solution)/shard_map/pallas_call | solution.py:285
  75.1 0.0 copy-start.1
  75.1 0.8 copy-done.1
  75.9 9.9 %all_gather.9.s_sent = f32[4,256,128]{2,1,0:T(8,128)S(1)} all-gather(f32[1,256,128]{2,1,0:T(8,128)S(1)} %bitcast.13), channel_id=1, replica_groups=mesh['grp'=16,'row'=4,'col'=8] {'row'}, dimensions={0}, use_global_device_ids=true | all-gather | bytes 655360 | tf_op jit(solution)/shard_map/all_gather | solution.py:347
  85.8 4.0 %shard_map.97 = (f32[8,2,128,128]{3,2,1,0:T(8,128)}, f32[264,128]{1,0:T(8,128)S(1)}) custom-call(s32[1,4]{1,0:T(1,128)S(1)} %copy-done.3, s32[2]{0:T(128)S(1)} %pad_add_fusion.place, f32[8,4,128,128]{3,2,1,0:T(8,128)S(1)} %all-to-all-done.all_ref, f32[128,128]{1,0:T(8,128)S(1)} %copy-done, f32[8,128,128]{2,1,0:T(8,128)S(1)} %get-tuple-element.23.qr_ref, ...), custom_call_target="tpu_custom_call" | custom-call | tf_op jit(solution)/shard_map/pallas_call | solution.py:285
  89.9 8.0 %all-to-all-start.2 = ((f32[8,2,128,128]{3,2,1,0:T(8,128)}), f32[8,2,128,128]{3,2,1,0:T(8,128)}, u32[]{:S(2)}, u32[]{:S(2)}) async-start(f32[8,2,128,128]{3,2,1,0:T(8,128)} %get-tuple-element.32), calls=%async_computation.2 | async-start | bytes 2097152 | tf_op jit(solution)/shard_map/all_to_all | solution.py:355
  97.9 11.3 %all-gather = f32[1056,128]{1,0:T(8,128)S(1)} all-gather(f32[264,128]{1,0:T(8,128)S(1)} %get-tuple-element.35), channel_id=2, replica_groups=mesh['grp'=16,'row'=4,'col'=8] {'row'}, dimensions={0}, use_global_device_ids=true | all-gather | bytes 675840 | tf_op jit(solution)/shard_map/all_gather | solution.py:356
  109.1 0.0 copy-start.2
  109.1 1.0 copy-done.2
  110.2 2.5 %shard_map.98 = f32[8,2,128,128]{3,2,1,0:T(8,128)S(1)} custom-call(s32[1,4]{1,0:T(1,128)S(1)} %copy-done.3, s32[2]{0:T(128)S(1)} %pad_add_fusion.place, f32[8,4,128,128]{3,2,1,0:T(8,128)S(1)} %all-to-all-done.all_ref, f32[128,128]{1,0:T(8,128)S(1)} %copy-done, f32[8,128,128]{2,1,0:T(8,128)S(1)} %copy-done.2, f32[4,128,128]{2,1,0:T(8,128)S(1)} %get-tuple-element.34.b_ref, ...), custom_call_target="tpu_custom_call" | custom-call | tf_op jit(solution)/shard_map/pallas_call | solution.py:285
  112.7 0.4 all-to-all-done.2.first_ref
  113.1 21.5 %all_to_all.21.second_ref = f32[8,2,128,128]{3,2,1,0:T(8,128)S(1)} all-to-all(f32[8,2,128,128]{3,2,1,0:T(8,128)S(1)} %shard_map.98), channel_id=1, replica_groups=mesh['grp'=16,'row'=4,'col'=8] {'col'}, dimensions={0} | all-to-all | bytes 2097152 | tf_op jit(solution)/shard_map/all_to_all | solution.py:364
  134.6 2.4 %shard_map.99 = (bf16[128,1024]{1,0:T(8,128)(2,1)}, bf16[128,1024]{1,0:T(8,128)(2,1)}, bf16[128,1024]{1,0:T(8,128)(2,1)}, bf16[128,1024]{1,0:T(8,128)(2,1)}) custom-call(f32[8,2,128,128]{3,2,1,0:T(8,128)} %all-to-all-done.2.first_ref, f32[8,2,128,128]{3,2,1,0:T(8,128)S(1)} %all_to_all.21.second_ref), custom_call_target="tpu_custom_call" | custom-call | tf_op jit(solution)/shard_map/pallas_call | solution.py:285
  (4 shorter events, 0.0 us)
Async XLA Ops:
  5.4 10.6 %copy-start.4 = (f32[8,128]{1,0:T(8,128)S(1)}, f32[8,128]{1,0:T(8,128)}, u32[]{:S(2)}) copy-start(f32[8,128]{1,0:T(8,128)} %get-tuple-element.26) | copy-start | bytes 12292
  5.4 46.1 %copy-start = (f32[128,128]{1,0:T(8,128)S(1)}, f32[128,128]{1,0:T(8,128)}, u32[]{:S(2)}) copy-start(f32[128,128]{1,0:T(8,128)} %f_ref.7) | copy-start | bytes 196612
  5.4 46.1 %copy-start.3 = (s32[1,4]{1,0:T(1,128)S(1)}, s32[1,4]{1,0:T(1,128)}, u32[]{:S(2)}) copy-start(s32[1,4]{1,0:T(1,128)} %lens.7) | copy-start | bytes 52
  5.5 46.0 %all-to-all-start = ((f32[8,4,128,128]{3,2,1,0:T(8,128)}), f32[8,4,128,128]{3,2,1,0:T(8,128)S(1)}, u32[]{:S(2)}, u32[]{:S(2)}) async-start(f32[8,4,128,128]{3,2,1,0:T(8,128)} %get-tuple-element.22), calls=%async_computation | async-start | bytes 4194304 | tf_op jit(solution)/shard_map/all_to_all | solution.py:333
  16.0 8.5 %collective-permute-start.1 = (f32[8,128]{1,0:T(8,128)S(1)}, f32[8,128]{1,0:T(8,128)S(1)}, u32[]{:S(2)}, u32[]{:S(2)}) collective-permute-start(f32[8,128]{1,0:T(8,128)S(1)} %copy-done.4), channel_id=1, source_target_pairs={{0,480},{32,0},{64,32},{96,64},{128,96},{160,128},{192,160},{224,1... | collective-permute-start | bytes 12296 | tf_op jit(solution)/shard_map/ppermute | solution.py:305
  22.5 5.9 %collective-permute-start = (f32[8,128]{1,0:T(8,128)S(1)}, f32[8,128]{1,0:T(8,128)S(1)}, u32[]{:S(2)}, u32[]{:S(2)}) collective-permute-start(f32[8,128]{1,0:T(8,128)S(1)} %copy-done.4), channel_id=1, source_target_pairs={{0,32},{32,64},{64,96},{96,128},{128,160},{160,192},{192,224},{224... | collective-permute-start | bytes 12296 | tf_op jit(solution)/shard_map/ppermute | solution.py:304
  28.4 7.1 %collective-permute-start.3 = (f32[8,128]{1,0:T(8,128)S(1)}, f32[8,128]{1,0:T(8,128)S(1)}, u32[]{:S(2)}, u32[]{:S(2)}) collective-permute-start(f32[8,128]{1,0:T(8,128)S(1)} %maximum_maximum_fusion.2), channel_id=1, source_target_pairs={{0,416},{32,448},{64,480},{96,0},{128,32},{160,64},{192,96},{224,1... | collective-permute-start | bytes 12296 | tf_op jit(solution)/shard_map/ppermute | solution.py:305
  31.2 7.4 %collective-permute-start.2 = (f32[8,128]{1,0:T(8,128)S(1)}, f32[8,128]{1,0:T(8,128)S(1)}, u32[]{:S(2)}, u32[]{:S(2)}) collective-permute-start(f32[8,128]{1,0:T(8,128)S(1)} %maximum_maximum_fusion.2), channel_id=1, source_target_pairs={{0,96},{32,128},{64,160},{96,192},{128,224},{160,256},{192,288},{2... | collective-permute-start | bytes 12296 | tf_op jit(solution)/shard_map/ppermute | solution.py:304
  38.5 9.3 %collective-permute-start.5 = (f32[8,128]{1,0:T(8,128)S(1)}, f32[8,128]{1,0:T(8,128)S(1)}, u32[]{:S(2)}, u32[]{:S(2)}) collective-permute-start(f32[8,128]{1,0:T(8,128)S(1)} %maximum_maximum_fusion.1), channel_id=1, source_target_pairs={{0,384},{32,416},{64,448},{96,480},{128,0},{160,32},{192,64},{224,... | collective-permute-start | bytes 12296 | tf_op jit(solution)/shard_map/ppermute | solution.py:305
  43.2 8.3 %collective-permute-start.4 = (f32[8,128]{1,0:T(8,128)S(1)}, f32[8,128]{1,0:T(8,128)S(1)}, u32[]{:S(2)}, u32[]{:S(2)}) collective-permute-start(f32[8,128]{1,0:T(8,128)S(1)} %maximum_maximum_fusion.1), channel_id=1, source_target_pairs={{0,128},{32,160},{64,192},{96,224},{128,256},{160,288},{192,320},{... | collective-permute-start | bytes 12296 | tf_op jit(solution)/shard_map/ppermute | solution.py:304
  75.1 0.8 copy-start.1
  89.9 23.2 %all-to-all-start.2 = ((f32[8,2,128,128]{3,2,1,0:T(8,128)}), f32[8,2,128,128]{3,2,1,0:T(8,128)}, u32[]{:S(2)}, u32[]{:S(2)}) async-start(f32[8,2,128,128]{3,2,1,0:T(8,128)} %get-tuple-element.32), calls=%async_computation.2 | async-start | bytes 2097152 | tf_op jit(solution)/shard_map/all_to_all | solution.py:355
  109.1 1.0 copy-start.2

commit v5 on v4

v5 whole, which is shorter than its diff:
```python
import jax
import jax.numpy as jnp
from jax import lax
from jax.experimental import pallas as pl
from jax.experimental.pallas import tpu as pltpu
from jax.sharding import Mesh
from jax.sharding import PartitionSpec as P

H = 8
D = 128
M = 128
CHAINS = 4
EPS = 1e-06
SCALE = D ** (-0.25)
RATIO = M ** (-0.5)
F32 = jnp.float32
BF16 = jnp.bfloat16
NN = (((1,), (0,)), ((), ()))
NT = (((1,), (1,)), ((), ()))
TN = (((0,), (0,)), ((), ()))
K, V, Q, G = range(4)
OUT, GQ = range(2)
GK, GV = range(2)


def dot(a, b, dims):
    return lax.dot_general(a, b, dims, preferred_element_type=F32)


def split(x):
    hi = x.astype(BF16)
    return hi, (x - hi.astype(F32)).astype(BF16)


def split3(x):
    hi = x.astype(BF16)
    rest = x - hi.astype(F32)
    mid = rest.astype(BF16)
    return hi, mid, (rest - mid.astype(F32)).astype(BF16)


def dot3(a, b, dims):
    (ah, al), (bh, bl) = a, b
    return dot(ah, bh, dims) + (dot(ah, bl, dims) + dot(al, bh, dims))


def head(h):
    return slice(h * D, (h + 1) * D)


def logits_of(x, parts):
    f1, f2, f3 = parts
    y = x.astype(BF16)
    z = dot(y, f1, NT) + (dot(y, f2, NT) + dot(y, f3, NT))
    return SCALE * z - (0.5 * SCALE * SCALE) * jnp.sum(x * x, axis=1, keepdims=True)


class Chains:
    def __init__(self, lens, me, blocks, rows):
        self.rows = rows
        self.span = blocks * rows
        self.me = me
        l0, l1, l2 = lens[0, 0], lens[0, 1], lens[0, 2]
        self.starts = (jnp.int32(0), l0, l0 + l1, l0 + l1 + l2)
        self.lens = lens

    def count_ended(self, position):
        c = jnp.int32(0)
        for s in self.starts[1:]:
            c = c + (position >= s).astype(jnp.int32)
        return c

    def ends_of(self, which):
        return self.count_ended(which * self.span), self.count_ended((which + 1) * self.span - 1)

    def start_of(self, c):
        s = self.starts
        return jnp.where(c == 0, s[0], jnp.where(c == 1, s[1], jnp.where(c == 2, s[2], s[3])))

    def mask(self, c, block):
        low = self.start_of(c) - (self.me * self.span + block * self.rows)
        at = lax.broadcasted_iota(jnp.int32, (self.rows, D), 0)
        return (at >= low) & (at < low + self.lens[0, c])


def pack_kernel(k_hbm, v_hbm, q_hbm, g_hbm, out_hbm, rows_ref, wide_ref, in_sem, out_sem):
    sources = (k_hbm, v_hbm, q_hbm, g_hbm)
    loads = [pltpu.make_async_copy(r, rows_ref.at[i], in_sem.at[i]) for i, r in enumerate(sources)]
    for load in loads:
        load.start()
    for load in loads:
        load.wait()
    stores = [pltpu.make_async_copy(wide_ref.at[h], out_hbm.at[h], out_sem.at[h]) for h in range(H)]
    for h in range(H):
        for i in range(4):
            wide_ref[h, i] = rows_ref[i, :, head(h)].astype(F32)
        stores[h].start()
    for store in stores:
        store.wait()


def total_kernel(lens, place, k_ref, f_ref, pay_ref, kl_ref):
    rows = k_ref.shape[0]
    chains = Chains(lens, place[0] * H + place[1], 1, rows)
    parts = split3(f_ref[...])
    pay_ref[: CHAINS * H, :] = jnp.zeros((CHAINS * H, M), F32)
    for h in range(H):
        logits = logits_of(k_ref[:, head(h)].astype(F32), parts)
        peak = jnp.max(logits, axis=(0, 1), keepdims=True)
        kl_ref[h] = jnp.exp(logits - peak)
        pay_ref[CHAINS * H + h : CHAINS * H + h + 1, :] = jnp.broadcast_to(peak, (1, M))
    low, high = chains.ends_of(chains.me)

    def one(c, carry):
        mask = chains.mask(c, 0)
        for h in range(H):
            total = jnp.sum(jnp.where(mask, kl_ref[h], 0.0), axis=0, keepdims=True)
            pay_ref[pl.ds(c * H + h, 1), :] = total
        return carry

    lax.fori_loop(low, high + 1, one, 0)


def state_kernel(
    lens, place, all_ref, f_ref, pay_ref,
    er_ref, qr_ref, tot_ref, z_ref, s_ref, send_ref, sums_ref,
):
    blocks, _, rows, _ = all_ref.shape
    chains = Chains(lens, place[0], blocks, rows)
    peaks = jnp.max(pay_ref[:, CHAINS * H :, :], axis=0)
    sums = [jnp.zeros((H, M), F32) for _ in range(CHAINS)]
    for d in range(pay_ref.shape[0]):
        share = jnp.exp(pay_ref[d, CHAINS * H :, :] - peaks)
        for c in range(CHAINS):
            sums[c] = sums[c] + share * pay_ref[d, c * H : (c + 1) * H, :]
    for c in range(CHAINS):
        sums_ref[c * H : (c + 1) * H, :] = sums[c]
    sums_ref[CHAINS * H :, :] = peaks
    tot_ref[...] = jnp.zeros_like(tot_ref)
    for c in range(CHAINS + 1):
        tot_ref[c : c + 1, :] = sums_ref[pl.ds(c * H + place[1], 1), :]
    peak = tot_ref[CHAINS : CHAINS + 1, :]
    for i in range(z_ref.shape[0]):
        z_ref[i] = jnp.broadcast_to(peak, z_ref.shape[1:])
    parts = split3(f_ref[...])
    for b in range(blocks):
        er_ref[b] = jnp.exp(logits_of(all_ref[b, K], parts) - peak)
        ql = logits_of(all_ref[b, Q], parts)
        qr_ref[b] = jnp.exp(ql - jnp.max(ql, axis=1, keepdims=True)) * RATIO
    s_ref[...] = jnp.zeros_like(s_ref)
    low, high = chains.ends_of(chains.me)

    def one(c, carry):
        state = jnp.zeros((M, D), F32)
        total = jnp.zeros((rows, D), F32)
        for b in range(blocks):
            mask = chains.mask(c, b)
            hi, lo = split(jnp.where(mask, er_ref[b], 0.0))
            v = all_ref[b, V]
            total = total + jnp.where(mask, v, 0.0)
            v = v.astype(BF16)
            state = state + (dot(hi, v, TN) + dot(lo, v, TN))
        s_ref[c, :M, :] = state
        s_ref[c, M : M + 1, :] = jnp.sum(total, axis=0, keepdims=True)
        return carry

    lax.fori_loop(low, high + 1, one, 0)
    send_ref[0] = s_ref[low]
    send_ref[1] = s_ref[high] * (high != low).astype(F32)


def query_kernel(
    lens, place, all_ref, f_ref, er_ref, qr_ref, tot_ref, z_ref, s_ref, s1_ref, s2_ref, s3_ref,
    res_ref, send_ref, bt_ref, b_ref, share_ref, full_ref, num_ref, gs_ref, inv_ref, tr_ref, t_ref,
):
    blocks, _, rows, _ = all_ref.shape
    chains = Chains(lens, place[0], blocks, rows)
    peak = jnp.max(jnp.max(z_ref[...], axis=0), axis=0, keepdims=True)
    share = jnp.exp(tot_ref[CHAINS : CHAINS + 1, :] - peak)
    share_ref[...] = jnp.broadcast_to(RATIO * share, share_ref.shape)
    for c in range(CHAINS):
        count = lens[0, c].astype(F32)
        t_ref[c : c + 1, :] = RATIO * (share * tot_ref[c : c + 1, :] + EPS * count)
    full_ref[...] = s_ref[...]
    for step, sent_ref in ((1, s1_ref), (2, s2_ref), (3, s3_ref)):
        ends = chains.ends_of(lax.rem(chains.me + (4 - step), 4))
        for i, c in enumerate(ends):
            full_ref[c] += sent_ref[i]
    b_ref[...] = jnp.zeros_like(b_ref)
    low, high = chains.ends_of(chains.me)

    def one(c, carry):
        state = RATIO * (share * full_ref[c, :M, :] + EPS * full_ref[c, M : M + 1, :])
        state = split(state)
        weights = t_ref[pl.ds(c, 1), :]
        back = jnp.zeros((M, D), F32)
        for b in range(blocks):
            mask = chains.mask(c, b)
            qf = qr_ref[b] + EPS * RATIO
            inv = 1.0 / jnp.sum(qf * weights, axis=1, keepdims=True)
            inv_ref[b] = jnp.where(mask, inv, inv_ref[b])
            tr_ref[b] = jnp.where(mask, weights, tr_ref[b])
            num = dot3(split(qf), state, NN)
            num_ref[b] = jnp.where(mask, num, num_ref[b])
            g = all_ref[b, G].astype(BF16)
            gs = dot(g, state[0], NT) + dot(g, state[1], NT)
            gs_ref[b] = jnp.where(mask, gs, gs_ref[b])
            hi, lo = split(jnp.where(mask, qf * inv, 0.0))
            back = back + (dot(hi, g, TN) + dot(lo, g, TN))
        b_ref[c] = back
        return carry

    lax.fori_loop(low, high + 1, one, 0)
    feats = split(f_ref[...])
    for b in range(blocks):
        inv = inv_ref[b]
        exact = num_ref[b] * inv
        res_ref[b, OUT] = exact
        grad_denom = -jnp.sum(all_ref[b, G] * exact, axis=1, keepdims=True) * inv
        raised = qr_ref[b]
        num_ref[b] = (raised + EPS * RATIO) * grad_denom
        grad_logits = (gs_ref[b] * inv + grad_denom * tr_ref[b]) * raised
        back = dot3(split(grad_logits), feats, NN)
        back = back - jnp.sum(grad_logits, axis=1, keepdims=True) * (SCALE * all_ref[b, Q])
        res_ref[b, GQ] = back * SCALE
    bt_ref[...] = jnp.zeros_like(bt_ref)

    def two(c, carry):
        total = jnp.zeros((rows, M), F32)
        for b in range(blocks):
            total = total + jnp.where(chains.mask(c, b), num_ref[b], 0.0)
        bt_ref[pl.ds(c, 1), :] = jnp.sum(total, axis=0, keepdims=True)
        return carry

    lax.fori_loop(low, high + 1, two, 0)
    send_ref[0:M, :] = b_ref[low]
    send_ref[M : 2 * M, :] = b_ref[high] * (high != low).astype(F32)
    send_ref[2 * M :, :] = bt_ref[...]


def key_kernel(
    lens, place, all_ref, f_ref, er_ref, share_ref, b_ref, sent_ref,
    res_ref, full_ref, sum_ref, dk_ref,
):
    blocks, _, rows, _ = all_ref.shape
    chains = Chains(lens, place[0], blocks, rows)
    full_ref[...] = b_ref[...]
    for r in range(sent_ref.shape[0]):
        low, high = chains.ends_of(r)

        @pl.when(chains.me != r)
        def _():
            full_ref[low] += sent_ref[r, :M, :]
            full_ref[high] += sent_ref[r, M : 2 * M, :]

    sum_ref[...] = jnp.sum(sent_ref[:, 2 * M :, :], axis=0)
    share = share_ref[0:1, :]
    low, high = chains.ends_of(chains.me)

    def one(c, carry):
        back = split(full_ref[c])
        total = sum_ref[pl.ds(c, 1), :]
        for b in range(blocks):
            mask = chains.mask(c, b)
            dv = dot3(split(er_ref[b] * share + EPS * RATIO), back, NN)
            res_ref[b, GV] = jnp.where(mask, dv, res_ref[b, GV])
            v = all_ref[b, V].astype(BF16)
            dk = dot(v, back[0], NT) + dot(v, back[1], NT) + total
            dk_ref[b] = jnp.where(mask, dk, dk_ref[b])
        return carry

    lax.fori_loop(low, high + 1, one, 0)
    feats = split(f_ref[...])
    for b in range(blocks):
        grad_logits = dk_ref[b] * (er_ref[b] * share)
        back = dot3(split(grad_logits), feats, NN)
        back = back - jnp.sum(grad_logits, axis=1, keepdims=True) * (SCALE * all_ref[b, K])
        res_ref[b, GK] = back * SCALE


def unpack_kernel(res_ref, *outs):
    for h in range(H):
        for i, out in enumerate(outs):
            out[:, head(h)] = res_ref[h, i].astype(BF16)


def call(kernel, shapes, args, scalars=0, scratch=()):
    vmem = pl.BlockSpec(memory_space=pltpu.VMEM)
    smem = pl.BlockSpec(memory_space=pltpu.SMEM)
    return pl.pallas_call(
        kernel,
        out_shape=shapes,
        in_specs=[smem] * scalars + [vmem] * (len(args) - scalars),
        out_specs=[vmem] * len(shapes),
        scratch_shapes=list(scratch),
        compiler_params=pltpu.CompilerParams(vmem_limit_bytes=40 * 2**20),
    )(*args)


def f32(*shape):
    return jax.ShapeDtypeStruct(shape, F32)


def on_device(queries, keys, values, grad_attended, features, chain_lengths):
    rows, width = queries.shape[1:]
    q, k, v, g = (a.reshape(rows, width) for a in (queries, keys, values, grad_attended))
    place = jnp.stack([lax.axis_index("row"), lax.axis_index("col")]).astype(jnp.int32)
    where = (chain_lengths, place)
    groups, lines, blocks = (lax.axis_size(a) for a in ("grp", "row", "col"))
    wide = (blocks, rows, D)
    hbm = pl.BlockSpec(memory_space=pltpu.HBM)
    packed = pl.pallas_call(
        pack_kernel,
        out_shape=f32(H, 4, rows, D),
        in_specs=[hbm] * 4,
        out_specs=hbm,
        scratch_shapes=[
            pltpu.VMEM((4, rows, width), BF16),
            pltpu.VMEM((H, 4, rows, D), F32),
            pltpu.SemaphoreType.DMA((4,)),
            pltpu.SemaphoreType.DMA((H,)),
        ],
        compiler_params=pltpu.CompilerParams(vmem_limit_bytes=60 * 2**20),
    )(k, v, q, g)
    own = lax.all_to_all(packed, "col", 0, 0, tiled=True)
    small = f32(2 * CHAINS, M)
    lots = ((CHAINS + 1) * H, M)
    (payload,) = call(
        total_kernel, [f32(*lots)], (*where, k, features), 2, [pltpu.VMEM((H, rows, M), F32)]
    )
    payload = lax.all_gather(payload, ("row", "col"))
    states = (CHAINS, M + 8, D)
    key_raised, raised, totals, peaks, own_states, ends = call(
        state_kernel,
        [f32(*wide), f32(*wide), small, f32(groups, 8, M), f32(*states), f32(2, M + 8, D)],
        (*where, own, features, payload),
        2,
        [pltpu.VMEM(lots, F32)],
    )
    sent = [
        lax.ppermute(ends, "row", [(i, (i + step) % lines) for i in range(lines)])
        for step in range(1, lines)
    ]
    peaks = lax.all_to_all(peaks, "grp", 0, 0, tiled=True)
    first, back_ends, _, backs, share = call(
        query_kernel,
        [f32(blocks, 2, rows, D), f32(2 * M + 2 * CHAINS, D), small, f32(CHAINS, M, D), small],
        (*where, own, features, key_raised, raised, totals, peaks, own_states, *sent),
        2,
        [pltpu.VMEM(states, F32)] + [pltpu.VMEM(wide, F32)] * 4 + [pltpu.VMEM((2 * CHAINS, M), F32)],
    )
    first = lax.all_to_all(first, "col", 0, 0, tiled=True)
    back_ends = lax.all_gather(back_ends, "row")
    (second,) = call(
        key_kernel,
        [f32(blocks, 2, rows, D)],
        (*where, own, features, key_raised, share, backs, back_ends),
        2,
        [pltpu.VMEM((CHAINS, M, D), F32), pltpu.VMEM((2 * CHAINS, M), F32), pltpu.VMEM(wide, F32)],
    )
    second = lax.all_to_all(second, "col", 0, 0, tiled=True)
    narrow = [jax.ShapeDtypeStruct((rows, width), BF16)] * 2
    outs = (*call(unpack_kernel, narrow, (first,)), *call(unpack_kernel, narrow, (second,)))
    return tuple(a.reshape(1, rows, width) for a in outs)


def solution(mesh):
    groups, seq = mesh.devices.shape
    fine = Mesh(mesh.devices.reshape(groups, seq // H, H), ("grp", "row", "col"))
    rows = P("grp", ("row", "col"), None)
    return jax.shard_map(
        on_device,
        mesh=fine,
        in_specs=(rows, rows, rows, rows, P(), P("grp", None)),
        out_specs=(rows, rows, rows, rows),
        check_vma=False,
    )
```

time: 138 us -> 140 us (1.014)
  waiting for transfers between devices: 11.1 us -> 21.2 us
  blocking collectives: 61.5 us -> 53 us
  local copies, waits for them, and re-layouts: 1.85 us -> 7.86 us
  Pallas kernels: 18.4 us -> 13.6 us
  starting transfers between devices: 43.2 us -> 41.7 us
    all_to_all x2 -> x0, blocking collectives: 40.3 us -> none  [the longest x1 21.5 us: on_device(): second = lax.all_to_all(second, 'col', 0, 0, tiled=True)]
    all_gather x1, blocking collectives: 9.89 us -> 41.9 us  [on_device(): payload = lax.all_gather(payload, ('row', 'col'))]
    all_to_all x0 -> x2, starting transfers between devices: none -> 18.2 us  [the longest x1 11.7 us: on_device(): peaks = lax.all_to_all(peaks, 'grp', 0, 0, tiled=True)]
    ppermute x6 -> x3, starting transfers between devices: 24.7 us -> 8.53 us  [on_device(): lax.ppermute(ends, 'row', [(i, (i + step) % lines) for i in range(lines)])]
    all_to_all x0 -> x2, waiting for transfers between devices: none -> 14.2 us  [the longest x1 14.2 us: on_device(): second = lax.all_to_all(second, 'col', 0, 0, tiled=True)]
    unnamed x10 -> x26, local copies, waits for them, and re-layouts: 1.85 us -> 7.86 us
    ppermute x6 -> x3, waiting for transfers between devices: 10.7 us -> 6.88 us  [on_device(): lax.ppermute(ends, 'row', [(i, (i + step) % lines) for i in range(lines)])]
    all_to_all x1, starting transfers between devices: 7.99 us -> 4.41 us  [on_device(): first = lax.all_to_all(first, 'col', 0, 0, tiled=True)]
  transfers between devices with their start and end apart: 8 -> 7, of which waited for: 4 -> 4; matrix products, arithmetic and copies ran while one was open for 0% -> 0% of each run, Pallas kernels for 2% -> 3%
where the time goes in v5:
time: 140 us; the launch traced here: 138 us
  blocking collectives  53 us (38%)
  starting transfers between devices  41.7 us (30%)
  waiting for transfers between devices  21.2 us (15%)
  Pallas kernels  13.6 us (10%)
  local copies, waits for them, and re-layouts  7.86 us (6%)
    all_gather x1, blocking collectives, on_device(): payload = lax.all_gather(payload, ('row', 'col'))  41.9 us
    all_to_all x1, waiting for transfers between devices, on_device(): second = lax.all_to_all(second, 'col', 0, 0, tiled=True)  14.2 us
    all_to_all x1, starting transfers between devices, on_device(): peaks = lax.all_to_all(peaks, 'grp', 0, 0, tiled=True)  11.7 us
    all_gather x1, blocking collectives, on_device(): back_ends = lax.all_gather(back_ends, 'row')  11.2 us
    pallas_call x6, Pallas kernels, call(): pl.pallas_call(kernel, out_shape=shapes, in_specs=[smem] * scalars + [vme...  11 us
    all_to_all x1, starting transfers between devices, on_device(): own = lax.all_to_all(packed, 'col', 0, 0, tiled=True)  10.5 us
    ppermute x3, starting transfers between devices, on_device(): lax.ppermute(ends, 'row', [(i, (i + step) % lines) for i in range(lines)])  8.53 us
    unnamed x26, local copies, waits for them, and re-layouts  7.86 us
  transfers between devices with their start and end apart: 7, of which 4 were waited for; matrix products, arithmetic and copies ran while one was open for 0% of the time, Pallas kernels for 3%

profile of v5, /device:TPU:1, one launch (start us, length us, event | category | flops | bytes accessed | tf_op | source)
XLA Modules:
  0.0 138.3 jit_solution(16891179819878218738)
XLA Ops:
  0.6 2.7 %shard_map.93 = f32[8,4,128,128]{3,2,1,0:T(8,128)} custom-call(bf16[128,1024]{1,0:T(8,128)(2,1)} %bitcast.14, bf16[128,1024]{1,0:T(8,128)(2,1)} %bitcast.16, bf16[128,1024]{1,0:T(8,128)(2,1)} %bitcast.17, bf16[128,1024]{1,0:T(8,128)(2,1)} %bitcast.18), custom_call_target="tpu_custom_call" | custom-call | tf_op jit(solution)/shard_map/pallas_call | solution.py:312
  3.3 0.0 copy-start.3
  3.3 0.0 copy-start.4
  3.3 0.0 copy-start.11
  3.3 10.5 %all-to-all-start = ((f32[8,4,128,128]{3,2,1,0:T(8,128)}), f32[8,4,128,128]{3,2,1,0:T(8,128)S(1)}, u32[]{:S(2)}, u32[]{:S(2)}) async-start(f32[8,4,128,128]{3,2,1,0:T(8,128)} %shard_map.93), calls=%async_computation | async-start | bytes 4194304 | tf_op jit(solution)/shard_map/all_to_all | solution.py:325
  13.9 0.1 pad_add_fusion.place
  13.9 0.0 copy-done.3
  13.9 0.0 copy-done.4
  13.9 0.0 copy-done.11
  13.9 1.4 %shard_map.94 = f32[40,128]{1,0:T(8,128)S(1)} custom-call(s32[1,4]{1,0:T(1,128)S(1)} %copy-done.11, s32[2]{0:T(128)S(1)} %pad_add_fusion.place, bf16[128,1024]{1,0:T(8,128)(2,1)S(1)} %bitcast.15, f32[128,128]{1,0:T(8,128)S(1)} %copy-done.4), custom_call_target="tpu_custom_call" | custom-call | tf_op jit(solution)/shard_map/pallas_call | solution.py:290
  15.4 41.9 %all-gather = f32[1280,128]{1,0:T(8,128)S(1)} all-gather(f32[40,128]{1,0:T(8,128)S(1)} %shard_map.94), channel_id=2, replica_groups=mesh['grp'=16,'row'=4,'col'=8] {'row','col'}, dimensions={0}, use_global_device_ids=true | all-gather | bytes 675840 | tf_op jit(solution)/shard_map/all_gather | solution.py:331
  57.2 0.0 all-to-all-done.all_ref
  57.3 3.0 %shard_map.95 = (f32[8,128,128]{2,1,0:T(8,128)S(1)}, f32[8,128,128]{2,1,0:T(8,128)S(1)}, f32[8,128]{1,0:T(8,128)S(1)}, f32[16,8,128]{2,1,0:T(8,128)}, f32[4,136,...) custom-call(s32[1,4]{1,0:T(1,128)S(1)} %copy-done.11, s32[2]{0:T(128)S(1)} %pad_add_fusion.place, ...), custom_call_target="tpu_custom_call" | custom-call | tf_op jit(solution)/shard_map/pallas_call | solution.py:290
  60.2 0.0 copy-start.6
  60.2 0.8 copy-done.6
  61.0 0.0 copy-start.8
  61.0 0.7 copy-done.8
  61.8 0.0 copy-start.12
  61.8 0.7 copy-done.12
  62.4 0.0 copy-start.1
  62.4 11.7 %all-to-all-start.1 = ((f32[16,8,128]{2,1,0:T(8,128)}), f32[16,8,128]{2,1,0:T(8,128)S(1)}, u32[]{:S(2)}, u32[]{:S(2)}) async-start(f32[16,8,128]{2,1,0:T(8,128)} %get-tuple-element.21), calls=%async_computation.1 | async-start | bytes 131072 | tf_op jit(solution)/shard_map/all_to_all | solution.py:344
  74.2 3.7 %collective-permute-start.2 = (f32[2,136,128]{2,1,0:T(8,128)}, f32[2,136,128]{2,1,0:T(8,128)S(1)}, u32[]{:S(2)}, u32[]{:S(2)}) collective-permute-start(f32[2,136,128]{2,1,0:T(8,128)} %copy-done.12), channel_id=1, source_target_pairs={{0,24},{8,0},{16,8},{24,16},{1,25},{9,1},{17,9},{25,17},{2,26},{10... | collective-permute-start | bytes 417800 | tf_op jit(solution)/shard_map/ppermute | solution.py:341
  77.9 2.1 %collective-permute-start.1 = (f32[2,136,128]{2,1,0:T(8,128)}, f32[2,136,128]{2,1,0:T(8,128)S(1)}, u32[]{:S(2)}, u32[]{:S(2)}) collective-permute-start(f32[2,136,128]{2,1,0:T(8,128)} %copy-done.12), channel_id=1, source_target_pairs={{0,16},{8,24},{16,0},{24,8},{1,17},{9,25},{17,1},{25,9},{2,18},{10... | collective-permute-start | bytes 417800 | tf_op jit(solution)/shard_map/ppermute | solution.py:341
  79.9 2.8 %collective-permute-start = (f32[2,136,128]{2,1,0:T(8,128)}, f32[2,136,128]{2,1,0:T(8,128)S(1)}, u32[]{:S(2)}, u32[]{:S(2)}) collective-permute-start(f32[2,136,128]{2,1,0:T(8,128)} %copy-done.12), channel_id=1, source_target_pairs={{0,8},{8,16},{16,24},{24,0},{1,9},{9,17},{17,25},{25,1},{2,10},{10... | collective-permute-start | bytes 417800 | tf_op jit(solution)/shard_map/ppermute | solution.py:341
  82.7 0.0 collective-permute-done.2.s3_ref
  82.7 3.3 %collective-permute-done.1.s2_ref = f32[2,136,128]{2,1,0:T(8,128)S(1)} collective-permute-done((f32[2,136,128]{2,1,0:T(8,128)}, f32[2,136,128]{2,1,0:T(8,128)S(1)}, u32[]{:S(2)}, u32[]{:S(2)}) %collective-permute-start.1) | collective-permute-done | bytes 139296 | tf_op jit(solution)/shard_map/ppermute | solution.py:341
  86.0 3.6 %collective-permute-done.s1_ref = f32[2,136,128]{2,1,0:T(8,128)S(1)} collective-permute-done((f32[2,136,128]{2,1,0:T(8,128)}, f32[2,136,128]{2,1,0:T(8,128)S(1)}, u32[]{:S(2)}, u32[]{:S(2)}) %collective-permute-start) | collective-permute-done | bytes 139296 | tf_op jit(solution)/shard_map/ppermute | solution.py:341
  89.6 0.0 all-to-all-done.1.z_ref
  89.6 0.0 copy-start.7
  89.6 1.0 copy-done.7
  90.7 0.0 copy-start.9
  90.7 1.0 copy-done.9
  91.6 3.0 %shard_map.96 = (f32[8,2,128,128]{3,2,1,0:T(8,128)S(1)}, f32[264,128]{1,0:T(8,128)S(1)}, f32[8,128]{1,0:T(8,128)}, f32[4,128,128]{2,1,0:T(8,128)S(1)}, f32[8,128]{1,0:T(8,128)S(1)}) custom-call(s32[1,4]{1,0:T(1,128)S(1)} %copy-done.11, s32[2]{0:T(128)S(1)} %pad_add_fusion.place, f32[8,4,128,128]{3,2,1,0:T(8,128)S(1)} %all-to-all-done.all_ref, ...), custom_call_target="tpu_custom_call" | custom-call | tf_op jit(solution)/shard_map/pallas_call | solution.py:290
  94.6 0.0 copy-start.5
  94.6 1.0 copy-done.5
  95.6 0.7 copy-done.10
  96.2 0.0 copy-done.1
  96.2 4.4 %all-to-all-start.2 = ((f32[8,2,128,128]{3,2,1,0:T(8,128)}), f32[8,2,128,128]{3,2,1,0:T(8,128)S(1)}, u32[]{:S(2)}, u32[]{:S(2)}) async-start(f32[8,2,128,128]{3,2,1,0:T(8,128)} %copy-done.5), calls=%async_computation.2 | async-start | bytes 2097152 | tf_op jit(solution)/shard_map/all_to_all | solution.py:352
  100.6 11.2 %all-gather.1 = f32[1056,128]{1,0:T(8,128)S(1)} all-gather(f32[264,128]{1,0:T(8,128)} %copy-done.10), channel_id=3, replica_groups=mesh['grp'=16,'row'=4,'col'=8] {'row'}, dimensions={0}, use_global_device_ids=true | all-gather | bytes 675840 | tf_op jit(solution)/shard_map/all_gather | solution.py:353
  111.8 1.0 copy-done.2
  112.9 1.8 %shard_map.98 = f32[8,2,128,128]{3,2,1,0:T(8,128)S(1)} custom-call(s32[1,4]{1,0:T(1,128)S(1)} %copy-done.11, s32[2]{0:T(128)S(1)} %pad_add_fusion.place, f32[8,4,128,128]{3,2,1,0:T(8,128)S(1)} %all-to-all-done.all_ref, f32[128,128]{1,0:T(8,128)S(1)} %copy-done.4, f32[8,128,128]{2,1,0:T(8,128)S(1)} %copy-done.2, f32[8,128]{1,0:T(8,128)S(1)} %get-tuple-element.27.share_ref, ...), custom_call_target="tpu_custom_call" | custom-call | tf_op jit(solution)/shard_map/pallas_call | solution.py:290
  114.6 0.0 copy-start
  114.7 0.9 copy-done
  115.6 0.2 all-to-all-done.2.res_ref
  115.8 6.5 %all-to-all-start.3 = ((f32[8,2,128,128]{3,2,1,0:T(8,128)}), f32[8,2,128,128]{3,2,1,0:T(8,128)S(1)}, u32[]{:S(2)}, u32[]{:S(2)}) async-start(f32[8,2,128,128]{3,2,1,0:T(8,128)} %copy-done), calls=%async_computation.3 | async-start | bytes 2097152 | tf_op jit(solution)/shard_map/all_to_all | solution.py:361
  122.3 0.9 shard_map.97
  123.2 14.2 %all-to-all-done.3.res_ref = f32[8,2,128,128]{3,2,1,0:T(8,128)S(1)} async-done(((f32[8,2,128,128]{3,2,1,0:T(8,128)}), f32[8,2,128,128]{3,2,1,0:T(8,128)S(1)}, u32[]{:S(2)}, u32[]{:S(2)}) %all-to-all-start.3) | async-done | bytes 1048608 | tf_op jit(solution)/shard_map/all_to_all | solution.py:361
  137.4 0.9 shard_map.99
  (2 shorter events, 0.0 us)
Async XLA Ops:
  3.3 10.6 %copy-start.3 = (bf16[1,128,1024]{2,1,0:T(8,128)(2,1)S(1)}, bf16[1,128,1024]{2,1,0:T(8,128)(2,1)}, u32[]{:S(2)}) copy-start(bf16[1,128,1024]{2,1,0:T(8,128)(2,1)} %param.7) | copy-start | bytes 786436
  3.3 10.6 %copy-start.4 = (f32[128,128]{1,0:T(8,128)S(1)}, f32[128,128]{1,0:T(8,128)}, u32[]{:S(2)}) copy-start(f32[128,128]{1,0:T(8,128)} %f_ref.7) | copy-start | bytes 196612
  3.3 10.6 %copy-start.11 = (s32[1,4]{1,0:T(1,128)S(1)}, s32[1,4]{1,0:T(1,128)}, u32[]{:S(2)}) copy-start(s32[1,4]{1,0:T(1,128)} %lens.7) | copy-start | bytes 52
  3.3 53.9 %all-to-all-start = ((f32[8,4,128,128]{3,2,1,0:T(8,128)}), f32[8,4,128,128]{3,2,1,0:T(8,128)S(1)}, u32[]{:S(2)}, u32[]{:S(2)}) async-start(f32[8,4,128,128]{3,2,1,0:T(8,128)} %shard_map.93), calls=%async_computation | async-start | bytes 4194304 | tf_op jit(solution)/shard_map/all_to_all | solution.py:325
  60.2 0.8 copy-start.6
  61.0 0.7 copy-start.8
  61.8 0.7 copy-start.12
  62.4 33.8 %copy-start.1 = (f32[8,128,128]{2,1,0:T(8,128)}, f32[8,128,128]{2,1,0:T(8,128)S(1)}, u32[]{:S(2)}) copy-start(f32[8,128,128]{2,1,0:T(8,128)S(1)} %get-tuple-element.18.er_ref) | copy-start | bytes 1572868
  62.4 27.2 %all-to-all-start.1 = ((f32[16,8,128]{2,1,0:T(8,128)}), f32[16,8,128]{2,1,0:T(8,128)S(1)}, u32[]{:S(2)}, u32[]{:S(2)}) async-start(f32[16,8,128]{2,1,0:T(8,128)} %get-tuple-element.21), calls=%async_computation.1 | async-start | bytes 131072 | tf_op jit(solution)/shard_map/all_to_all | solution.py:344
  74.2 8.6 %collective-permute-start.2 = (f32[2,136,128]{2,1,0:T(8,128)}, f32[2,136,128]{2,1,0:T(8,128)S(1)}, u32[]{:S(2)}, u32[]{:S(2)}) collective-permute-start(f32[2,136,128]{2,1,0:T(8,128)} %copy-done.12), channel_id=1, source_target_pairs={{0,24},{8,0},{16,8},{24,16},{1,25},{9,1},{17,9},{25,17},{2,26},{10... | collective-permute-start | bytes 417800 | tf_op jit(solution)/shard_map/ppermute | solution.py:341
  77.9 8.1 %collective-permute-start.1 = (f32[2,136,128]{2,1,0:T(8,128)}, f32[2,136,128]{2,1,0:T(8,128)S(1)}, u32[]{:S(2)}, u32[]{:S(2)}) collective-permute-start(f32[2,136,128]{2,1,0:T(8,128)} %copy-done.12), channel_id=1, source_target_pairs={{0,16},{8,24},{16,0},{24,8},{1,17},{9,25},{17,1},{25,9},{2,18},{10... | collective-permute-start | bytes 417800 | tf_op jit(solution)/shard_map/ppermute | solution.py:341
  79.9 9.7 %collective-permute-start = (f32[2,136,128]{2,1,0:T(8,128)}, f32[2,136,128]{2,1,0:T(8,128)S(1)}, u32[]{:S(2)}, u32[]{:S(2)}) collective-permute-start(f32[2,136,128]{2,1,0:T(8,128)} %copy-done.12), channel_id=1, source_target_pairs={{0,8},{8,16},{16,24},{24,0},{1,9},{9,17},{17,25},{25,1},{2,10},{10... | collective-permute-start | bytes 417800 | tf_op jit(solution)/shard_map/ppermute | solution.py:341
  89.6 1.0 copy-start.7
  90.7 1.0 copy-start.9
  94.6 1.0 copy-start.5
  95.6 0.7 copy-start.10
  96.2 19.5 %all-to-all-start.2 = ((f32[8,2,128,128]{3,2,1,0:T(8,128)}), f32[8,2,128,128]{3,2,1,0:T(8,128)S(1)}, u32[]{:S(2)}, u32[]{:S(2)}) async-start(f32[8,2,128,128]{3,2,1,0:T(8,128)} %copy-done.5), calls=%async_computation.2 | async-start | bytes 2097152 | tf_op jit(solution)/shard_map/all_to_all | solution.py:352
  111.8 1.0 copy-start.2
  114.6 0.9 copy-start
  115.8 21.6 %all-to-all-start.3 = ((f32[8,2,128,128]{3,2,1,0:T(8,128)}), f32[8,2,128,128]{3,2,1,0:T(8,128)S(1)}, u32[]{:S(2)}, u32[]{:S(2)}) async-start(f32[8,2,128,128]{3,2,1,0:T(8,128)} %copy-done), calls=%async_computation.3 | async-start | bytes 2097152 | tf_op jit(solution)/shard_map/all_to_all | solution.py:361

commit v6 on v5

--- a/solution.py
+++ b/solution.py
@@ -21,6 +21,7 @@
 K, V, Q, G = range(4)
 OUT, GQ = range(2)
 GK, GV = range(2)
+VALUES, TOTALS, PEAK = M, M + 1, M + 2
 
 
 def dot(a, b, dims):
@@ -99,98 +100,89 @@
         store.wait()
 
 
-def total_kernel(lens, place, k_ref, f_ref, pay_ref, kl_ref):
-    rows = k_ref.shape[0]
-    chains = Chains(lens, place[0] * H + place[1], 1, rows)
-    parts = split3(f_ref[...])
-    pay_ref[: CHAINS * H, :] = jnp.zeros((CHAINS * H, M), F32)
-    for h in range(H):
-        logits = logits_of(k_ref[:, head(h)].astype(F32), parts)
-        peak = jnp.max(logits, axis=(0, 1), keepdims=True)
-        kl_ref[h] = jnp.exp(logits - peak)
-        pay_ref[CHAINS * H + h : CHAINS * H + h + 1, :] = jnp.broadcast_to(peak, (1, M))
-    low, high = chains.ends_of(chains.me)
-
-    def one(c, carry):
-        mask = chains.mask(c, 0)
-        for h in range(H):
-            total = jnp.sum(jnp.where(mask, kl_ref[h], 0.0), axis=0, keepdims=True)
-            pay_ref[pl.ds(c * H + h, 1), :] = total
-        return carry
-
-    lax.fori_loop(low, high + 1, one, 0)
-
-
 def state_kernel(
-    lens, place, all_ref, f_ref, pay_ref,
-    er_ref, qr_ref, tot_ref, z_ref, s_ref, send_ref, sums_ref,
+    lens, place, all_ref, f_ref, z_hbm, s_ref, send_hbm, er_ref, send_ref, z_ref, sem, z_sem
 ):
     blocks, _, rows, _ = all_ref.shape
     chains = Chains(lens, place[0], blocks, rows)
-    peaks = jnp.max(pay_ref[:, CHAINS * H :, :], axis=0)
-    sums = [jnp.zeros((H, M), F32) for _ in range(CHAINS)]
-    for d in range(pay_ref.shape[0]):
-        share = jnp.exp(pay_ref[d, CHAINS * H :, :] - peaks)
-        for c in range(CHAINS):
-            sums[c] = sums[c] + share * pay_ref[d, c * H : (c + 1) * H, :]
-    for c in range(CHAINS):
-        sums_ref[c * H : (c + 1) * H, :] = sums[c]
-    sums_ref[CHAINS * H :, :] = peaks
-    tot_ref[...] = jnp.zeros_like(tot_ref)
-    for c in range(CHAINS + 1):
-        tot_ref[c : c + 1, :] = sums_ref[pl.ds(c * H + place[1], 1), :]
-    peak = tot_ref[CHAINS : CHAINS + 1, :]
+    parts = split3(f_ref[...])
+    peak = jnp.full((1, 1), -jnp.inf, F32)
+    for b in range(blocks):
+        logits = logits_of(all_ref[b, K], parts)
+        er_ref[b] = logits
+        peak = jnp.maximum(peak, jnp.max(logits, axis=(0, 1), keepdims=True))
+    for b in range(blocks):
+        er_ref[b] = jnp.exp(er_ref[b] - peak)
     for i in range(z_ref.shape[0]):
         z_ref[i] = jnp.broadcast_to(peak, z_ref.shape[1:])
-    parts = split3(f_ref[...])
-    for b in range(blocks):
-        er_ref[b] = jnp.exp(logits_of(all_ref[b, K], parts) - peak)
-        ql = logits_of(all_ref[b, Q], parts)
-        qr_ref[b] = jnp.exp(ql - jnp.max(ql, axis=1, keepdims=True)) * RATIO
+    z_store = pltpu.make_async_copy(z_ref, z_hbm, z_sem)
+    z_store.start()
     s_ref[...] = jnp.zeros_like(s_ref)
+    for c in range(CHAINS):
+        s_ref[c, PEAK : PEAK + 1, :] = jnp.broadcast_to(peak, (1, D))
     low, high = chains.ends_of(chains.me)
 
     def one(c, carry):
         state = jnp.zeros((M, D), F32)
-        total = jnp.zeros((rows, D), F32)
+        values = jnp.zeros((rows, D), F32)
+        totals = jnp.zeros((rows, M), F32)
         for b in range(blocks):
             mask = chains.mask(c, b)
-            hi, lo = split(jnp.where(mask, er_ref[b], 0.0))
+            raised = jnp.where(mask, er_ref[b], 0.0)
+            totals = totals + raised
+            hi, lo = split(raised)
             v = all_ref[b, V]
-            total = total + jnp.where(mask, v, 0.0)
+            values = values + jnp.where(mask, v, 0.0)
             v = v.astype(BF16)
             state = state + (dot(hi, v, TN) + dot(lo, v, TN))
         s_ref[c, :M, :] = state
-        s_ref[c, M : M + 1, :] = jnp.sum(total, axis=0, keepdims=True)
+        s_ref[c, VALUES : VALUES + 1, :] = jnp.sum(values, axis=0, keepdims=True)
+        s_ref[c, TOTALS : TOTALS + 1, :] = jnp.sum(totals, axis=0, keepdims=True)
         return carry
 
     lax.fori_loop(low, high + 1, one, 0)
     send_ref[0] = s_ref[low]
     send_ref[1] = s_ref[high] * (high != low).astype(F32)
+    store = pltpu.make_async_copy(send_ref, send_hbm, sem)
+    store.start()
+    z_store.wait()
+    store.wait()
 
 
 def query_kernel(
-    lens, place, all_ref, f_ref, er_ref, qr_ref, tot_ref, z_ref, s_ref, s1_ref, s2_ref, s3_ref,
-    res_ref, send_ref, bt_ref, b_ref, share_ref, full_ref, num_ref, gs_ref, inv_ref, tr_ref, t_ref,
+    lens, place, all_ref, f_ref, z_ref, s_ref, sent_ref,
+    res_hbm, send_hbm, b_ref, peak_ref,
+    qr_ref, full_ref, num_ref, gs_ref, inv_ref, tr_ref, t_ref, bt_ref, res_ref, send_ref, res_sem, send_sem,
 ):
     blocks, _, rows, _ = all_ref.shape
     chains = Chains(lens, place[0], blocks, rows)
+    parts = split3(f_ref[...])
+    for b in range(blocks):
+        ql = logits_of(all_ref[b, Q], parts)
+        qr_ref[b] = jnp.exp(ql - jnp.max(ql, axis=1, keepdims=True)) * RATIO
     peak = jnp.max(jnp.max(z_ref[...], axis=0), axis=0, keepdims=True)
-    share = jnp.exp(tot_ref[CHAINS : CHAINS + 1, :] - peak)
-    share_ref[...] = jnp.broadcast_to(RATIO * share, share_ref.shape)
+    peak_ref[...] = jnp.broadcast_to(peak, peak_ref.shape)
+    row = lax.broadcasted_iota(jnp.int32, (M + 8, D), 0)
+    share = jnp.where(row == VALUES, 1.0, jnp.exp(s_ref[0, PEAK : PEAK + 1, :] - peak))
+    for c in range(CHAINS):
+        full_ref[c] = s_ref[c] * share
+    for r in range(sent_ref.shape[0]):
+        ends = chains.ends_of(r)
+
+        @pl.when(chains.me != r)
+        def _():
+            share = jnp.where(row == VALUES, 1.0, jnp.exp(sent_ref[r, 0, PEAK : PEAK + 1, :] - peak))
+            for i, c in enumerate(ends):
+                full_ref[c] += sent_ref[r, i] * share
+
     for c in range(CHAINS):
         count = lens[0, c].astype(F32)
-        t_ref[c : c + 1, :] = RATIO * (share * tot_ref[c : c + 1, :] + EPS * count)
-    full_ref[...] = s_ref[...]
-    for step, sent_ref in ((1, s1_ref), (2, s2_ref), (3, s3_ref)):
-        ends = chains.ends_of(lax.rem(chains.me + (4 - step), 4))
-        for i, c in enumerate(ends):
-            full_ref[c] += sent_ref[i]
+        t_ref[c : c + 1, :] = RATIO * (full_ref[c, TOTALS : TOTALS + 1, :] + EPS * count)
     b_ref[...] = jnp.zeros_like(b_ref)
     low, high = chains.ends_of(chains.me)
 
     def one(c, carry):
-        state = RATIO * (share * full_ref[c, :M, :] + EPS * full_ref[c, M : M + 1, :])
+        state = RATIO * (full_ref[c, :M, :] + EPS * full_ref[c, VALUES : VALUES + 1, :])
         state = split(state)
         weights = t_ref[pl.ds(c, 1), :]
         back = jnp.zeros((M, D), F32)
@@ -211,7 +203,8 @@
         return carry
 
     lax.fori_loop(low, high + 1, one, 0)
-    feats = split(f_ref[...])
+    feats = parts[:2]
+    stores = [pltpu.make_async_copy(res_ref.at[b], res_hbm.at[b], res_sem.at[b]) for b in range(blocks)]
     for b in range(blocks):
         inv = inv_ref[b]
         exact = num_ref[b] * inv
@@ -223,6 +216,7 @@
         back = dot3(split(grad_logits), feats, NN)
         back = back - jnp.sum(grad_logits, axis=1, keepdims=True) * (SCALE * all_ref[b, Q])
         res_ref[b, GQ] = back * SCALE
+        stores[b].start()
     bt_ref[...] = jnp.zeros_like(bt_ref)
 
     def two(c, carry):
@@ -236,14 +230,23 @@
     send_ref[0:M, :] = b_ref[low]
     send_ref[M : 2 * M, :] = b_ref[high] * (high != low).astype(F32)
     send_ref[2 * M :, :] = bt_ref[...]
+    store = pltpu.make_async_copy(send_ref, send_hbm, send_sem)
+    store.start()
+    for one_store in stores:
+        one_store.wait()
+    store.wait()
 
 
 def key_kernel(
-    lens, place, all_ref, f_ref, er_ref, share_ref, b_ref, sent_ref,
-    res_ref, full_ref, sum_ref, dk_ref,
+    lens, place, all_ref, f_ref, peak_ref, b_ref, sent_ref,
+    res_hbm, kr_ref, full_ref, sum_ref, dk_ref, res_ref, res_sem,
 ):
     blocks, _, rows, _ = all_ref.shape
     chains = Chains(lens, place[0], blocks, rows)
+    parts = split3(f_ref[...])
+    peak = peak_ref[0:1, :]
+    for b in range(blocks):
+        kr_ref[b] = jnp.exp(logits_of(all_ref[b, K], parts) - peak) * RATIO
     full_ref[...] = b_ref[...]
     for r in range(sent_ref.shape[0]):
         low, high = chains.ends_of(r)
@@ -254,7 +257,6 @@
             full_ref[high] += sent_ref[r, M : 2 * M, :]
 
     sum_ref[...] = jnp.sum(sent_ref[:, 2 * M :, :], axis=0)
-    share = share_ref[0:1, :]
     low, high = chains.ends_of(chains.me)
 
     def one(c, carry):
@@ -262,7 +264,7 @@
         total = sum_ref[pl.ds(c, 1), :]
         for b in range(blocks):
             mask = chains.mask(c, b)
-            dv = dot3(split(er_ref[b] * share + EPS * RATIO), back, NN)
+            dv = dot3(split(kr_ref[b] + EPS * RATIO), back, NN)
             res_ref[b, GV] = jnp.where(mask, dv, res_ref[b, GV])
             v = all_ref[b, V].astype(BF16)
             dk = dot(v, back[0], NT) + dot(v, back[1], NT) + total
@@ -270,12 +272,16 @@
         return carry
 
     lax.fori_loop(low, high + 1, one, 0)
-    feats = split(f_ref[...])
-    for b in range(blocks):
-        grad_logits = dk_ref[b] * (er_ref[b] * share)
+    feats = parts[:2]
+    stores = [pltpu.make_async_copy(res_ref.at[b], res_hbm.at[b], res_sem.at[b]) for b in range(blocks)]
+    for b in range(blocks):
+        grad_logits = dk_ref[b] * kr_ref[b]
         back = dot3(split(grad_logits), feats, NN)
         back = back - jnp.sum(grad_logits, axis=1, keepdims=True) * (SCALE * all_ref[b, K])
         res_ref[b, GK] = back * SCALE
+        stores[b].start()
+    for store in stores:
+        store.wait()
 
 
 def unpack_kernel(res_ref, *outs):
@@ -284,14 +290,19 @@
             out[:, head(h)] = res_ref[h, i].astype(BF16)
 
 
+def is_hbm(shape):
+    return getattr(shape, "memory_space", None) is pltpu.HBM
+
+
 def call(kernel, shapes, args, scalars=0, scratch=()):
     vmem = pl.BlockSpec(memory_space=pltpu.VMEM)
     smem = pl.BlockSpec(memory_space=pltpu.SMEM)
+    hbm = pl.BlockSpec(memory_space=pltpu.HBM)
     return pl.pallas_call(
         kernel,
         out_shape=shapes,
         in_specs=[smem] * scalars + [vmem] * (len(args) - scalars),
-        out_specs=[vmem] * len(shapes),
+        out_specs=[hbm if is_hbm(a) else vmem for a in shapes],
         scratch_shapes=list(scratch),
         compiler_params=pltpu.CompilerParams(vmem_limit_bytes=40 * 2**20),
     )(*args)
@@ -323,40 +334,40 @@
         compiler_params=pltpu.CompilerParams(vmem_limit_bytes=60 * 2**20),
     )(k, v, q, g)
     own = lax.all_to_all(packed, "col", 0, 0, tiled=True)
-    small = f32(2 * CHAINS, M)
-    lots = ((CHAINS + 1) * H, M)
-    (payload,) = call(
-        total_kernel, [f32(*lots)], (*where, k, features), 2, [pltpu.VMEM((H, rows, M), F32)]
+    states = (CHAINS, M + 8, D)
+    peers = (groups * lines, 8, M)
+    dma = pltpu.SemaphoreType.DMA
+    peaks, own_states, ends = call(
+        state_kernel,
+        [pltpu.HBM(peers, F32), f32(*states), pltpu.HBM((2, M + 8, D), F32)],
+        (*where, own, features),
+        2,
+        [pltpu.VMEM(wide, F32), pltpu.VMEM((2, M + 8, D), F32), pltpu.VMEM(peers, F32), dma, dma],
     )
-    payload = lax.all_gather(payload, ("row", "col"))
-    states = (CHAINS, M + 8, D)
-    key_raised, raised, totals, peaks, own_states, ends = call(
-        state_kernel,
-        [f32(*wide), f32(*wide), small, f32(groups, 8, M), f32(*states), f32(2, M + 8, D)],
-        (*where, own, features, payload),
+    peaks = lax.all_to_all(peaks, ("grp", "row"), 0, 0, tiled=True)
+    ends = lax.all_gather(ends, "row")
+    pair = (blocks, 2, rows, D)
+    back = (2 * M + 2 * CHAINS, D)
+    small = (2 * CHAINS, M)
+    first, back_ends, backs, peak = call(
+        query_kernel,
+        [pltpu.HBM(pair, F32), pltpu.HBM(back, F32), f32(CHAINS, M, D), f32(*small)],
+        (*where, own, features, peaks, own_states, ends),
         2,
-        [pltpu.VMEM(lots, F32)],
-    )
-    sent = [
-        lax.ppermute(ends, "row", [(i, (i + step) % lines) for i in range(lines)])
-        for step in range(1, lines)
-    ]
-    peaks = lax.all_to_all(peaks, "grp", 0, 0, tiled=True)
-    first, back_ends, _, backs, share = call(
-        query_kernel,
-        [f32(blocks, 2, rows, D), f32(2 * M + 2 * CHAINS, D), small, f32(CHAINS, M, D), small],
-        (*where, own, features, key_raised, raised, totals, peaks, own_states, *sent),
-        2,
-        [pltpu.VMEM(states, F32)] + [pltpu.VMEM(wide, F32)] * 4 + [pltpu.VMEM((2 * CHAINS, M), F32)],
+        [pltpu.VMEM(wide, F32), pltpu.VMEM(states, F32)]
+        + [pltpu.VMEM(wide, F32)] * 4
+        + [pltpu.VMEM(small, F32)] * 2
+        + [pltpu.VMEM(pair, F32), pltpu.VMEM(back, F32), dma((blocks,)), dma],
     )
     first = lax.all_to_all(first, "col", 0, 0, tiled=True)
     back_ends = lax.all_gather(back_ends, "row")
     (second,) = call(
         key_kernel,
-        [f32(blocks, 2, rows, D)],
-        (*where, own, features, key_raised, share, backs, back_ends),
+        [pltpu.HBM(pair, F32)],
+        (*where, own, features, peak, backs, back_ends),
         2,
-        [pltpu.VMEM((CHAINS, M, D), F32), pltpu.VMEM((2 * CHAINS, M), F32), pltpu.VMEM(wide, F32)],
+        [pltpu.VMEM(wide, F32), pltpu.VMEM((CHAINS, M, D), F32), pltpu.VMEM(small, F32)]
+        + [pltpu.VMEM(wide, F32), pltpu.VMEM(pair, F32), dma((blocks,))],
     )
     second = lax.all_to_all(second, "col", 0, 0, tiled=True)
     narrow = [jax.ShapeDtypeStruct((rows, width), BF16)] * 2

time: 140 us -> 128 us (0.914)
  blocking collectives: 53 us -> 24.3 us
  waiting for transfers between devices: 21.2 us -> 47 us
  local copies, waits for them, and re-layouts: 7.86 us -> 0.71 us
  starting transfers between devices: 41.7 us -> 39.4 us
    all_gather x1, blocking collectives: 41.9 us -> 12.9 us  [on_device(): ends = lax.all_gather(ends, 'row')]
    all_to_all x1, waiting for transfers between devices: 0.01 us -> 26.3 us  [on_device(): own = lax.all_to_all(packed, 'col', 0, 0, tiled=True)]
    ppermute x3 -> x0, starting transfers between devices: 8.53 us -> none  [on_device(): lax.ppermute(ends, 'row', [(i, (i + step) % lines) for i in range(lines)])]
    unnamed x26 -> x8, local copies, waits for them, and re-layouts: 7.86 us -> 0.71 us
    ppermute x3 -> x0, waiting for transfers between devices: 6.88 us -> none  [on_device(): lax.ppermute(ends, 'row', [(i, (i + step) % lines) for i in range(lines)])]
    all_to_all x1, waiting for transfers between devices: 0.01 us -> 6.22 us  [on_device(): peaks = lax.all_to_all(peaks, ('grp', 'row'), 0, 0, tiled=True)]
    all_to_all x1, starting transfers between devices: 4.41 us -> 8.01 us  [on_device(): first = lax.all_to_all(first, 'col', 0, 0, tiled=True)]
    all_to_all x1, starting transfers between devices: 11.7 us -> 14.8 us  [on_device(): peaks = lax.all_to_all(peaks, ('grp', 'row'), 0, 0, tiled=True)]
  transfers between devices with their start and end apart: 7 -> 4, of which waited for: 4 -> 4; matrix products, arithmetic and copies ran while one was open for 0% -> 0% of each run, Pallas kernels for 3% -> 3%
where the time goes in v6:
time: 128 us; the launch traced here: 127 us
  waiting for transfers between devices  47 us (37%)
  starting transfers between devices  39.4 us (31%)
  blocking collectives  24.3 us (19%)
  Pallas kernels  14.2 us (11%)
    all_to_all x1, waiting for transfers between devices, on_device(): own = lax.all_to_all(packed, 'col', 0, 0, tiled=True)  26.3 us
    all_to_all x1, starting transfers between devices, on_device(): peaks = lax.all_to_all(peaks, ('grp', 'row'), 0, 0, tiled=True)  14.8 us
    all_to_all x1, waiting for transfers between devices, on_device(): second = lax.all_to_all(second, 'col', 0, 0, tiled=True)  14.2 us
    all_gather x1, blocking collectives, on_device(): ends = lax.all_gather(ends, 'row')  12.9 us
    pallas_call x5, Pallas kernels, call(): pl.pallas_call(kernel, out_shape=shapes, in_specs=[smem] * scalars + [vme...  11.6 us
    all_gather x1, blocking collectives, on_device(): back_ends = lax.all_gather(back_ends, 'row')  11.4 us
    all_to_all x1, starting transfers between devices, on_device(): own = lax.all_to_all(packed, 'col', 0, 0, tiled=True)  10.5 us
    all_to_all x1, starting transfers between devices, on_device(): first = lax.all_to_all(first, 'col', 0, 0, tiled=True)  8.01 us
  transfers between devices with their start and end apart: 4, of which 4 were waited for; matrix products, arithmetic and copies ran while one was open for 0% of the time, Pallas kernels for 3%

profile of v6, /device:TPU:1, one launch (start us, length us, event | category | flops | bytes accessed | tf_op | source)
XLA Modules:
  0.0 126.5 jit_solution(601079394872108867)
XLA Ops:
  0.6 2.7 %shard_map.93 = f32[8,4,128,128]{3,2,1,0:T(8,128)} custom-call(bf16[128,1024]{1,0:T(8,128)(2,1)} %bitcast.14, bf16[128,1024]{1,0:T(8,128)(2,1)} %bitcast.15, bf16[128,1024]{1,0:T(8,128)(2,1)} %bitcast.16, bf16[128,1024]{1,0:T(8,128)(2,1)} %bitcast.17), custom_call_target="tpu_custom_call" | custom-call | tf_op jit(solution)/shard_map/pallas_call | solution.py:323
  3.3 0.0 copy-start
  3.3 0.0 copy-start.3
  3.3 10.5 %all-to-all-start = ((f32[8,4,128,128]{3,2,1,0:T(8,128)}), f32[8,4,128,128]{3,2,1,0:T(8,128)S(1)}, u32[]{:S(2)}, u32[]{:S(2)}) async-start(f32[8,4,128,128]{3,2,1,0:T(8,128)} %shard_map.93), calls=%async_computation | async-start | bytes 4194304 | tf_op jit(solution)/shard_map/all_to_all | solution.py:336
  13.9 0.1 pad_add_fusion.place
  13.9 26.3 %all-to-all-done.all_ref = f32[8,4,128,128]{3,2,1,0:T(8,128)S(1)} async-done(((f32[8,4,128,128]{3,2,1,0:T(8,128)}), f32[8,4,128,128]{3,2,1,0:T(8,128)S(1)}, u32[]{:S(2)}, u32[]{:S(2)}) %all-to-all-start) | async-done | bytes 2097184 | tf_op jit(solution)/shard_map/all_to_all | solution.py:336
  40.2 0.0 copy-done
  40.2 0.0 copy-done.3
  40.2 2.6 %shard_map.94 = (f32[64,8,128]{2,1,0:T(8,128)}, f32[4,136,128]{2,1,0:T(8,128)S(1)}, f32[2,136,128]{2,1,0:T(8,128)}) custom-call(s32[1,4]{1,0:T(1,128)S(1)} %copy-done.3, s32[2]{0:T(128)S(1)} %pad_add_fusion.place, f32[8,4,128,128]{3,2,1,0:T(8,128)S(1)} %all-to-all-done.all_ref, f32[128,128]{1,0:T(8,128)S(1)} %copy-done), custom_call_target="tpu_custom_call" | custom-call | tf_op jit(solution)/shard_map/pallas_call | solution.py:301
  42.8 14.8 %all-to-all-start.1 = ((f32[64,8,128]{2,1,0:T(8,128)}), f32[64,8,128]{2,1,0:T(8,128)S(1)}, u32[]{:S(2)}, u32[]{:S(2)}) async-start(f32[64,8,128]{2,1,0:T(8,128)} %get-tuple-element.15), calls=%async_computation.1 | async-start | bytes 524288 | tf_op jit(solution)/shard_map/all_to_all | solution.py:347
  57.6 12.9 %all-gather = f32[8,136,128]{2,1,0:T(8,128)S(1)} all-gather(f32[2,136,128]{2,1,0:T(8,128)} %get-tuple-element.17), channel_id=2, replica_groups=mesh['grp'=16,'row'=4,'col'=8] {'row'}, dimensions={0}, use_global_device_ids=true | all-gather | bytes 696320 | tf_op jit(solution)/shard_map/all_gather | solution.py:348
  70.5 6.2 %all-to-all-done.1.z_ref = f32[64,8,128]{2,1,0:T(8,128)S(1)} async-done(((f32[64,8,128]{2,1,0:T(8,128)}), f32[64,8,128]{2,1,0:T(8,128)S(1)}, u32[]{:S(2)}, u32[]{:S(2)}) %all-to-all-start.1) | async-done | bytes 262176 | tf_op jit(solution)/shard_map/all_to_all | solution.py:347
  76.8 3.8 %shard_map.95 = (f32[8,2,128,128]{3,2,1,0:T(8,128)}, f32[264,128]{1,0:T(8,128)}, f32[4,128,128]{2,1,0:T(8,128)S(1)}, f32[8,128]{1,0:T(8,128)S(1)}) custom-call(s32[1,4]{1,0:T(1,128)S(1)} %copy-done.3, s32[2]{0:T(128)S(1)} %pad_add_fusion.place, f32[8,4,128,128]{3,2,1,0:T(8,128)S(1)} %all-to-all-done.all_ref, f32[128,128]{1,0:T(8,128)S(1)} %copy-done, ...), custom_call_target="tpu_custom_call" | custom-call | tf_op jit(solution)/shard_map/pallas_call | solution.py:301
  80.6 0.0 copy-start.1
  80.6 0.7 copy-done.1
  81.3 0.0 copy-start.2
  81.3 8.0 %all-to-all-start.2 = ((f32[8,2,128,128]{3,2,1,0:T(8,128)}), f32[8,2,128,128]{3,2,1,0:T(8,128)S(1)}, u32[]{:S(2)}, u32[]{:S(2)}) async-start(f32[8,2,128,128]{3,2,1,0:T(8,128)} %get-tuple-element.18), calls=%async_computation.2 | async-start | bytes 2097152 | tf_op jit(solution)/shard_map/all_to_all | solution.py:362
  89.3 11.4 %all-gather.1 = f32[1056,128]{1,0:T(8,128)S(1)} all-gather(f32[264,128]{1,0:T(8,128)} %get-tuple-element.23), channel_id=3, replica_groups=mesh['grp'=16,'row'=4,'col'=8] {'row'}, dimensions={0}, use_global_device_ids=true | all-gather | bytes 675840 | tf_op jit(solution)/shard_map/all_gather | solution.py:363
  100.7 0.0 copy-done.2
  100.7 3.3 %shard_map.97 = f32[8,2,128,128]{3,2,1,0:T(8,128)} custom-call(s32[1,4]{1,0:T(1,128)S(1)} %copy-done.3, s32[2]{0:T(128)S(1)} %pad_add_fusion.place, f32[8,4,128,128]{3,2,1,0:T(8,128)S(1)} %all-to-all-done.all_ref, f32[128,128]{1,0:T(8,128)S(1)} %copy-done, f32[8,128]{1,0:T(8,128)S(1)} %get-tuple-element.21.peak_ref, f32[4,128,128]{2,1,0:T(8,128)S(1)} %copy-done.2, ...), custom_call_target="tpu_custom_call" | custom-call | tf_op jit(solution)/shard_map/pallas_call | solution.py:301
  104.0 0.4 all-to-all-done.2.res_ref
  104.4 6.1 %all-to-all-start.3 = ((f32[8,2,128,128]{3,2,1,0:T(8,128)}), f32[8,2,128,128]{3,2,1,0:T(8,128)S(1)}, u32[]{:S(2)}, u32[]{:S(2)}) async-start(f32[8,2,128,128]{3,2,1,0:T(8,128)} %shard_map.97), calls=%async_computation.3 | async-start | bytes 2097152 | tf_op jit(solution)/shard_map/all_to_all | solution.py:372
  110.5 0.9 shard_map.96
  111.4 14.2 %all-to-all-done.3.res_ref = f32[8,2,128,128]{3,2,1,0:T(8,128)S(1)} async-done(((f32[8,2,128,128]{3,2,1,0:T(8,128)}), f32[8,2,128,128]{3,2,1,0:T(8,128)S(1)}, u32[]{:S(2)}, u32[]{:S(2)}) %all-to-all-start.3) | async-done | bytes 1048608 | tf_op jit(solution)/shard_map/all_to_all | solution.py:372
  125.6 0.9 shard_map.98
Async XLA Ops:
  3.3 36.9 %copy-start = (f32[128,128]{1,0:T(8,128)S(1)}, f32[128,128]{1,0:T(8,128)}, u32[]{:S(2)}) copy-start(f32[128,128]{1,0:T(8,128)} %f_ref.5) | copy-start | bytes 196612
  3.3 36.9 %copy-start.3 = (s32[1,4]{1,0:T(1,128)S(1)}, s32[1,4]{1,0:T(1,128)}, u32[]{:S(2)}) copy-start(s32[1,4]{1,0:T(1,128)} %lens.5) | copy-start | bytes 52
  3.3 36.9 %all-to-all-start = ((f32[8,4,128,128]{3,2,1,0:T(8,128)}), f32[8,4,128,128]{3,2,1,0:T(8,128)S(1)}, u32[]{:S(2)}, u32[]{:S(2)}) async-start(f32[8,4,128,128]{3,2,1,0:T(8,128)} %shard_map.93), calls=%async_computation | async-start | bytes 4194304 | tf_op jit(solution)/shard_map/all_to_all | solution.py:336
  42.8 33.9 %all-to-all-start.1 = ((f32[64,8,128]{2,1,0:T(8,128)}), f32[64,8,128]{2,1,0:T(8,128)S(1)}, u32[]{:S(2)}, u32[]{:S(2)}) async-start(f32[64,8,128]{2,1,0:T(8,128)} %get-tuple-element.15), calls=%async_computation.1 | async-start | bytes 524288 | tf_op jit(solution)/shard_map/all_to_all | solution.py:347
  80.6 0.7 copy-start.1
  81.3 19.4 %copy-start.2 = (f32[4,128,128]{2,1,0:T(8,128)S(1)}, f32[4,128,128]{2,1,0:T(8,128)}, u32[]{:S(2)}) copy-start(f32[4,128,128]{2,1,0:T(8,128)} %copy-done.1) | copy-start | bytes 786436
  81.3 23.1 %all-to-all-start.2 = ((f32[8,2,128,128]{3,2,1,0:T(8,128)}), f32[8,2,128,128]{3,2,1,0:T(8,128)S(1)}, u32[]{:S(2)}, u32[]{:S(2)}) async-start(f32[8,2,128,128]{3,2,1,0:T(8,128)} %get-tuple-element.18), calls=%async_computation.2 | async-start | bytes 2097152 | tf_op jit(solution)/shard_map/all_to_all | solution.py:362
  104.4 21.2 %all-to-all-start.3 = ((f32[8,2,128,128]{3,2,1,0:T(8,128)}), f32[8,2,128,128]{3,2,1,0:T(8,128)S(1)}, u32[]{:S(2)}, u32[]{:S(2)}) async-start(f32[8,2,128,128]{3,2,1,0:T(8,128)} %shard_map.97), calls=%async_computation.3 | async-start | bytes 2097152 | tf_op jit(solution)/shard_map/all_to_all | solution.py:372

commit v7 on v6

--- a/solution.py
+++ b/solution.py
@@ -100,8 +100,16 @@
         store.wait()
 
 
+def peak_kernel(k_ref, f_ref, peak_ref):
+    parts = split3(f_ref[...])
+    for h in range(H):
+        logits = logits_of(k_ref[:, head(h)].astype(F32), parts)
+        peak = jnp.max(logits, axis=(0, 1), keepdims=True)
+        peak_ref[h : h + 1, :] = jnp.broadcast_to(peak, (1, M))
+
+
 def state_kernel(
-    lens, place, all_ref, f_ref, z_hbm, s_ref, send_hbm, er_ref, send_ref, z_ref, sem, z_sem
+    lens, place, all_ref, f_ref, lines_ref, z_hbm, s_ref, send_hbm, er_ref, send_ref, z_ref, sem, z_sem
 ):
     blocks, _, rows, _ = all_ref.shape
     chains = Chains(lens, place[0], blocks, rows)
@@ -114,7 +122,8 @@
     for b in range(blocks):
         er_ref[b] = jnp.exp(er_ref[b] - peak)
     for i in range(z_ref.shape[0]):
-        z_ref[i] = jnp.broadcast_to(peak, z_ref.shape[1:])
+        h = i % H
+        z_ref[i] = jnp.broadcast_to(lines_ref[h : h + 1, :], z_ref.shape[1:])
     z_store = pltpu.make_async_copy(z_ref, z_hbm, z_sem)
     z_store.start()
     s_ref[...] = jnp.zeros_like(s_ref)
@@ -294,7 +303,7 @@
     return getattr(shape, "memory_space", None) is pltpu.HBM
 
 
-def call(kernel, shapes, args, scalars=0, scratch=()):
+def call(kernel, shapes, args, scalars=0, scratch=(), limit=40):
     vmem = pl.BlockSpec(memory_space=pltpu.VMEM)
     smem = pl.BlockSpec(memory_space=pltpu.SMEM)
     hbm = pl.BlockSpec(memory_space=pltpu.HBM)
@@ -304,12 +313,24 @@
         in_specs=[smem] * scalars + [vmem] * (len(args) - scalars),
         out_specs=[hbm if is_hbm(a) else vmem for a in shapes],
         scratch_shapes=list(scratch),
-        compiler_params=pltpu.CompilerParams(vmem_limit_bytes=40 * 2**20),
+        compiler_params=pltpu.CompilerParams(vmem_limit_bytes=limit * 2**20),
     )(*args)
 
 
 def f32(*shape):
     return jax.ShapeDtypeStruct(shape, F32)
+
+
+def max_over(x, axis):
+    count = lax.axis_size(axis)
+    reach = 0
+    while 2 * reach + 1 < count:
+        step = min(2 * reach + 1, count // 2 - reach)
+        up = lax.ppermute(x, axis, [(i, (i + step) % count) for i in range(count)])
+        down = lax.ppermute(x, axis, [(i, (i - step) % count) for i in range(count)])
+        x = jnp.maximum(x, jnp.maximum(up, down))
+        reach += step
+    return x
 
 
 def on_device(queries, keys, values, grad_attended, features, chain_lengths):
@@ -317,9 +338,11 @@
     q, k, v, g = (a.reshape(rows, width) for a in (queries, keys, values, grad_attended))
     place = jnp.stack([lax.axis_index("row"), lax.axis_index("col")]).astype(jnp.int32)
     where = (chain_lengths, place)
-    groups, lines, blocks = (lax.axis_size(a) for a in ("grp", "row", "col"))
+    lines, blocks = (lax.axis_size(a) for a in ("row", "col"))
     wide = (blocks, rows, D)
     hbm = pl.BlockSpec(memory_space=pltpu.HBM)
+    (peaks,) = call(peak_kernel, [f32(H, M)], (k, features), limit=60)
+    peaks = max_over(peaks, "grp")
     packed = pl.pallas_call(
         pack_kernel,
         out_shape=f32(H, 4, rows, D),
@@ -335,23 +358,23 @@
     )(k, v, q, g)
     own = lax.all_to_all(packed, "col", 0, 0, tiled=True)
     states = (CHAINS, M + 8, D)
-    peers = (groups * lines, 8, M)
+    peers = (lines * blocks, 8, M)
     dma = pltpu.SemaphoreType.DMA
     peaks, own_states, ends = call(
         state_kernel,
-        [pltpu.HBM(peers, F32), f32(*states), pltpu.HBM((2, M + 8, D), F32)],
-        (*where, own, features),
+        [pltpu.HBM(peers, F32), pltpu.VMEM(states, F32), pltpu.HBM((2, M + 8, D), F32)],
+        (*where, own, features, peaks),
         2,
         [pltpu.VMEM(wide, F32), pltpu.VMEM((2, M + 8, D), F32), pltpu.VMEM(peers, F32), dma, dma],
     )
-    peaks = lax.all_to_all(peaks, ("grp", "row"), 0, 0, tiled=True)
+    peaks = lax.all_to_all(peaks, ("row", "col"), 0, 0, tiled=True)
     ends = lax.all_gather(ends, "row")
     pair = (blocks, 2, rows, D)
     back = (2 * M + 2 * CHAINS, D)
     small = (2 * CHAINS, M)
     first, back_ends, backs, peak = call(
         query_kernel,
-        [pltpu.HBM(pair, F32), pltpu.HBM(back, F32), f32(CHAINS, M, D), f32(*small)],
+        [pltpu.HBM(pair, F32), pltpu.HBM(back, F32), pltpu.VMEM((CHAINS, M, D), F32), f32(*small)],
         (*where, own, features, peaks, own_states, ends),
         2,
         [pltpu.VMEM(wide, F32), pltpu.VMEM(states, F32)]

time: 128 us -> 130 us (1.016)
  waiting for transfers between devices: 47 us -> 25.1 us
  starting transfers between devices: 39.4 us -> 60.6 us
  Pallas kernels: 14.2 us -> 16.7 us
    all_to_all x1, waiting for transfers between devices: 26.3 us -> 0.01 us  [on_device(): own = lax.all_to_all(packed, 'col', 0, 0, tiled=True)]
    ppermute x0 -> x6, starting transfers between devices: none -> 24.7 us  [the longest x3 14 us: max_over(): lax.ppermute(x, axis, [(i, (i - step) % count) for i in range(count)])]
    ppermute x0 -> x6, waiting for transfers between devices: none -> 10.9 us  [the longest x3 10.9 us: max_over(): up = lax.ppermute(x, axis, [(i, (i + step) % count) for i in range(count)])]
    all_to_all x1, waiting for transfers between devices: 6.22 us -> 0.01 us  [on_device(): peaks = lax.all_to_all(peaks, ('row', 'col'), 0, 0, tiled=True)]
    all_to_all x1, starting transfers between devices: 14.8 us -> 12.1 us  [on_device(): peaks = lax.all_to_all(peaks, ('row', 'col'), 0, 0, tiled=True)]
    pallas_call x5 -> x6, Pallas kernels: 11.6 us -> 14 us  [call(): pl.pallas_call(kernel, out_shape=shapes, in_specs=[smem] * scalars + [vme...]
  transfers between devices with their start and end apart: 4 -> 10, of which waited for: 4 -> 4; matrix products, arithmetic and copies ran while one was open for 0% -> 1% of each run, Pallas kernels for 3% -> 5%
where the time goes in v7:
time: 130 us; the launch traced here: 128 us
  starting transfers between devices  60.6 us (47%)
  waiting for transfers between devices  25.1 us (19%)
  blocking collectives  23.8 us (18%)
  Pallas kernels  16.7 us (13%)
    all_to_all x1, waiting for transfers between devices, on_device(): second = lax.all_to_all(second, 'col', 0, 0, tiled=True)  14.2 us
    ppermute x3, starting transfers between devices, max_over(): lax.ppermute(x, axis, [(i, (i - step) % count) for i in range(count)])  14 us
    pallas_call x6, Pallas kernels, call(): pl.pallas_call(kernel, out_shape=shapes, in_specs=[smem] * scalars + [vme...  14 us
    all_to_all x1, starting transfers between devices, on_device(): peaks = lax.all_to_all(peaks, ('row', 'col'), 0, 0, tiled=True)  12.1 us
    all_gather x1, blocking collectives, on_device(): back_ends = lax.all_gather(back_ends, 'row')  12 us
    all_gather x1, blocking collectives, on_device(): ends = lax.all_gather(ends, 'row')  11.8 us
    ppermute x3, waiting for transfers between devices, max_over(): up = lax.ppermute(x, axis, [(i, (i + step) % count) for i in range(count)])  10.9 us
    ppermute x3, starting transfers between devices, max_over(): up = lax.ppermute(x, axis, [(i, (i + step) % count) for i in range(count)])  10.7 us
  transfers between devices with their start and end apart: 10, of which 4 were waited for; matrix products, arithmetic and copies ran while one was open for 1% of the time, Pallas kernels for 5%

profile of v7, /device:TPU:1, one launch (start us, length us, event | category | flops | bytes accessed | tf_op | source)
XLA Modules:
  0.0 127.7 jit_solution(7718454602358348617)
XLA Ops:
  0.6 2.7 %shard_map.93 = f32[8,4,128,128]{3,2,1,0:T(8,128)} custom-call(bf16[128,1024]{1,0:T(8,128)(2,1)} %bitcast.14, bf16[128,1024]{1,0:T(8,128)(2,1)} %bitcast.16, bf16[128,1024]{1,0:T(8,128)(2,1)} %bitcast.17, bf16[128,1024]{1,0:T(8,128)(2,1)} %bitcast.18), custom_call_target="tpu_custom_call" | custom-call | tf_op jit(solution)/shard_map/pallas_call | solution.py:346
  3.3 0.0 copy-start
  3.3 0.0 copy-start.1
  3.3 10.5 %all-to-all-start = ((f32[8,4,128,128]{3,2,1,0:T(8,128)}), f32[8,4,128,128]{3,2,1,0:T(8,128)S(1)}, u32[]{:S(2)}, u32[]{:S(2)}) async-start(f32[8,4,128,128]{3,2,1,0:T(8,128)} %shard_map.93), calls=%async_computation | async-start | bytes 4194304 | tf_op jit(solution)/shard_map/all_to_all | solution.py:359
  13.9 2.3 %shard_map.94 = f32[8,128]{1,0:T(8,128)} custom-call(bf16[128,1024]{1,0:T(8,128)(2,1)} %bitcast.15, f32[128,128]{1,0:T(8,128)} %f_ref.7), custom_call_target="tpu_custom_call" | custom-call | tf_op jit(solution)/shard_map/pallas_call | solution.py:310
  16.2 6.5 %collective-permute-start.1 = (f32[8,128]{1,0:T(8,128)}, f32[8,128]{1,0:T(8,128)S(1)}, u32[]{:S(2)}, u32[]{:S(2)}) collective-permute-start(f32[8,128]{1,0:T(8,128)} %shard_map.94), channel_id=1, source_target_pairs={{0,480},{32,0},{64,32},{96,64},{128,96},{160,128},{192,160},{224,1... | collective-permute-start | bytes 12296 | tf_op jit(solution)/shard_map/ppermute | solution.py:330
  22.7 1.9 %collective-permute-start = (f32[8,128]{1,0:T(8,128)}, f32[8,128]{1,0:T(8,128)S(1)}, u32[]{:S(2)}, u32[]{:S(2)}) collective-permute-start(f32[8,128]{1,0:T(8,128)} %shard_map.94), channel_id=1, source_target_pairs={{0,32},{32,64},{64,96},{96,128},{128,160},{160,192},{192,224},{224... | collective-permute-start | bytes 12296 | tf_op jit(solution)/shard_map/ppermute | solution.py:329
  24.7 0.0 collective-permute-done.1
  24.7 4.1 %collective-permute-done = f32[8,128]{1,0:T(8,128)S(1)} collective-permute-done((f32[8,128]{1,0:T(8,128)}, f32[8,128]{1,0:T(8,128)S(1)}, u32[]{:S(2)}, u32[]{:S(2)}) %collective-permute-start) | collective-permute-done | bytes 4128 | tf_op jit(solution)/shard_map/ppermute | solution.py:329
  28.8 0.7 maximum_maximum_fusion.2
  29.5 2.8 %collective-permute-start.3 = (f32[8,128]{1,0:T(8,128)S(1)}, f32[8,128]{1,0:T(8,128)S(1)}, u32[]{:S(2)}, u32[]{:S(2)}) collective-permute-start(f32[8,128]{1,0:T(8,128)S(1)} %maximum_maximum_fusion.2), channel_id=1, source_target_pairs={{0,416},{32,448},{64,480},{96,0},{128,32},{160,64},{192,96},{224,1... | collective-permute-start | bytes 12296 | tf_op jit(solution)/shard_map/ppermute | solution.py:330
  32.3 4.3 %collective-permute-start.2 = (f32[8,128]{1,0:T(8,128)S(1)}, f32[8,128]{1,0:T(8,128)S(1)}, u32[]{:S(2)}, u32[]{:S(2)}) collective-permute-start(f32[8,128]{1,0:T(8,128)S(1)} %maximum_maximum_fusion.2), channel_id=1, source_target_pairs={{0,96},{32,128},{64,160},{96,192},{128,224},{160,256},{192,288},{2... | collective-permute-start | bytes 12296 | tf_op jit(solution)/shard_map/ppermute | solution.py:329
  36.6 0.0 collective-permute-done.3
  36.6 3.1 %collective-permute-done.2 = f32[8,128]{1,0:T(8,128)S(1)} collective-permute-done((f32[8,128]{1,0:T(8,128)S(1)}, f32[8,128]{1,0:T(8,128)S(1)}, u32[]{:S(2)}, u32[]{:S(2)}) %collective-permute-start.2) | collective-permute-done | bytes 4128 | tf_op jit(solution)/shard_map/ppermute | solution.py:329
  39.7 4.7 %collective-permute-start.5 = (f32[8,128]{1,0:T(8,128)S(1)}, f32[8,128]{1,0:T(8,128)S(1)}, u32[]{:S(2)}, u32[]{:S(2)}) collective-permute-start(f32[8,128]{1,0:T(8,128)S(1)} %maximum_maximum_fusion.1), channel_id=1, source_target_pairs={{0,384},{32,416},{64,448},{96,480},{128,0},{160,32},{192,64},{224,... | collective-permute-start | bytes 12296 | tf_op jit(solution)/shard_map/ppermute | solution.py:330
  44.3 4.5 %collective-permute-start.4 = (f32[8,128]{1,0:T(8,128)S(1)}, f32[8,128]{1,0:T(8,128)S(1)}, u32[]{:S(2)}, u32[]{:S(2)}) collective-permute-start(f32[8,128]{1,0:T(8,128)S(1)} %maximum_maximum_fusion.1), channel_id=1, source_target_pairs={{0,128},{32,160},{64,192},{96,224},{128,256},{160,288},{192,320},{... | collective-permute-start | bytes 12296 | tf_op jit(solution)/shard_map/ppermute | solution.py:329
  48.8 0.1 pad_add_fusion.place
  48.9 0.0 collective-permute-done.5
  48.9 3.7 %collective-permute-done.4 = f32[8,128]{1,0:T(8,128)S(1)} collective-permute-done((f32[8,128]{1,0:T(8,128)S(1)}, f32[8,128]{1,0:T(8,128)S(1)}, u32[]{:S(2)}, u32[]{:S(2)}) %collective-permute-start.4) | collective-permute-done | bytes 4128 | tf_op jit(solution)/shard_map/ppermute | solution.py:329
  52.6 0.0 all-to-all-done.all_ref
  52.6 0.0 copy-done
  52.6 0.0 copy-done.1
  52.6 2.6 %shard_map.95 = (f32[32,8,128]{2,1,0:T(8,128)}, f32[4,136,128]{2,1,0:T(8,128)S(1)}, f32[2,136,128]{2,1,0:T(8,128)}) custom-call(s32[1,4]{1,0:T(1,128)S(1)} %copy-done.1, s32[2]{0:T(128)S(1)} %pad_add_fusion.place, f32[8,4,128,128]{3,2,1,0:T(8,128)S(1)} %all-to-all-done.all_ref, f32[128,128]{1,0:T(8,128)S(1)} %copy-done, ...), custom_call_target="tpu_custom_call" | custom-call | tf_op jit(solution)/shard_map/pallas_call | solution.py:310
  55.2 12.1 %all-to-all-start.1 = ((f32[32,8,128]{2,1,0:T(8,128)}), f32[32,8,128]{2,1,0:T(8,128)S(1)}, u32[]{:S(2)}, u32[]{:S(2)}) async-start(f32[32,8,128]{2,1,0:T(8,128)} %get-tuple-element.15), calls=%async_computation.1 | async-start | bytes 262144 | tf_op jit(solution)/shard_map/all_to_all | solution.py:370
  67.4 11.8 %all-gather = f32[8,136,128]{2,1,0:T(8,128)S(1)} all-gather(f32[2,136,128]{2,1,0:T(8,128)} %get-tuple-element.17), channel_id=2, replica_groups=mesh['grp'=16,'row'=4,'col'=8] {'row'}, dimensions={0}, use_global_device_ids=true | all-gather | bytes 696320 | tf_op jit(solution)/shard_map/all_gather | solution.py:371
  79.1 0.0 all-to-all-done.1.z_ref
  79.1 3.9 %shard_map.96 = (f32[8,2,128,128]{3,2,1,0:T(8,128)}, f32[264,128]{1,0:T(8,128)}, f32[4,128,128]{2,1,0:T(8,128)S(1)}, f32[8,128]{1,0:T(8,128)S(1)}) custom-call(s32[1,4]{1,0:T(1,128)S(1)} %copy-done.1, s32[2]{0:T(128)S(1)} %pad_add_fusion.place, f32[8,4,128,128]{3,2,1,0:T(8,128)S(1)} %all-to-all-done.all_ref, f32[128,128]{1,0:T(8,128)S(1)} %copy-done, ...), custom_call_target="tpu_custom_call" | custom-call | tf_op jit(solution)/shard_map/pallas_call | solution.py:310
  83.0 6.7 %all-to-all-start.2 = ((f32[8,2,128,128]{3,2,1,0:T(8,128)}), f32[8,2,128,128]{3,2,1,0:T(8,128)S(1)}, u32[]{:S(2)}, u32[]{:S(2)}) async-start(f32[8,2,128,128]{3,2,1,0:T(8,128)} %get-tuple-element.18), calls=%async_computation.2 | async-start | bytes 2097152 | tf_op jit(solution)/shard_map/all_to_all | solution.py:385
  89.8 12.0 %all-gather.1 = f32[1056,128]{1,0:T(8,128)S(1)} all-gather(f32[264,128]{1,0:T(8,128)} %get-tuple-element.23), channel_id=3, replica_groups=mesh['grp'=16,'row'=4,'col'=8] {'row'}, dimensions={0}, use_global_device_ids=true | all-gather | bytes 675840 | tf_op jit(solution)/shard_map/all_gather | solution.py:386
  101.8 3.3 %shard_map.98 = f32[8,2,128,128]{3,2,1,0:T(8,128)} custom-call(s32[1,4]{1,0:T(1,128)S(1)} %copy-done.1, s32[2]{0:T(128)S(1)} %pad_add_fusion.place, f32[8,4,128,128]{3,2,1,0:T(8,128)S(1)} %all-to-all-done.all_ref, f32[128,128]{1,0:T(8,128)S(1)} %copy-done, f32[8,128]{1,0:T(8,128)S(1)} %get-tuple-element.21.peak_ref, ...), custom_call_target="tpu_custom_call" | custom-call | tf_op jit(solution)/shard_map/pallas_call | solution.py:310
  105.1 0.0 all-to-all-done.2.res_ref
  105.1 6.5 %all-to-all-start.3 = ((f32[8,2,128,128]{3,2,1,0:T(8,128)}), f32[8,2,128,128]{3,2,1,0:T(8,128)S(1)}, u32[]{:S(2)}, u32[]{:S(2)}) async-start(f32[8,2,128,128]{3,2,1,0:T(8,128)} %shard_map.98), calls=%async_computation.3 | async-start | bytes 2097152 | tf_op jit(solution)/shard_map/all_to_all | solution.py:395
  111.6 0.9 shard_map.97
  112.6 14.2 %all-to-all-done.3.res_ref = f32[8,2,128,128]{3,2,1,0:T(8,128)S(1)} async-done(((f32[8,2,128,128]{3,2,1,0:T(8,128)}), f32[8,2,128,128]{3,2,1,0:T(8,128)S(1)}, u32[]{:S(2)}, u32[]{:S(2)}) %all-to-all-start.3) | async-done | bytes 1048608 | tf_op jit(solution)/shard_map/all_to_all | solution.py:395
  126.7 0.9 shard_map.99
  (2 shorter events, 0.0 us)
Async XLA Ops:
  3.3 49.3 %copy-start = (f32[128,128]{1,0:T(8,128)S(1)}, f32[128,128]{1,0:T(8,128)}, u32[]{:S(2)}) copy-start(f32[128,128]{1,0:T(8,128)} %f_ref.7) | copy-start | bytes 196612
  3.3 49.3 %copy-start.1 = (s32[1,4]{1,0:T(1,128)S(1)}, s32[1,4]{1,0:T(1,128)}, u32[]{:S(2)}) copy-start(s32[1,4]{1,0:T(1,128)} %lens.5) | copy-start | bytes 52
  3.3 49.3 %all-to-all-start = ((f32[8,4,128,128]{3,2,1,0:T(8,128)}), f32[8,4,128,128]{3,2,1,0:T(8,128)S(1)}, u32[]{:S(2)}, u32[]{:S(2)}) async-start(f32[8,4,128,128]{3,2,1,0:T(8,128)} %shard_map.93), calls=%async_computation | async-start | bytes 4194304 | tf_op jit(solution)/shard_map/all_to_all | solution.py:359
  16.2 8.5 %collective-permute-start.1 = (f32[8,128]{1,0:T(8,128)}, f32[8,128]{1,0:T(8,128)S(1)}, u32[]{:S(2)}, u32[]{:S(2)}) collective-permute-start(f32[8,128]{1,0:T(8,128)} %shard_map.94), channel_id=1, source_target_pairs={{0,480},{32,0},{64,32},{96,64},{128,96},{160,128},{192,160},{224,1... | collective-permute-start | bytes 12296 | tf_op jit(solution)/shard_map/ppermute | solution.py:330
  22.7 6.1 %collective-permute-start = (f32[8,128]{1,0:T(8,128)}, f32[8,128]{1,0:T(8,128)S(1)}, u32[]{:S(2)}, u32[]{:S(2)}) collective-permute-start(f32[8,128]{1,0:T(8,128)} %shard_map.94), channel_id=1, source_target_pairs={{0,32},{32,64},{64,96},{96,128},{128,160},{160,192},{192,224},{224... | collective-permute-start | bytes 12296 | tf_op jit(solution)/shard_map/ppermute | solution.py:329
  29.5 7.1 %collective-permute-start.3 = (f32[8,128]{1,0:T(8,128)S(1)}, f32[8,128]{1,0:T(8,128)S(1)}, u32[]{:S(2)}, u32[]{:S(2)}) collective-permute-start(f32[8,128]{1,0:T(8,128)S(1)} %maximum_maximum_fusion.2), channel_id=1, source_target_pairs={{0,416},{32,448},{64,480},{96,0},{128,32},{160,64},{192,96},{224,1... | collective-permute-start | bytes 12296 | tf_op jit(solution)/shard_map/ppermute | solution.py:330
  32.3 7.4 %collective-permute-start.2 = (f32[8,128]{1,0:T(8,128)S(1)}, f32[8,128]{1,0:T(8,128)S(1)}, u32[]{:S(2)}, u32[]{:S(2)}) collective-permute-start(f32[8,128]{1,0:T(8,128)S(1)} %maximum_maximum_fusion.2), channel_id=1, source_target_pairs={{0,96},{32,128},{64,160},{96,192},{128,224},{160,256},{192,288},{2... | collective-permute-start | bytes 12296 | tf_op jit(solution)/shard_map/ppermute | solution.py:329
  39.7 9.3 %collective-permute-start.5 = (f32[8,128]{1,0:T(8,128)S(1)}, f32[8,128]{1,0:T(8,128)S(1)}, u32[]{:S(2)}, u32[]{:S(2)}) collective-permute-start(f32[8,128]{1,0:T(8,128)S(1)} %maximum_maximum_fusion.1), channel_id=1, source_target_pairs={{0,384},{32,416},{64,448},{96,480},{128,0},{160,32},{192,64},{224,... | collective-permute-start | bytes 12296 | tf_op jit(solution)/shard_map/ppermute | solution.py:330
  44.3 8.3 %collective-permute-start.4 = (f32[8,128]{1,0:T(8,128)S(1)}, f32[8,128]{1,0:T(8,128)S(1)}, u32[]{:S(2)}, u32[]{:S(2)}) collective-permute-start(f32[8,128]{1,0:T(8,128)S(1)} %maximum_maximum_fusion.1), channel_id=1, source_target_pairs={{0,128},{32,160},{64,192},{96,224},{128,256},{160,288},{192,320},{... | collective-permute-start | bytes 12296 | tf_op jit(solution)/shard_map/ppermute | solution.py:329
  55.2 23.9 %all-to-all-start.1 = ((f32[32,8,128]{2,1,0:T(8,128)}), f32[32,8,128]{2,1,0:T(8,128)S(1)}, u32[]{:S(2)}, u32[]{:S(2)}) async-start(f32[32,8,128]{2,1,0:T(8,128)} %get-tuple-element.15), calls=%async_computation.1 | async-start | bytes 262144 | tf_op jit(solution)/shard_map/all_to_all | solution.py:370
  83.0 22.1 %all-to-all-start.2 = ((f32[8,2,128,128]{3,2,1,0:T(8,128)}), f32[8,2,128,128]{3,2,1,0:T(8,128)S(1)}, u32[]{:S(2)}, u32[]{:S(2)}) async-start(f32[8,2,128,128]{3,2,1,0:T(8,128)} %get-tuple-element.18), calls=%async_computation.2 | async-start | bytes 2097152 | tf_op jit(solution)/shard_map/all_to_all | solution.py:385
  105.1 21.6 %all-to-all-start.3 = ((f32[8,2,128,128]{3,2,1,0:T(8,128)}), f32[8,2,128,128]{3,2,1,0:T(8,128)S(1)}, u32[]{:S(2)}, u32[]{:S(2)}) async-start(f32[8,2,128,128]{3,2,1,0:T(8,128)} %shard_map.98), calls=%async_computation.3 | async-start | bytes 2097152 | tf_op jit(solution)/shard_map/all_to_all | solution.py:395

commit v8 on v6

--- a/solution.py
+++ b/solution.py
@@ -18,7 +18,8 @@
 NN = (((1,), (0,)), ((), ()))
 NT = (((1,), (1,)), ((), ()))
 TN = (((0,), (0,)), ((), ()))
-K, V, Q, G = range(4)
+K, V = range(2)
+Q, G = range(2)
 OUT, GQ = range(2)
 GK, GV = range(2)
 VALUES, TOTALS, PEAK = M, M + 1, M + 2
@@ -84,8 +85,8 @@
         return (at >= low) & (at < low + self.lens[0, c])
 
 
-def pack_kernel(k_hbm, v_hbm, q_hbm, g_hbm, out_hbm, rows_ref, wide_ref, in_sem, out_sem):
-    sources = (k_hbm, v_hbm, q_hbm, g_hbm)
+def pack_kernel(first_hbm, second_hbm, out_hbm, rows_ref, wide_ref, in_sem, out_sem):
+    sources = (first_hbm, second_hbm)
     loads = [pltpu.make_async_copy(r, rows_ref.at[i], in_sem.at[i]) for i, r in enumerate(sources)]
     for load in loads:
         load.start()
@@ -93,16 +94,14 @@
         load.wait()
     stores = [pltpu.make_async_copy(wide_ref.at[h], out_hbm.at[h], out_sem.at[h]) for h in range(H)]
     for h in range(H):
-        for i in range(4):
+        for i in range(2):
             wide_ref[h, i] = rows_ref[i, :, head(h)].astype(F32)
         stores[h].start()
     for store in stores:
         store.wait()
 
 
-def state_kernel(
-    lens, place, all_ref, f_ref, z_hbm, s_ref, send_hbm, er_ref, send_ref, z_ref, sem, z_sem
-):
+def state_kernel(lens, place, all_ref, f_ref, s_ref, send_hbm, er_ref, send_ref, sem):
     blocks, _, rows, _ = all_ref.shape
     chains = Chains(lens, place[0], blocks, rows)
     parts = split3(f_ref[...])
@@ -113,10 +112,6 @@
         peak = jnp.maximum(peak, jnp.max(logits, axis=(0, 1), keepdims=True))
     for b in range(blocks):
         er_ref[b] = jnp.exp(er_ref[b] - peak)
-    for i in range(z_ref.shape[0]):
-        z_ref[i] = jnp.broadcast_to(peak, z_ref.shape[1:])
-    z_store = pltpu.make_async_copy(z_ref, z_hbm, z_sem)
-    z_store.start()
     s_ref[...] = jnp.zeros_like(s_ref)
     for c in range(CHAINS):
         s_ref[c, PEAK : PEAK + 1, :] = jnp.broadcast_to(peak, (1, D))
@@ -145,23 +140,26 @@
     send_ref[1] = s_ref[high] * (high != low).astype(F32)
     store = pltpu.make_async_copy(send_ref, send_hbm, sem)
     store.start()
-    z_store.wait()
     store.wait()
 
 
-def query_kernel(
-    lens, place, all_ref, f_ref, z_ref, s_ref, sent_ref,
-    res_hbm, send_hbm, b_ref, peak_ref,
-    qr_ref, full_ref, num_ref, gs_ref, inv_ref, tr_ref, t_ref, bt_ref, res_ref, send_ref, res_sem, send_sem,
-):
+def peak_kernel(sent_ref, wait_ref, z_hbm, z_ref, sem):
+    peak = jnp.max(sent_ref[:, 0, PEAK : PEAK + 1, :], axis=0)
+    for i in range(z_ref.shape[0]):
+        z_ref[i] = jnp.broadcast_to(peak, z_ref.shape[1:])
+    store = pltpu.make_async_copy(z_ref, z_hbm, sem)
+    store.start()
+    store.wait()
+
+
+def ahead_kernel(lens, place, all_ref, f_ref, s_ref, sent_ref, full_ref, qr_ref, num_ref, gs_ref):
     blocks, _, rows, _ = all_ref.shape
     chains = Chains(lens, place[0], blocks, rows)
     parts = split3(f_ref[...])
     for b in range(blocks):
         ql = logits_of(all_ref[b, Q], parts)
         qr_ref[b] = jnp.exp(ql - jnp.max(ql, axis=1, keepdims=True)) * RATIO
-    peak = jnp.max(jnp.max(z_ref[...], axis=0), axis=0, keepdims=True)
-    peak_ref[...] = jnp.broadcast_to(peak, peak_ref.shape)
+    peak = jnp.max(sent_ref[:, 0, PEAK : PEAK + 1, :], axis=0)
     row = lax.broadcasted_iota(jnp.int32, (M + 8, D), 0)
     share = jnp.where(row == VALUES, 1.0, jnp.exp(s_ref[0, PEAK : PEAK + 1, :] - peak))
     for c in range(CHAINS):
@@ -176,15 +174,43 @@
                 full_ref[c] += sent_ref[r, i] * share
 
     for c in range(CHAINS):
+        full_ref[c, PEAK : PEAK + 1, :] = peak
+    low, high = chains.ends_of(chains.me)
+
+    def one(c, carry):
+        state = split(full_ref[c, :M, :])
+        for b in range(blocks):
+            mask = chains.mask(c, b)
+            num = dot3(split(qr_ref[b] + EPS * RATIO), state, NN)
+            num_ref[b] = jnp.where(mask, num, num_ref[b])
+            g = all_ref[b, G].astype(BF16)
+            gs = dot(g, state[0], NT) + dot(g, state[1], NT)
+            gs_ref[b] = jnp.where(mask, gs, gs_ref[b])
+        return carry
+
+    lax.fori_loop(low, high + 1, one, 0)
+
+
+def query_kernel(
+    lens, place, all_ref, f_ref, z_ref, full_ref, qr_ref, num_in, gs_in,
+    res_hbm, send_hbm, b_ref, peak_ref,
+    num_ref, gs_ref, inv_ref, tr_ref, t_ref, bt_ref, res_ref, send_ref, res_sem, send_sem,
+):
+    blocks, _, rows, _ = all_ref.shape
+    chains = Chains(lens, place[0], blocks, rows)
+    parts = split(f_ref[...])
+    peak = jnp.max(jnp.max(z_ref[...], axis=0), axis=0, keepdims=True)
+    peak_ref[...] = jnp.broadcast_to(peak, peak_ref.shape)
+    share = RATIO * jnp.exp(full_ref[0, PEAK : PEAK + 1, :] - peak)
+    for c in range(CHAINS):
         count = lens[0, c].astype(F32)
-        t_ref[c : c + 1, :] = RATIO * (full_ref[c, TOTALS : TOTALS + 1, :] + EPS * count)
+        t_ref[c : c + 1, :] = share * full_ref[c, TOTALS : TOTALS + 1, :] + EPS * RATIO * count
     b_ref[...] = jnp.zeros_like(b_ref)
     low, high = chains.ends_of(chains.me)
 
     def one(c, carry):
-        state = RATIO * (full_ref[c, :M, :] + EPS * full_ref[c, VALUES : VALUES + 1, :])
-        state = split(state)
         weights = t_ref[pl.ds(c, 1), :]
+        values = EPS * RATIO * full_ref[c, VALUES : VALUES + 1, :]
         back = jnp.zeros((M, D), F32)
         for b in range(blocks):
             mask = chains.mask(c, b)
@@ -192,18 +218,19 @@
             inv = 1.0 / jnp.sum(qf * weights, axis=1, keepdims=True)
             inv_ref[b] = jnp.where(mask, inv, inv_ref[b])
             tr_ref[b] = jnp.where(mask, weights, tr_ref[b])
-            num = dot3(split(qf), state, NN)
+            num = share * num_in[b] + jnp.sum(qf, axis=1, keepdims=True) * values
             num_ref[b] = jnp.where(mask, num, num_ref[b])
-            g = all_ref[b, G].astype(BF16)
-            gs = dot(g, state[0], NT) + dot(g, state[1], NT)
+            g = all_ref[b, G]
+            gs = share * gs_in[b] + jnp.sum(g * values, axis=1, keepdims=True)
             gs_ref[b] = jnp.where(mask, gs, gs_ref[b])
             hi, lo = split(jnp.where(mask, qf * inv, 0.0))
+            g = g.astype(BF16)
             back = back + (dot(hi, g, TN) + dot(lo, g, TN))
         b_ref[c] = back
         return carry
 
     lax.fori_loop(low, high + 1, one, 0)
-    feats = parts[:2]
+    feats = parts
     stores = [pltpu.make_async_copy(res_ref.at[b], res_hbm.at[b], res_sem.at[b]) for b in range(blocks)]
     for b in range(blocks):
         inv = inv_ref[b]
@@ -320,42 +347,55 @@
     groups, lines, blocks = (lax.axis_size(a) for a in ("grp", "row", "col"))
     wide = (blocks, rows, D)
     hbm = pl.BlockSpec(memory_space=pltpu.HBM)
-    packed = pl.pallas_call(
-        pack_kernel,
-        out_shape=f32(H, 4, rows, D),
-        in_specs=[hbm] * 4,
+    dma = pltpu.SemaphoreType.DMA
+    pair = (blocks, 2, rows, D)
+
+    def exchanged(*two):
+        packed = pl.pallas_call(
+            pack_kernel,
+            out_shape=pltpu.HBM((H, 2, rows, D), F32),
+            in_specs=[hbm] * 2,
+            out_specs=hbm,
+            scratch_shapes=[
+                pltpu.VMEM((2, rows, width), BF16), pltpu.VMEM((H, 2, rows, D), F32), dma((2,)), dma((H,)),
+            ],
+            compiler_params=pltpu.CompilerParams(vmem_limit_bytes=60 * 2**20),
+        )(*two)
+        return lax.all_to_all(packed, "col", 0, 0, tiled=True)
+
+    key_rows, query_rows = exchanged(k, v), exchanged(q, g)
+    states = (CHAINS, M + 8, D)
+    own_states, ends = call(
+        state_kernel,
+        [pltpu.VMEM(states, F32), pltpu.HBM((2, M + 8, D), F32)],
+        (*where, key_rows, features),
+        2,
+        [pltpu.VMEM(wide, F32), pltpu.VMEM((2, M + 8, D), F32), dma],
+    )
+    ends = lax.all_gather(ends, "row")
+    peers = (groups, 8, M)
+    peaks = pl.pallas_call(
+        peak_kernel,
+        out_shape=pltpu.HBM(peers, F32),
+        in_specs=[pl.BlockSpec(memory_space=pltpu.VMEM), pl.BlockSpec(memory_space=pl.ANY)],
         out_specs=hbm,
-        scratch_shapes=[
-            pltpu.VMEM((4, rows, width), BF16),
-            pltpu.VMEM((H, 4, rows, D), F32),
-            pltpu.SemaphoreType.DMA((4,)),
-            pltpu.SemaphoreType.DMA((H,)),
-        ],
-        compiler_params=pltpu.CompilerParams(vmem_limit_bytes=60 * 2**20),
-    )(k, v, q, g)
-    own = lax.all_to_all(packed, "col", 0, 0, tiled=True)
-    states = (CHAINS, M + 8, D)
-    peers = (groups * lines, 8, M)
-    dma = pltpu.SemaphoreType.DMA
-    peaks, own_states, ends = call(
-        state_kernel,
-        [pltpu.HBM(peers, F32), f32(*states), pltpu.HBM((2, M + 8, D), F32)],
-        (*where, own, features),
+        scratch_shapes=[pltpu.VMEM(peers, F32), dma],
+    )(ends, query_rows)
+    peaks = lax.all_to_all(peaks, "grp", 0, 0, tiled=True)
+    full_states, raised, products, grad_products = call(
+        ahead_kernel,
+        [f32(*states), f32(*wide), f32(*wide), f32(*wide)],
+        (*where, query_rows, features, own_states, ends),
         2,
-        [pltpu.VMEM(wide, F32), pltpu.VMEM((2, M + 8, D), F32), pltpu.VMEM(peers, F32), dma, dma],
     )
-    peaks = lax.all_to_all(peaks, ("grp", "row"), 0, 0, tiled=True)
-    ends = lax.all_gather(ends, "row")
-    pair = (blocks, 2, rows, D)
     back = (2 * M + 2 * CHAINS, D)
     small = (2 * CHAINS, M)
     first, back_ends, backs, peak = call(
         query_kernel,
-        [pltpu.HBM(pair, F32), pltpu.HBM(back, F32), f32(CHAINS, M, D), f32(*small)],
-        (*where, own, features, peaks, own_states, ends),
+        [pltpu.HBM(pair, F32), pltpu.HBM(back, F32), pltpu.VMEM((CHAINS, M, D), F32), f32(*small)],
+        (*where, query_rows, features, peaks, full_states, raised, products, grad_products),
         2,
-        [pltpu.VMEM(wide, F32), pltpu.VMEM(states, F32)]
-        + [pltpu.VMEM(wide, F32)] * 4
+        [pltpu.VMEM(wide, F32)] * 4
         + [pltpu.VMEM(small, F32)] * 2
         + [pltpu.VMEM(pair, F32), pltpu.VMEM(back, F32), dma((blocks,)), dma],
     )
@@ -364,7 +404,7 @@
     (second,) = call(
         key_kernel,
         [pltpu.HBM(pair, F32)],
-        (*where, own, features, peak, backs, back_ends),
+        (*where, key_rows, features, peak, backs, back_ends),
         2,
         [pltpu.VMEM(wide, F32), pltpu.VMEM((CHAINS, M, D), F32), pltpu.VMEM(small, F32)]
         + [pltpu.VMEM(wide, F32), pltpu.VMEM(pair, F32), dma((blocks,))],

time: 128 us -> 130 us (1.016)
  waiting for transfers between devices: 47 us -> 32.4 us
  Pallas kernels: 14.2 us -> 22 us
  local copies, waits for them, and re-layouts: 0.71 us -> 8.16 us
  starting transfers between devices: 39.4 us -> 42.7 us
  blocking collectives: 24.3 us -> 22.8 us
    all_to_all x2 -> x3, waiting for transfers between devices: 32.5 us -> 18.3 us  [the longest x2 13 us: exchanged(): return lax.all_to_all(packed, 'col', 0, 0, tiled=True)]
    unnamed x8 -> x26, local copies, waits for them, and re-layouts: 0.71 us -> 8.16 us
    pallas_call x5 -> x6, Pallas kernels: 11.6 us -> 16 us  [call(): pl.pallas_call(kernel, out_shape=shapes, in_specs=[smem] * scalars + [vme...]
    pallas_call x1 -> x3, Pallas kernels: 2.66 us -> 6 us  [the longest x2 4.23 us: exchanged(): pl.pallas_call(pack_kernel, out_shape=pltpu.HBM((H, 2, rows, D), F32), in...]
    all_to_all x2 -> x3, starting transfers between devices: 25.3 us -> 27.3 us  [the longest x2 14.7 us: exchanged(): return lax.all_to_all(packed, 'col', 0, 0, tiled=True)]
  transfers between devices with their start and end apart: 4 -> 5, of which waited for: 4 -> 3; matrix products, arithmetic and copies ran while one was open for 0% -> 0% of each run, Pallas kernels for 3% -> 10%
where the time goes in v8:
time: 130 us; the launch traced here: 129 us
  starting transfers between devices  42.7 us (33%)
  waiting for transfers between devices  32.4 us (25%)
  blocking collectives  22.8 us (18%)
  Pallas kernels  22 us (17%)
  local copies, waits for them, and re-layouts  8.16 us (6%)
    pallas_call x6, Pallas kernels, call(): pl.pallas_call(kernel, out_shape=shapes, in_specs=[smem] * scalars + [vme...  16 us
    all_to_all x2, starting transfers between devices, exchanged(): return lax.all_to_all(packed, 'col', 0, 0, tiled=True)  14.7 us
    all_to_all x1, waiting for transfers between devices, on_device(): second = lax.all_to_all(second, 'col', 0, 0, tiled=True)  14.2 us
    all_to_all x2, waiting for transfers between devices, exchanged(): return lax.all_to_all(packed, 'col', 0, 0, tiled=True)  13 us
    all_to_all x1, starting transfers between devices, on_device(): peaks = lax.all_to_all(peaks, 'grp', 0, 0, tiled=True)  12.6 us
    all_gather x1, blocking collectives, on_device(): ends = lax.all_gather(ends, 'row')  11.7 us
    all_gather x1, blocking collectives, on_device(): back_ends = lax.all_gather(back_ends, 'row')  11.1 us
    all_to_all x1, starting transfers between devices, on_device(): first = lax.all_to_all(first, 'col', 0, 0, tiled=True)  8.28 us
  transfers between devices with their start and end apart: 5, of which 3 were waited for; matrix products, arithmetic and copies ran while one was open for 0% of the time, Pallas kernels for 10%

profile of v8, /device:TPU:1, one launch (start us, length us, event | category | flops | bytes accessed | tf_op | source)
XLA Modules:
  0.0 128.9 jit_solution(45131805578924312)
XLA Ops:
  0.6 2.1 %shard_map.94 = f32[8,2,128,128]{3,2,1,0:T(8,128)} custom-call(bf16[128,1024]{1,0:T(8,128)(2,1)} %bitcast.15, bf16[128,1024]{1,0:T(8,128)(2,1)} %bitcast.16), custom_call_target="tpu_custom_call" | custom-call | tf_op jit(solution)/shard_map/pallas_call | solution.py:354
  2.7 10.3 %all-to-all-start.1 = ((f32[8,2,128,128]{3,2,1,0:T(8,128)}), f32[8,2,128,128]{3,2,1,0:T(8,128)S(1)}, u32[]{:S(2)}, u32[]{:S(2)}) async-start(f32[8,2,128,128]{3,2,1,0:T(8,128)} %shard_map.94), calls=%async_computation.1 | async-start | bytes 2097152 | tf_op jit(solution)/shard_map/all_to_all | solution.py:364
  13.1 2.1 %shard_map.93 = f32[8,2,128,128]{3,2,1,0:T(8,128)} custom-call(bf16[128,1024]{1,0:T(8,128)(2,1)} %bitcast.17, bf16[128,1024]{1,0:T(8,128)(2,1)} %bitcast.18), custom_call_target="tpu_custom_call" | custom-call | tf_op jit(solution)/shard_map/pallas_call | solution.py:354
  15.2 0.0 copy-start.4
  15.2 13.0 %all-to-all-done.1.all_ref = f32[8,2,128,128]{3,2,1,0:T(8,128)S(1)} async-done(((f32[8,2,128,128]{3,2,1,0:T(8,128)}), f32[8,2,128,128]{3,2,1,0:T(8,128)S(1)}, u32[]{:S(2)}, u32[]{:S(2)}) %all-to-all-start.1) | async-done | bytes 1048608 | tf_op jit(solution)/shard_map/all_to_all | solution.py:364
  28.2 4.3 %all-to-all-start = ((f32[8,2,128,128]{3,2,1,0:T(8,128)}), f32[8,2,128,128]{3,2,1,0:T(8,128)S(1)}, u32[]{:S(2)}, u32[]{:S(2)}) async-start(f32[8,2,128,128]{3,2,1,0:T(8,128)} %shard_map.93), calls=%async_computation | async-start | bytes 2097152 | tf_op jit(solution)/shard_map/all_to_all | solution.py:364
  32.5 0.0 copy-start.11
  32.5 0.1 pad_add_fusion.place
  32.6 0.0 copy-done.4
  32.6 0.6 copy-done.11
  33.2 3.0 %shard_map.95 = (f32[4,136,128]{2,1,0:T(8,128)S(1)}, f32[2,136,128]{2,1,0:T(8,128)}) custom-call(s32[1,4]{1,0:T(1,128)S(1)} %copy-done.11, s32[2]{0:T(128)S(1)} %pad_add_fusion.place, f32[8,2,128,128]{3,2,1,0:T(8,128)S(1)} %all-to-all-done.1.all_ref, f32[128,128]{1,0:T(8,128)S(1)} %copy-done.4), custom_call_target="tpu_custom_call" | custom-call | tf_op jit(solution)/shard_map/pallas_call | solution.py:328
  36.2 11.7 %all-gather = f32[8,136,128]{2,1,0:T(8,128)} all-gather(f32[2,136,128]{2,1,0:T(8,128)} %get-tuple-element.18), channel_id=2, replica_groups=mesh['grp'=16,'row'=4,'col'=8] {'row'}, dimensions={0}, use_global_device_ids=true | all-gather | bytes 696320 | tf_op jit(solution)/shard_map/all_gather | solution.py:375
  47.9 0.0 all-to-all-done.wait_ref.all_ref
  47.9 0.0 copy-start
  47.9 1.0 copy-done
  49.0 0.0 copy-start.3
  49.0 1.8 %shard_map.96 = f32[16,8,128]{2,1,0:T(8,128)} custom-call(f32[4,2,136,128]{3,2,1,0:T(8,128)} %bitcast.12, f32[8,2,128,128]{3,2,1,0:T(8,128)} %copy-done), custom_call_target="tpu_custom_call" | custom-call | tf_op jit(solution)/shard_map/pallas_call | solution.py:377
  50.7 12.6 %all-to-all-start.2 = ((f32[16,8,128]{2,1,0:T(8,128)}), f32[16,8,128]{2,1,0:T(8,128)}, u32[]{:S(2)}, u32[]{:S(2)}) async-start(f32[16,8,128]{2,1,0:T(8,128)} %shard_map.96), calls=%async_computation.2 | async-start | bytes 131072 | tf_op jit(solution)/shard_map/all_to_all | solution.py:384
  63.3 0.0 copy-done.3
  63.3 0.0 copy-start.1
  63.3 1.2 copy-done.1
  64.6 0.0 copy-start.2
  64.6 2.9 %shard_map.97 = (f32[4,136,128]{2,1,0:T(8,128)S(1)}, f32[8,128,128]{2,1,0:T(8,128)S(1)}, f32[8,128,128]{2,1,0:T(8,128)S(1)}, f32[8,128,128]{2,1,0:T(8,128)S(1)}) custom-call(s32[1,4]{1,0:T(1,128)S(1)} %copy-done.11, s32[2]{0:T(128)S(1)} %pad_add_fusion.place, f32[8,2,128,128]{3,2,1,0:T(8,128)S(1)} %copy-done.1, f32[128,128]{1,0:T(8,128)S(1)} %copy-done.4, ...), custom_call_target="tpu_custom_call" | custom-call | tf_op jit(solution)/shard_map/pallas_call | solution.py:328
  67.4 0.0 copy-start.5
  67.4 0.8 copy-done.5
  68.2 0.0 copy-start.7
  68.2 0.8 copy-done.7
  69.0 0.0 copy-start.9
  69.0 0.7 copy-done.9
  69.7 5.3 %all-to-all-done.2.z_ref = f32[16,8,128]{2,1,0:T(8,128)} async-done(((f32[16,8,128]{2,1,0:T(8,128)}), f32[16,8,128]{2,1,0:T(8,128)}, u32[]{:S(2)}, u32[]{:S(2)}) %all-to-all-start.2) | async-done | bytes 65568 | tf_op jit(solution)/shard_map/all_to_all | solution.py:384
  75.0 0.0 copy-done.2
  75.0 0.0 copy-start.6
  75.0 1.0 copy-done.6
  76.1 0.0 copy-start.8
  76.1 1.0 copy-done.8
  77.1 0.0 copy-start.10
  77.1 1.0 copy-done.10
  78.1 4.2 %shard_map.98 = (f32[8,2,128,128]{3,2,1,0:T(8,128)}, f32[264,128]{1,0:T(8,128)}, f32[4,128,128]{2,1,0:T(8,128)S(1)}, f32[8,128]{1,0:T(8,128)S(1)}) custom-call(s32[1,4]{1,0:T(1,128)S(1)} %copy-done.11, s32[2]{0:T(128)S(1)} %pad_add_fusion.place, f32[8,2,128,128]{3,2,1,0:T(8,128)S(1)} %copy-done.2, f32[128,128]{1,0:T(8,128)S(1)} %copy-done.4, ...), custom_call_target="tpu_custom_call" | custom-call | tf_op jit(solution)/shard_map/pallas_call | solution.py:328
  82.3 0.0 copy-start.12
  82.3 8.3 %all-to-all-start.3 = ((f32[8,2,128,128]{3,2,1,0:T(8,128)}), f32[8,2,128,128]{3,2,1,0:T(8,128)S(1)}, u32[]{:S(2)}, u32[]{:S(2)}) async-start(f32[8,2,128,128]{3,2,1,0:T(8,128)} %get-tuple-element.24), calls=%async_computation.3 | async-start | bytes 2097152 | tf_op jit(solution)/shard_map/all_to_all | solution.py:402
  90.6 0.0 copy-done.12
  90.6 11.1 %all-gather.1 = f32[1056,128]{1,0:T(8,128)S(1)} all-gather(f32[264,128]{1,0:T(8,128)S(1)} %copy-done.12), channel_id=3, replica_groups=mesh['grp'=16,'row'=4,'col'=8] {'row'}, dimensions={0}, use_global_device_ids=true | all-gather | bytes 675840 | tf_op jit(solution)/shard_map/all_gather | solution.py:403
  101.7 4.0 %shard_map.100 = f32[8,2,128,128]{3,2,1,0:T(8,128)} custom-call(s32[1,4]{1,0:T(1,128)S(1)} %copy-done.11, s32[2]{0:T(128)S(1)} %pad_add_fusion.place, f32[8,2,128,128]{3,2,1,0:T(8,128)S(1)} %all-to-all-done.1.all_ref, f32[128,128]{1,0:T(8,128)S(1)} %copy-done.4, f32[8,128]{1,0:T(8,128)S(1)} %get-tuple-element.27.peak_ref, ...), custom_call_target="tpu_custom_call" | custom-call | tf_op jit(solution)/shard_map/pallas_call | solution.py:328
  105.7 0.0 all-to-all-done.3.res_ref
  105.8 7.1 %all-to-all-start.4 = ((f32[8,2,128,128]{3,2,1,0:T(8,128)}), f32[8,2,128,128]{3,2,1,0:T(8,128)S(1)}, u32[]{:S(2)}, u32[]{:S(2)}) async-start(f32[8,2,128,128]{3,2,1,0:T(8,128)} %shard_map.100), calls=%async_computation.4 | async-start | bytes 2097152 | tf_op jit(solution)/shard_map/all_to_all | solution.py:412
  112.9 0.9 shard_map.99
  113.8 14.2 %all-to-all-done.4.res_ref = f32[8,2,128,128]{3,2,1,0:T(8,128)S(1)} async-done(((f32[8,2,128,128]{3,2,1,0:T(8,128)}), f32[8,2,128,128]{3,2,1,0:T(8,128)S(1)}, u32[]{:S(2)}, u32[]{:S(2)}) %all-to-all-start.4) | async-done | bytes 1048608 | tf_op jit(solution)/shard_map/all_to_all | solution.py:412
  128.0 0.9 shard_map.101
Async XLA Ops:
  2.7 25.5 %all-to-all-start.1 = ((f32[8,2,128,128]{3,2,1,0:T(8,128)}), f32[8,2,128,128]{3,2,1,0:T(8,128)S(1)}, u32[]{:S(2)}, u32[]{:S(2)}) async-start(f32[8,2,128,128]{3,2,1,0:T(8,128)} %shard_map.94), calls=%async_computation.1 | async-start | bytes 2097152 | tf_op jit(solution)/shard_map/all_to_all | solution.py:364
  15.2 17.4 %copy-start.4 = (f32[128,128]{1,0:T(8,128)S(1)}, f32[128,128]{1,0:T(8,128)}, u32[]{:S(2)}) copy-start(f32[128,128]{1,0:T(8,128)} %f_ref.7) | copy-start | bytes 196612
  28.2 19.7 %all-to-all-start = ((f32[8,2,128,128]{3,2,1,0:T(8,128)}), f32[8,2,128,128]{3,2,1,0:T(8,128)S(1)}, u32[]{:S(2)}, u32[]{:S(2)}) async-start(f32[8,2,128,128]{3,2,1,0:T(8,128)} %shard_map.93), calls=%async_computation | async-start | bytes 2097152 | tf_op jit(solution)/shard_map/all_to_all | solution.py:364
  32.5 0.7 copy-start.11
  47.9 1.0 copy-start
  49.0 14.4 %copy-start.3 = (f32[8,136,128]{2,1,0:T(8,128)S(1)}, f32[8,136,128]{2,1,0:T(8,128)}, u32[]{:S(2)}) copy-start(f32[8,136,128]{2,1,0:T(8,128)} %all-gather) | copy-start | bytes 1671172
  50.7 24.3 %all-to-all-start.2 = ((f32[16,8,128]{2,1,0:T(8,128)}), f32[16,8,128]{2,1,0:T(8,128)}, u32[]{:S(2)}, u32[]{:S(2)}) async-start(f32[16,8,128]{2,1,0:T(8,128)} %shard_map.96), calls=%async_computation.2 | async-start | bytes 131072 | tf_op jit(solution)/shard_map/all_to_all | solution.py:384
  63.3 1.2 copy-start.1
  64.6 10.5 %copy-start.2 = (f32[8,2,128,128]{3,2,1,0:T(8,128)S(1)}, f32[8,2,128,128]{3,2,1,0:T(8,128)}, u32[]{:S(2)}) copy-start(f32[8,2,128,128]{3,2,1,0:T(8,128)} %copy-done) | copy-start | bytes 3145732
  67.4 0.8 copy-start.5
  68.2 0.8 copy-start.7
  69.0 0.7 copy-start.9
  75.0 1.0 copy-start.6
  76.1 1.0 copy-start.8
  77.1 1.0 copy-start.10
  82.3 8.3 %copy-start.12 = (f32[264,128]{1,0:T(8,128)S(1)}, f32[264,128]{1,0:T(8,128)}, u32[]{:S(2)}) copy-start(f32[264,128]{1,0:T(8,128)} %get-tuple-element.29) | copy-start | bytes 405508
  82.3 23.4 %all-to-all-start.3 = ((f32[8,2,128,128]{3,2,1,0:T(8,128)}), f32[8,2,128,128]{3,2,1,0:T(8,128)S(1)}, u32[]{:S(2)}, u32[]{:S(2)}) async-start(f32[8,2,128,128]{3,2,1,0:T(8,128)} %get-tuple-element.24), calls=%async_computation.3 | async-start | bytes 2097152 | tf_op jit(solution)/shard_map/all_to_all | solution.py:402
  105.8 22.2 %all-to-all-start.4 = ((f32[8,2,128,128]{3,2,1,0:T(8,128)}), f32[8,2,128,128]{3,2,1,0:T(8,128)S(1)}, u32[]{:S(2)}, u32[]{:S(2)}) async-start(f32[8,2,128,128]{3,2,1,0:T(8,128)} %shard_map.100), calls=%async_computation.4 | async-start | bytes 2097152 | tf_op jit(solution)/shard_map/all_to_all | solution.py:412

commit v9 on v8

--- a/solution.py
+++ b/solution.py
@@ -143,23 +143,34 @@
     store.wait()
 
 
-def peak_kernel(sent_ref, wait_ref, z_hbm, z_ref, sem):
-    peak = jnp.max(sent_ref[:, 0, PEAK : PEAK + 1, :], axis=0)
+def peak_kernel(sent_hbm, wait_ref, z_hbm, tile_ref, z_ref, sems):
+    load = pltpu.make_async_copy(sent_hbm.at[:, 0, pl.ds(M, 8), :], tile_ref, sems.at[0])
+    load.start()
+    load.wait()
+    peak = jnp.max(tile_ref[:, PEAK - M : PEAK - M + 1, :], axis=0)
     for i in range(z_ref.shape[0]):
         z_ref[i] = jnp.broadcast_to(peak, z_ref.shape[1:])
-    store = pltpu.make_async_copy(z_ref, z_hbm, sem)
+    store = pltpu.make_async_copy(z_ref, z_hbm, sems.at[1])
     store.start()
     store.wait()
 
 
-def ahead_kernel(lens, place, all_ref, f_ref, s_ref, sent_ref, full_ref, qr_ref, num_ref, gs_ref):
+def ahead_kernel(
+    sent_hbm, lens, place, key_ref, all_ref, f_ref, s_ref,
+    full_ref, qr_ref, num_ref, gs_ref, num_eps_ref, gs_eps_ref, er_ref, sent_ref, sem,
+):
+    load = pltpu.make_async_copy(sent_hbm, sent_ref, sem)
+    load.start()
     blocks, _, rows, _ = all_ref.shape
     chains = Chains(lens, place[0], blocks, rows)
     parts = split3(f_ref[...])
     for b in range(blocks):
         ql = logits_of(all_ref[b, Q], parts)
         qr_ref[b] = jnp.exp(ql - jnp.max(ql, axis=1, keepdims=True)) * RATIO
+    load.wait()
     peak = jnp.max(sent_ref[:, 0, PEAK : PEAK + 1, :], axis=0)
+    for b in range(blocks):
+        er_ref[b] = jnp.exp(logits_of(key_ref[b, K], parts) - peak)
     row = lax.broadcasted_iota(jnp.int32, (M + 8, D), 0)
     share = jnp.where(row == VALUES, 1.0, jnp.exp(s_ref[0, PEAK : PEAK + 1, :] - peak))
     for c in range(CHAINS):
@@ -179,11 +190,18 @@
 
     def one(c, carry):
         state = split(full_ref[c, :M, :])
+        values = EPS * RATIO * full_ref[c, VALUES : VALUES + 1, :]
         for b in range(blocks):
             mask = chains.mask(c, b)
-            num = dot3(split(qr_ref[b] + EPS * RATIO), state, NN)
+            qf = qr_ref[b] + EPS * RATIO
+            num = dot3(split(qf), state, NN)
             num_ref[b] = jnp.where(mask, num, num_ref[b])
-            g = all_ref[b, G].astype(BF16)
+            num_eps = jnp.sum(qf, axis=1, keepdims=True) * values
+            num_eps_ref[b] = jnp.where(mask, num_eps, num_eps_ref[b])
+            g = all_ref[b, G]
+            gs_eps = jnp.sum(g * values, axis=1, keepdims=True)
+            gs_eps_ref[b] = jnp.where(mask, gs_eps, gs_eps_ref[b])
+            g = g.astype(BF16)
             gs = dot(g, state[0], NT) + dot(g, state[1], NT)
             gs_ref[b] = jnp.where(mask, gs, gs_ref[b])
         return carry
@@ -192,16 +210,16 @@
 
 
 def query_kernel(
-    lens, place, all_ref, f_ref, z_ref, full_ref, qr_ref, num_in, gs_in,
-    res_hbm, send_hbm, b_ref, peak_ref,
-    num_ref, gs_ref, inv_ref, tr_ref, t_ref, bt_ref, res_ref, send_ref, res_sem, send_sem,
+    lens, place, all_ref, f_ref, z_ref, full_ref, qr_ref, num_ref, gs_ref, num_eps_ref, gs_eps_ref,
+    res_hbm, send_hbm, b_ref, share_ref,
+    bt_rows, inv_ref, tr_ref, t_ref, bt_ref, res_ref, send_ref, res_sem, send_sem,
 ):
     blocks, _, rows, _ = all_ref.shape
     chains = Chains(lens, place[0], blocks, rows)
     parts = split(f_ref[...])
     peak = jnp.max(jnp.max(z_ref[...], axis=0), axis=0, keepdims=True)
-    peak_ref[...] = jnp.broadcast_to(peak, peak_ref.shape)
     share = RATIO * jnp.exp(full_ref[0, PEAK : PEAK + 1, :] - peak)
+    share_ref[...] = jnp.broadcast_to(share, share_ref.shape)
     for c in range(CHAINS):
         count = lens[0, c].astype(F32)
         t_ref[c : c + 1, :] = share * full_ref[c, TOTALS : TOTALS + 1, :] + EPS * RATIO * count
@@ -210,7 +228,6 @@
 
     def one(c, carry):
         weights = t_ref[pl.ds(c, 1), :]
-        values = EPS * RATIO * full_ref[c, VALUES : VALUES + 1, :]
         back = jnp.zeros((M, D), F32)
         for b in range(blocks):
             mask = chains.mask(c, b)
@@ -218,13 +235,8 @@
             inv = 1.0 / jnp.sum(qf * weights, axis=1, keepdims=True)
             inv_ref[b] = jnp.where(mask, inv, inv_ref[b])
             tr_ref[b] = jnp.where(mask, weights, tr_ref[b])
-            num = share * num_in[b] + jnp.sum(qf, axis=1, keepdims=True) * values
-            num_ref[b] = jnp.where(mask, num, num_ref[b])
-            g = all_ref[b, G]
-            gs = share * gs_in[b] + jnp.sum(g * values, axis=1, keepdims=True)
-            gs_ref[b] = jnp.where(mask, gs, gs_ref[b])
             hi, lo = split(jnp.where(mask, qf * inv, 0.0))
-            g = g.astype(BF16)
+            g = all_ref[b, G].astype(BF16)
             back = back + (dot(hi, g, TN) + dot(lo, g, TN))
         b_ref[c] = back
         return carry
@@ -234,12 +246,13 @@
     stores = [pltpu.make_async_copy(res_ref.at[b], res_hbm.at[b], res_sem.at[b]) for b in range(blocks)]
     for b in range(blocks):
         inv = inv_ref[b]
-        exact = num_ref[b] * inv
+        exact = (share * num_ref[b] + num_eps_ref[b]) * inv
         res_ref[b, OUT] = exact
         grad_denom = -jnp.sum(all_ref[b, G] * exact, axis=1, keepdims=True) * inv
         raised = qr_ref[b]
-        num_ref[b] = (raised + EPS * RATIO) * grad_denom
-        grad_logits = (gs_ref[b] * inv + grad_denom * tr_ref[b]) * raised
+        bt_rows[b] = (raised + EPS * RATIO) * grad_denom
+        gs = share * gs_ref[b] + gs_eps_ref[b]
+        grad_logits = (gs * inv + grad_denom * tr_ref[b]) * raised
         back = dot3(split(grad_logits), feats, NN)
         back = back - jnp.sum(grad_logits, axis=1, keepdims=True) * (SCALE * all_ref[b, Q])
         res_ref[b, GQ] = back * SCALE
@@ -249,7 +262,7 @@
     def two(c, carry):
         total = jnp.zeros((rows, M), F32)
         for b in range(blocks):
-            total = total + jnp.where(chains.mask(c, b), num_ref[b], 0.0)
+            total = total + jnp.where(chains.mask(c, b), bt_rows[b], 0.0)
         bt_ref[pl.ds(c, 1), :] = jnp.sum(total, axis=0, keepdims=True)
         return carry
 
@@ -265,15 +278,14 @@
 
 
 def key_kernel(
-    lens, place, all_ref, f_ref, peak_ref, b_ref, sent_ref,
+    lens, place, all_ref, f_ref, er_ref, share_ref, b_ref, sent_ref,
     res_hbm, kr_ref, full_ref, sum_ref, dk_ref, res_ref, res_sem,
 ):
     blocks, _, rows, _ = all_ref.shape
     chains = Chains(lens, place[0], blocks, rows)
-    parts = split3(f_ref[...])
-    peak = peak_ref[0:1, :]
-    for b in range(blocks):
-        kr_ref[b] = jnp.exp(logits_of(all_ref[b, K], parts) - peak) * RATIO
+    share = share_ref[0:1, :]
+    for b in range(blocks):
+        kr_ref[b] = er_ref[b] * share
     full_ref[...] = b_ref[...]
     for r in range(sent_ref.shape[0]):
         low, high = chains.ends_of(r)
@@ -299,7 +311,7 @@
         return carry
 
     lax.fori_loop(low, high + 1, one, 0)
-    feats = parts[:2]
+    feats = split(f_ref[...])
     stores = [pltpu.make_async_copy(res_ref.at[b], res_hbm.at[b], res_sem.at[b]) for b in range(blocks)]
     for b in range(blocks):
         grad_logits = dk_ref[b] * kr_ref[b]
@@ -321,14 +333,16 @@
     return getattr(shape, "memory_space", None) is pltpu.HBM
 
 
-def call(kernel, shapes, args, scalars=0, scratch=()):
+def call(kernel, shapes, args, scalars=0, scratch=(), anys=0):
     vmem = pl.BlockSpec(memory_space=pltpu.VMEM)
     smem = pl.BlockSpec(memory_space=pltpu.SMEM)
     hbm = pl.BlockSpec(memory_space=pltpu.HBM)
     return pl.pallas_call(
         kernel,
         out_shape=shapes,
-        in_specs=[smem] * scalars + [vmem] * (len(args) - scalars),
+        in_specs=[pl.BlockSpec(memory_space=pl.ANY)] * anys
+        + [smem] * scalars
+        + [vmem] * (len(args) - anys - scalars),
         out_specs=[hbm if is_hbm(a) else vmem for a in shapes],
         scratch_shapes=list(scratch),
         compiler_params=pltpu.CompilerParams(vmem_limit_bytes=40 * 2**20),
@@ -377,25 +391,28 @@
     peaks = pl.pallas_call(
         peak_kernel,
         out_shape=pltpu.HBM(peers, F32),
-        in_specs=[pl.BlockSpec(memory_space=pltpu.VMEM), pl.BlockSpec(memory_space=pl.ANY)],
+        in_specs=[pl.BlockSpec(memory_space=pl.ANY)] * 2,
         out_specs=hbm,
-        scratch_shapes=[pltpu.VMEM(peers, F32), dma],
+        scratch_shapes=[pltpu.VMEM((lines, 8, D), F32), pltpu.VMEM(peers, F32), dma((2,))],
     )(ends, query_rows)
     peaks = lax.all_to_all(peaks, "grp", 0, 0, tiled=True)
-    full_states, raised, products, grad_products = call(
+    held = pltpu.VMEM(wide, F32)
+    full_states, *query_parts, key_raised = call(
         ahead_kernel,
-        [f32(*states), f32(*wide), f32(*wide), f32(*wide)],
-        (*where, query_rows, features, own_states, ends),
+        [pltpu.VMEM(states, F32)] + [held] * 6,
+        (ends, *where, key_rows, query_rows, features, own_states),
         2,
+        [pltpu.VMEM((lines, 2, M + 8, D), F32), dma],
+        anys=1,
     )
     back = (2 * M + 2 * CHAINS, D)
     small = (2 * CHAINS, M)
-    first, back_ends, backs, peak = call(
+    first, back_ends, backs, share = call(
         query_kernel,
         [pltpu.HBM(pair, F32), pltpu.HBM(back, F32), pltpu.VMEM((CHAINS, M, D), F32), f32(*small)],
-        (*where, query_rows, features, peaks, full_states, raised, products, grad_products),
+        (*where, query_rows, features, peaks, full_states, *query_parts),
         2,
-        [pltpu.VMEM(wide, F32)] * 4
+        [pltpu.VMEM(wide, F32)] * 3
         + [pltpu.VMEM(small, F32)] * 2
         + [pltpu.VMEM(pair, F32), pltpu.VMEM(back, F32), dma((blocks,)), dma],
     )
@@ -404,7 +421,7 @@
     (second,) = call(
         key_kernel,
         [pltpu.HBM(pair, F32)],
-        (*where, key_rows, features, peak, backs, back_ends),
+        (*where, key_rows, features, key_raised, share, backs, back_ends),
         2,
         [pltpu.VMEM(wide, F32), pltpu.VMEM((CHAINS, M, D), F32), pltpu.VMEM(small, F32)]
         + [pltpu.VMEM(wide, F32), pltpu.VMEM(pair, F32), dma((blocks,))],

time: 130 us -> 130 us (level)
  local copies, waits for them, and re-layouts: 8.16 us -> 12.9 us
  Pallas kernels: 22 us -> 18.8 us
  waiting for transfers between devices: 32.4 us -> 30.7 us
    unnamed x26 -> x38, local copies, waits for them, and re-layouts: 8.16 us -> 12.9 us
    pallas_call x6, Pallas kernels: 16 us -> 13.1 us  [call(): pl.pallas_call(kernel, out_shape=shapes, in_specs=[pl.BlockSpec(memory_sp...]
    all_to_all x1, waiting for transfers between devices: 5.3 us -> 2.53 us  [on_device(): peaks = lax.all_to_all(peaks, 'grp', 0, 0, tiled=True)]
  transfers between devices with their start and end apart: 5 -> 5, of which waited for: 3 -> 4; matrix products, arithmetic and copies ran while one was open for 0% -> 0% of each run, Pallas kernels for 10% -> 9%
where the time goes in v9:
time: 130 us; the launch traced here: 129 us
  starting transfers between devices  42.4 us (33%)
  waiting for transfers between devices  30.7 us (24%)
  blocking collectives  23.3 us (18%)
  Pallas kernels  18.8 us (14%)
  local copies, waits for them, and re-layouts  12.9 us (10%)
    all_to_all x2, starting transfers between devices, exchanged(): return lax.all_to_all(packed, 'col', 0, 0, tiled=True)  14.7 us
    all_to_all x1, waiting for transfers between devices, on_device(): second = lax.all_to_all(second, 'col', 0, 0, tiled=True)  14.2 us
    all_to_all x1, starting transfers between devices, on_device(): peaks = lax.all_to_all(peaks, 'grp', 0, 0, tiled=True)  13.3 us
    pallas_call x6, Pallas kernels, call(): pl.pallas_call(kernel, out_shape=shapes, in_specs=[pl.BlockSpec(memory_sp...  13.1 us
    all_to_all x2, waiting for transfers between devices, exchanged(): return lax.all_to_all(packed, 'col', 0, 0, tiled=True)  13 us
    unnamed x38, local copies, waits for them, and re-layouts  12.9 us
    all_gather x1, blocking collectives, on_device(): ends = lax.all_gather(ends, 'row')  11.9 us
    all_gather x1, blocking collectives, on_device(): back_ends = lax.all_gather(back_ends, 'row')  11.4 us
  transfers between devices with their start and end apart: 5, of which 4 were waited for; matrix products, arithmetic and copies ran while one was open for 0% of the time, Pallas kernels for 9%

profile of v9, /device:TPU:1, one launch (start us, length us, event | category | flops | bytes accessed | tf_op | source)
XLA Modules:
  0.0 128.9 jit_solution(15429071225037850833)
XLA Ops:
  0.6 2.1 %shard_map.94 = f32[8,2,128,128]{3,2,1,0:T(8,128)} custom-call(bf16[128,1024]{1,0:T(8,128)(2,1)} %bitcast.15, bf16[128,1024]{1,0:T(8,128)(2,1)} %bitcast.16), custom_call_target="tpu_custom_call" | custom-call | tf_op jit(solution)/shard_map/pallas_call | solution.py:368
  2.7 10.3 %all-to-all-start.1 = ((f32[8,2,128,128]{3,2,1,0:T(8,128)}), f32[8,2,128,128]{3,2,1,0:T(8,128)S(1)}, u32[]{:S(2)}, u32[]{:S(2)}) async-start(f32[8,2,128,128]{3,2,1,0:T(8,128)} %shard_map.94), calls=%async_computation.1 | async-start | bytes 2097152 | tf_op jit(solution)/shard_map/all_to_all | solution.py:378
  13.1 2.1 %shard_map.93 = f32[8,2,128,128]{3,2,1,0:T(8,128)} custom-call(bf16[128,1024]{1,0:T(8,128)(2,1)} %bitcast.17, bf16[128,1024]{1,0:T(8,128)(2,1)} %bitcast.18), custom_call_target="tpu_custom_call" | custom-call | tf_op jit(solution)/shard_map/pallas_call | solution.py:368
  15.2 0.0 copy-start.4
  15.2 13.0 %all-to-all-done.1.all_ref.key_ref = f32[8,2,128,128]{3,2,1,0:T(8,128)S(1)} async-done(((f32[8,2,128,128]{3,2,1,0:T(8,128)}), f32[8,2,128,128]{3,2,1,0:T(8,128)S(1)}, u32[]{:S(2)}, u32[]{:S(2)}) %all-to-all-start.1) | async-done | bytes 1048608 | tf_op jit(solution)/shard_map/all_to_all | solution.py:378
  28.2 4.3 %all-to-all-start = ((f32[8,2,128,128]{3,2,1,0:T(8,128)}), f32[8,2,128,128]{3,2,1,0:T(8,128)S(1)}, u32[]{:S(2)}, u32[]{:S(2)}) async-start(f32[8,2,128,128]{3,2,1,0:T(8,128)} %shard_map.93), calls=%async_computation | async-start | bytes 2097152 | tf_op jit(solution)/shard_map/all_to_all | solution.py:378
  32.5 0.0 copy-start.17
  32.5 0.1 pad_add_fusion.place
  32.6 0.0 copy-done.4
  32.6 0.6 copy-done.17
  33.2 2.6 %shard_map.95 = (f32[4,136,128]{2,1,0:T(8,128)S(1)}, f32[2,136,128]{2,1,0:T(8,128)}) custom-call(s32[1,4]{1,0:T(1,128)S(1)} %copy-done.17, s32[2]{0:T(128)S(1)} %pad_add_fusion.place, f32[8,2,128,128]{3,2,1,0:T(8,128)S(1)} %all-to-all-done.1.all_ref.key_ref, f32[128,128]{1,0:T(8,128)S(1)} %copy-done.4), custom_call_target="tpu_custom_call" | custom-call | tf_op jit(solution)/shard_map/pallas_call | solution.py:340
  35.8 0.0 copy-start.15
  35.8 11.9 %all-gather = f32[8,136,128]{2,1,0:T(8,128)} all-gather(f32[2,136,128]{2,1,0:T(8,128)} %get-tuple-element.21), channel_id=2, replica_groups=mesh['grp'=16,'row'=4,'col'=8] {'row'}, dimensions={0}, use_global_device_ids=true | all-gather | bytes 696320 | tf_op jit(solution)/shard_map/all_gather | solution.py:389
  47.7 0.0 copy-done.15
  47.7 0.0 all-to-all-done.wait_ref.all_ref
  47.7 0.0 copy-start
  47.7 1.0 copy-done
  48.7 1.4 %shard_map.96 = f32[16,8,128]{2,1,0:T(8,128)} custom-call(f32[4,2,136,128]{3,2,1,0:T(8,128)} %bitcast.12, f32[8,2,128,128]{3,2,1,0:T(8,128)} %copy-done), custom_call_target="tpu_custom_call" | custom-call | tf_op jit(solution)/shard_map/pallas_call | solution.py:391
  50.1 13.3 %all-to-all-start.2 = ((f32[16,8,128]{2,1,0:T(8,128)}), f32[16,8,128]{2,1,0:T(8,128)}, u32[]{:S(2)}, u32[]{:S(2)}) async-start(f32[16,8,128]{2,1,0:T(8,128)} %shard_map.96), calls=%async_computation.2 | async-start | bytes 131072 | tf_op jit(solution)/shard_map/all_to_all | solution.py:398
  63.4 0.0 copy-done.3
  63.4 0.0 copy-start.1
  63.5 1.2 copy-done.1
  64.7 1.0 copy-done.16
  65.6 3.0 %shard_map.97 = (f32[4,136,128]{2,1,0:T(8,128)S(1)}, f32[8,128,128]{2,1,0:T(8,128)S(1)}, f32[8,128,128]{2,1,0:T(8,128)S(1)}, f32[8,128,128]{2,1,0:T(8,128)S(1)},...) custom-call(f32[4,2,136,128]{3,2,1,0:T(8,128)S(1)} %bitcast.13, ...), custom_call_target="tpu_custom_call" | custom-call | tf_op jit(solution)/shard_map/pallas_call | solution.py:340
  68.6 0.0 copy-start.5
  68.7 0.8 copy-done.5
  69.4 0.8 copy-done.7
  70.2 0.8 copy-done.9
  71.0 0.8 copy-done.11
  71.8 0.8 copy-done.13
  72.6 2.5 %all-to-all-done.2.z_ref = f32[16,8,128]{2,1,0:T(8,128)} async-done(((f32[16,8,128]{2,1,0:T(8,128)}), f32[16,8,128]{2,1,0:T(8,128)}, u32[]{:S(2)}, u32[]{:S(2)}) %all-to-all-start.2) | async-done | bytes 65568 | tf_op jit(solution)/shard_map/all_to_all | solution.py:398
  75.2 0.0 copy-done.2
  75.2 1.0 copy-done.6
  76.2 1.0 copy-done.8
  77.2 1.0 copy-done.10
  78.3 1.0 copy-done.12
  79.3 1.0 copy-done.14
  80.4 3.0 %shard_map.98 = (f32[8,2,128,128]{3,2,1,0:T(8,128)}, f32[264,128]{1,0:T(8,128)}, f32[4,128,128]{2,1,0:T(8,128)S(1)}, f32[8,128]{1,0:T(8,128)S(1)}) custom-call(s32[1,4]{1,0:T(1,128)S(1)} %copy-done.17, s32[2]{0:T(128)S(1)} %pad_add_fusion.place, f32[8,2,128,128]{3,2,1,0:T(8,128)S(1)} %copy-done.2, f32[128,128]{1,0:T(8,128)S(1)} %copy-done.4, ...), custom_call_target="tpu_custom_call" | custom-call | tf_op jit(solution)/shard_map/pallas_call | solution.py:340
  83.4 0.0 copy-start.18
  83.4 8.3 %all-to-all-start.3 = ((f32[8,2,128,128]{3,2,1,0:T(8,128)}), f32[8,2,128,128]{3,2,1,0:T(8,128)S(1)}, u32[]{:S(2)}, u32[]{:S(2)}) async-start(f32[8,2,128,128]{3,2,1,0:T(8,128)} %get-tuple-element.29), calls=%async_computation.3 | async-start | bytes 2097152 | tf_op jit(solution)/shard_map/all_to_all | solution.py:419
  91.7 0.0 copy-done.18
  91.7 11.4 %all-gather.1 = f32[1056,128]{1,0:T(8,128)S(1)} all-gather(f32[264,128]{1,0:T(8,128)S(1)} %copy-done.18), channel_id=3, replica_groups=mesh['grp'=16,'row'=4,'col'=8] {'row'}, dimensions={0}, use_global_device_ids=true | all-gather | bytes 675840 | tf_op jit(solution)/shard_map/all_gather | solution.py:420
  103.1 2.7 %shard_map.100 = f32[8,2,128,128]{3,2,1,0:T(8,128)} custom-call(s32[1,4]{1,0:T(1,128)S(1)} %copy-done.17, s32[2]{0:T(128)S(1)} %pad_add_fusion.place, f32[8,2,128,128]{3,2,1,0:T(8,128)S(1)} %all-to-all-done.1.all_ref.key_ref, f32[128,128]{1,0:T(8,128)S(1)} %copy-done.4, f32[8,128,128]{2,1,0:T(8,128)S(1)} %get-tuple-element.32.er_ref, ...), custom_call_target="tpu_custom_call" | custom-call | tf_op jit(solution)/shard_map/pallas_call | solution.py:340
  105.8 1.0 all-to-all-done.3.res_ref
  106.8 6.1 %all-to-all-start.4 = ((f32[8,2,128,128]{3,2,1,0:T(8,128)}), f32[8,2,128,128]{3,2,1,0:T(8,128)S(1)}, u32[]{:S(2)}, u32[]{:S(2)}) async-start(f32[8,2,128,128]{3,2,1,0:T(8,128)} %shard_map.100), calls=%async_computation.4 | async-start | bytes 2097152 | tf_op jit(solution)/shard_map/all_to_all | solution.py:429
  112.9 0.9 shard_map.99
  113.8 14.2 %all-to-all-done.4.res_ref = f32[8,2,128,128]{3,2,1,0:T(8,128)S(1)} async-done(((f32[8,2,128,128]{3,2,1,0:T(8,128)}), f32[8,2,128,128]{3,2,1,0:T(8,128)S(1)}, u32[]{:S(2)}, u32[]{:S(2)}) %all-to-all-start.4) | async-done | bytes 1048608 | tf_op jit(solution)/shard_map/all_to_all | solution.py:429
  128.0 0.9 shard_map.101
  (12 shorter events, 0.0 us)
Async XLA Ops:
  2.7 25.5 %all-to-all-start.1 = ((f32[8,2,128,128]{3,2,1,0:T(8,128)}), f32[8,2,128,128]{3,2,1,0:T(8,128)S(1)}, u32[]{:S(2)}, u32[]{:S(2)}) async-start(f32[8,2,128,128]{3,2,1,0:T(8,128)} %shard_map.94), calls=%async_computation.1 | async-start | bytes 2097152 | tf_op jit(solution)/shard_map/all_to_all | solution.py:378
  15.2 17.4 %copy-start.4 = (f32[128,128]{1,0:T(8,128)S(1)}, f32[128,128]{1,0:T(8,128)}, u32[]{:S(2)}) copy-start(f32[128,128]{1,0:T(8,128)} %f_ref.7) | copy-start | bytes 196612
  28.2 19.5 %all-to-all-start = ((f32[8,2,128,128]{3,2,1,0:T(8,128)}), f32[8,2,128,128]{3,2,1,0:T(8,128)S(1)}, u32[]{:S(2)}, u32[]{:S(2)}) async-start(f32[8,2,128,128]{3,2,1,0:T(8,128)} %shard_map.93), calls=%async_computation | async-start | bytes 2097152 | tf_op jit(solution)/shard_map/all_to_all | solution.py:378
  32.5 0.7 copy-start.17
  35.8 11.9 %copy-start.15 = (f32[4,136,128]{2,1,0:T(8,128)}, f32[4,136,128]{2,1,0:T(8,128)S(1)}, u32[]{:S(2)}) copy-start(f32[4,136,128]{2,1,0:T(8,128)S(1)} %get-tuple-element.22.s_ref) | copy-start | bytes 835588
  47.7 1.0 copy-start
  48.7 14.8 %copy-start.3 = (f32[8,136,128]{2,1,0:T(8,128)S(1)}, f32[8,136,128]{2,1,0:T(8,128)}, u32[]{:S(2)}) copy-start(f32[8,136,128]{2,1,0:T(8,128)} %all-gather) | copy-start | bytes 1671172
  50.1 25.0 %all-to-all-start.2 = ((f32[16,8,128]{2,1,0:T(8,128)}), f32[16,8,128]{2,1,0:T(8,128)}, u32[]{:S(2)}, u32[]{:S(2)}) async-start(f32[16,8,128]{2,1,0:T(8,128)} %shard_map.96), calls=%async_computation.2 | async-start | bytes 131072 | tf_op jit(solution)/shard_map/all_to_all | solution.py:398
  63.4 1.2 copy-start.1
  64.7 1.0 copy-start.16
  65.6 9.5 %copy-start.2 = (f32[8,2,128,128]{3,2,1,0:T(8,128)S(1)}, f32[8,2,128,128]{3,2,1,0:T(8,128)}, u32[]{:S(2)}) copy-start(f32[8,2,128,128]{3,2,1,0:T(8,128)} %copy-done) | copy-start | bytes 3145732
  68.6 0.8 copy-start.5
  69.4 0.8 copy-start.7
  70.2 0.8 copy-start.9
  71.0 0.8 copy-start.11
  71.8 0.8 copy-start.13
  75.2 1.0 copy-start.6
  76.2 1.0 copy-start.8
  77.2 1.0 copy-start.10
  78.3 1.0 copy-start.12
  79.3 1.0 copy-start.14
  83.4 8.3 %copy-start.18 = (f32[264,128]{1,0:T(8,128)S(1)}, f32[264,128]{1,0:T(8,128)}, u32[]{:S(2)}) copy-start(f32[264,128]{1,0:T(8,128)} %get-tuple-element.35) | copy-start | bytes 405508
  83.4 23.4 %all-to-all-start.3 = ((f32[8,2,128,128]{3,2,1,0:T(8,128)}), f32[8,2,128,128]{3,2,1,0:T(8,128)S(1)}, u32[]{:S(2)}, u32[]{:S(2)}) async-start(f32[8,2,128,128]{3,2,1,0:T(8,128)} %get-tuple-element.29), calls=%async_computation.3 | async-start | bytes 2097152 | tf_op jit(solution)/shard_map/all_to_all | solution.py:419
  106.8 21.2 %all-to-all-start.4 = ((f32[8,2,128,128]{3,2,1,0:T(8,128)}), f32[8,2,128,128]{3,2,1,0:T(8,128)S(1)}, u32[]{:S(2)}, u32[]{:S(2)}) async-start(f32[8,2,128,128]{3,2,1,0:T(8,128)} %shard_map.100), calls=%async_computation.4 | async-start | bytes 2097152 | tf_op jit(solution)/shard_map/all_to_all | solution.py:429

commit v10 on v8

--- a/solution.py
+++ b/solution.py
@@ -143,23 +143,39 @@
     store.wait()
 
 
-def peak_kernel(sent_ref, wait_ref, z_hbm, z_ref, sem):
-    peak = jnp.max(sent_ref[:, 0, PEAK : PEAK + 1, :], axis=0)
+def peak_kernel(sent_hbm, wait_ref, z_hbm, tile_ref, z_ref, sems):
+    load = pltpu.make_async_copy(sent_hbm.at[:, 0, pl.ds(M, 8), :], tile_ref, sems.at[0])
+    load.start()
+    load.wait()
+    peak = jnp.max(tile_ref[:, PEAK - M : PEAK - M + 1, :], axis=0)
     for i in range(z_ref.shape[0]):
         z_ref[i] = jnp.broadcast_to(peak, z_ref.shape[1:])
-    store = pltpu.make_async_copy(z_ref, z_hbm, sem)
+    store = pltpu.make_async_copy(z_ref, z_hbm, sems.at[1])
     store.start()
     store.wait()
 
 
-def ahead_kernel(lens, place, all_ref, f_ref, s_ref, sent_ref, full_ref, qr_ref, num_ref, gs_ref):
+def raised_kernel(key_ref, f_ref, s_ref, er_ref):
+    parts = split3(f_ref[...])
+    peak = s_ref[0, PEAK : PEAK + 1, :]
+    for b in range(key_ref.shape[0]):
+        er_ref[b] = jnp.exp(logits_of(key_ref[b, K], parts) - peak)
+
+
+def query_kernel(
+    lens, place, all_ref, f_ref, z_ref, s_ref, sent_ref,
+    res_hbm, send_hbm, b_ref, share_ref,
+    qr_ref, full_ref, num_ref, gs_ref, inv_ref, tr_ref, t_ref, bt_ref, res_ref, send_ref, res_sem, send_sem,
+):
     blocks, _, rows, _ = all_ref.shape
     chains = Chains(lens, place[0], blocks, rows)
     parts = split3(f_ref[...])
     for b in range(blocks):
         ql = logits_of(all_ref[b, Q], parts)
         qr_ref[b] = jnp.exp(ql - jnp.max(ql, axis=1, keepdims=True)) * RATIO
-    peak = jnp.max(sent_ref[:, 0, PEAK : PEAK + 1, :], axis=0)
+    peak = jnp.max(jnp.max(z_ref[...], axis=0), axis=0, keepdims=True)
+    own_share = RATIO * jnp.exp(s_ref[0, PEAK : PEAK + 1, :] - peak)
+    share_ref[...] = jnp.broadcast_to(own_share, share_ref.shape)
     row = lax.broadcasted_iota(jnp.int32, (M + 8, D), 0)
     share = jnp.where(row == VALUES, 1.0, jnp.exp(s_ref[0, PEAK : PEAK + 1, :] - peak))
     for c in range(CHAINS):
@@ -174,43 +190,15 @@
                 full_ref[c] += sent_ref[r, i] * share
 
     for c in range(CHAINS):
-        full_ref[c, PEAK : PEAK + 1, :] = peak
-    low, high = chains.ends_of(chains.me)
-
-    def one(c, carry):
-        state = split(full_ref[c, :M, :])
-        for b in range(blocks):
-            mask = chains.mask(c, b)
-            num = dot3(split(qr_ref[b] + EPS * RATIO), state, NN)
-            num_ref[b] = jnp.where(mask, num, num_ref[b])
-            g = all_ref[b, G].astype(BF16)
-            gs = dot(g, state[0], NT) + dot(g, state[1], NT)
-            gs_ref[b] = jnp.where(mask, gs, gs_ref[b])
-        return carry
-
-    lax.fori_loop(low, high + 1, one, 0)
-
-
-def query_kernel(
-    lens, place, all_ref, f_ref, z_ref, full_ref, qr_ref, num_in, gs_in,
-    res_hbm, send_hbm, b_ref, peak_ref,
-    num_ref, gs_ref, inv_ref, tr_ref, t_ref, bt_ref, res_ref, send_ref, res_sem, send_sem,
-):
-    blocks, _, rows, _ = all_ref.shape
-    chains = Chains(lens, place[0], blocks, rows)
-    parts = split(f_ref[...])
-    peak = jnp.max(jnp.max(z_ref[...], axis=0), axis=0, keepdims=True)
-    peak_ref[...] = jnp.broadcast_to(peak, peak_ref.shape)
-    share = RATIO * jnp.exp(full_ref[0, PEAK : PEAK + 1, :] - peak)
-    for c in range(CHAINS):
         count = lens[0, c].astype(F32)
-        t_ref[c : c + 1, :] = share * full_ref[c, TOTALS : TOTALS + 1, :] + EPS * RATIO * count
+        t_ref[c : c + 1, :] = RATIO * (full_ref[c, TOTALS : TOTALS + 1, :] + EPS * count)
     b_ref[...] = jnp.zeros_like(b_ref)
     low, high = chains.ends_of(chains.me)
 
     def one(c, carry):
+        state = RATIO * (full_ref[c, :M, :] + EPS * full_ref[c, VALUES : VALUES + 1, :])
+        state = split(state)
         weights = t_ref[pl.ds(c, 1), :]
-        values = EPS * RATIO * full_ref[c, VALUES : VALUES + 1, :]
         back = jnp.zeros((M, D), F32)
         for b in range(blocks):
             mask = chains.mask(c, b)
@@ -218,19 +206,18 @@
             inv = 1.0 / jnp.sum(qf * weights, axis=1, keepdims=True)
             inv_ref[b] = jnp.where(mask, inv, inv_ref[b])
             tr_ref[b] = jnp.where(mask, weights, tr_ref[b])
-            num = share * num_in[b] + jnp.sum(qf, axis=1, keepdims=True) * values
+            num = dot3(split(qf), state, NN)
             num_ref[b] = jnp.where(mask, num, num_ref[b])
-            g = all_ref[b, G]
-            gs = share * gs_in[b] + jnp.sum(g * values, axis=1, keepdims=True)
+            g = all_ref[b, G].astype(BF16)
+            gs = dot(g, state[0], NT) + dot(g, state[1], NT)
             gs_ref[b] = jnp.where(mask, gs, gs_ref[b])
             hi, lo = split(jnp.where(mask, qf * inv, 0.0))
-            g = g.astype(BF16)
             back = back + (dot(hi, g, TN) + dot(lo, g, TN))
         b_ref[c] = back
         return carry
 
     lax.fori_loop(low, high + 1, one, 0)
-    feats = parts
+    feats = parts[:2]
     stores = [pltpu.make_async_copy(res_ref.at[b], res_hbm.at[b], res_sem.at[b]) for b in range(blocks)]
     for b in range(blocks):
         inv = inv_ref[b]
@@ -265,15 +252,14 @@
 
 
 def key_kernel(
-    lens, place, all_ref, f_ref, peak_ref, b_ref, sent_ref,
+    lens, place, all_ref, f_ref, er_ref, share_ref, b_ref, sent_ref,
     res_hbm, kr_ref, full_ref, sum_ref, dk_ref, res_ref, res_sem,
 ):
     blocks, _, rows, _ = all_ref.shape
     chains = Chains(lens, place[0], blocks, rows)
-    parts = split3(f_ref[...])
-    peak = peak_ref[0:1, :]
-    for b in range(blocks):
-        kr_ref[b] = jnp.exp(logits_of(all_ref[b, K], parts) - peak) * RATIO
+    share = share_ref[0:1, :]
+    for b in range(blocks):
+        kr_ref[b] = er_ref[b] * share
     full_ref[...] = b_ref[...]
     for r in range(sent_ref.shape[0]):
         low, high = chains.ends_of(r)
@@ -299,7 +285,7 @@
         return carry
 
     lax.fori_loop(low, high + 1, one, 0)
-    feats = parts[:2]
+    feats = split(f_ref[...])
     stores = [pltpu.make_async_copy(res_ref.at[b], res_hbm.at[b], res_sem.at[b]) for b in range(blocks)]
     for b in range(blocks):
         grad_logits = dk_ref[b] * kr_ref[b]
@@ -377,25 +363,21 @@
     peaks = pl.pallas_call(
         peak_kernel,
         out_shape=pltpu.HBM(peers, F32),
-        in_specs=[pl.BlockSpec(memory_space=pltpu.VMEM), pl.BlockSpec(memory_space=pl.ANY)],
+        in_specs=[pl.BlockSpec(memory_space=pl.ANY)] * 2,
         out_specs=hbm,
-        scratch_shapes=[pltpu.VMEM(peers, F32), dma],
+        scratch_shapes=[pltpu.VMEM((lines, 8, D), F32), pltpu.VMEM(peers, F32), dma((2,))],
     )(ends, query_rows)
     peaks = lax.all_to_all(peaks, "grp", 0, 0, tiled=True)
-    full_states, raised, products, grad_products = call(
-        ahead_kernel,
-        [f32(*states), f32(*wide), f32(*wide), f32(*wide)],
-        (*where, query_rows, features, own_states, ends),
-        2,
-    )
+    (key_raised,) = call(raised_kernel, [f32(*wide)], (key_rows, features, own_states))
     back = (2 * M + 2 * CHAINS, D)
     small = (2 * CHAINS, M)
-    first, back_ends, backs, peak = call(
+    first, back_ends, backs, share = call(
         query_kernel,
         [pltpu.HBM(pair, F32), pltpu.HBM(back, F32), pltpu.VMEM((CHAINS, M, D), F32), f32(*small)],
-        (*where, query_rows, features, peaks, full_states, raised, products, grad_products),
+        (*where, query_rows, features, peaks, own_states, ends),
         2,
-        [pltpu.VMEM(wide, F32)] * 4
+        [pltpu.VMEM(wide, F32), pltpu.VMEM(states, F32)]
+        + [pltpu.VMEM(wide, F32)] * 4
         + [pltpu.VMEM(small, F32)] * 2
         + [pltpu.VMEM(pair, F32), pltpu.VMEM(back, F32), dma((blocks,)), dma],
     )
@@ -404,7 +386,7 @@
     (second,) = call(
         key_kernel,
         [pltpu.HBM(pair, F32)],
-        (*where, key_rows, features, peak, backs, back_ends),
+        (*where, key_rows, features, key_raised, share, backs, back_ends),
         2,
         [pltpu.VMEM(wide, F32), pltpu.VMEM((CHAINS, M, D), F32), pltpu.VMEM(small, F32)]
         + [pltpu.VMEM(wide, F32), pltpu.VMEM(pair, F32), dma((blocks,))],

time: 130 us -> 126 us (0.969)
  blocking collectives: 22.8 us -> 47.7 us
  starting transfers between devices: 42.7 us -> 29.2 us
  local copies, waits for them, and re-layouts: 8.16 us -> 3.02 us
  Pallas kernels: 22 us -> 17.3 us
  waiting for transfers between devices: 32.4 us -> 27.8 us
    all_to_all x0 -> x1, blocking collectives: none -> 25 us  [on_device(): peaks = lax.all_to_all(peaks, 'grp', 0, 0, tiled=True)]
    all_to_all x1 -> x0, starting transfers between devices: 12.6 us -> none  [on_device(): peaks = lax.all_to_all(peaks, 'grp', 0, 0, tiled=True)]
    all_to_all x1 -> x0, waiting for transfers between devices: 5.3 us -> none  [on_device(): peaks = lax.all_to_all(peaks, 'grp', 0, 0, tiled=True)]
    unnamed x26 -> x12, local copies, waits for them, and re-layouts: 8.16 us -> 3.02 us
    pallas_call x6, Pallas kernels: 16 us -> 11.6 us  [call(): pl.pallas_call(kernel, out_shape=shapes, in_specs=[smem] * scalars + [vme...]
  transfers between devices with their start and end apart: 5 -> 4, of which waited for: 3 -> 3; matrix products, arithmetic and copies ran while one was open for 0% -> 0% of each run, Pallas kernels for 10% -> 7%
where the time goes in v10:
time: 126 us
  blocking collectives  47.7 us (38%)
  starting transfers between devices  29.2 us (23%)
  waiting for transfers between devices  27.8 us (22%)
  Pallas kernels  17.3 us (14%)
  local copies, waits for them, and re-layouts  3.02 us (2%)
    all_to_all x1, blocking collectives, on_device(): peaks = lax.all_to_all(peaks, 'grp', 0, 0, tiled=True)  25 us
    all_to_all x2, starting transfers between devices, exchanged(): return lax.all_to_all(packed, 'col', 0, 0, tiled=True)  14.7 us
    all_to_all x1, waiting for transfers between devices, on_device(): second = lax.all_to_all(second, 'col', 0, 0, tiled=True)  14.2 us
    all_to_all x2, waiting for transfers between devices, exchanged(): return lax.all_to_all(packed, 'col', 0, 0, tiled=True)  13 us
    all_gather x1, blocking collectives, on_device(): ends = lax.all_gather(ends, 'row')  11.9 us
    pallas_call x6, Pallas kernels, call(): pl.pallas_call(kernel, out_shape=shapes, in_specs=[smem] * scalars + [vme...  11.6 us
    all_gather x1, blocking collectives, on_device(): back_ends = lax.all_gather(back_ends, 'row')  10.8 us
    all_to_all x1, starting transfers between devices, on_device(): first = lax.all_to_all(first, 'col', 0, 0, tiled=True)  8.33 us
  transfers between devices with their start and end apart: 4, of which 3 were waited for; matrix products, arithmetic and copies ran while one was open for 0% of the time, Pallas kernels for 7%

profile of v10, /device:TPU:1, one launch (start us, length us, event | category | flops | bytes accessed | tf_op | source)
XLA Modules:
  0.0 125.8 jit_solution(729701884426067422)
XLA Ops:
  0.6 2.1 %shard_map.94 = f32[8,2,128,128]{3,2,1,0:T(8,128)} custom-call(bf16[128,1024]{1,0:T(8,128)(2,1)} %bitcast.15, bf16[128,1024]{1,0:T(8,128)(2,1)} %bitcast.16), custom_call_target="tpu_custom_call" | custom-call | tf_op jit(solution)/shard_map/pallas_call | solution.py:340
  2.8 10.3 %all-to-all-start.1 = ((f32[8,2,128,128]{3,2,1,0:T(8,128)}), f32[8,2,128,128]{3,2,1,0:T(8,128)S(1)}, u32[]{:S(2)}, u32[]{:S(2)}) async-start(f32[8,2,128,128]{3,2,1,0:T(8,128)} %shard_map.94), calls=%async_computation.1 | async-start | bytes 2097152 | tf_op jit(solution)/shard_map/all_to_all | solution.py:350
  13.1 2.1 %shard_map.93 = f32[8,2,128,128]{3,2,1,0:T(8,128)} custom-call(bf16[128,1024]{1,0:T(8,128)(2,1)} %bitcast.17, bf16[128,1024]{1,0:T(8,128)(2,1)} %bitcast.18), custom_call_target="tpu_custom_call" | custom-call | tf_op jit(solution)/shard_map/pallas_call | solution.py:340
  15.2 0.0 copy-start.3
  15.3 13.0 %all-to-all-done.1.all_ref.key_ref = f32[8,2,128,128]{3,2,1,0:T(8,128)S(1)} async-done(((f32[8,2,128,128]{3,2,1,0:T(8,128)}), f32[8,2,128,128]{3,2,1,0:T(8,128)S(1)}, u32[]{:S(2)}, u32[]{:S(2)}) %all-to-all-start.1) | async-done | bytes 1048608 | tf_op jit(solution)/shard_map/all_to_all | solution.py:350
  28.2 4.3 %all-to-all-start = ((f32[8,2,128,128]{3,2,1,0:T(8,128)}), f32[8,2,128,128]{3,2,1,0:T(8,128)S(1)}, u32[]{:S(2)}, u32[]{:S(2)}) async-start(f32[8,2,128,128]{3,2,1,0:T(8,128)} %shard_map.93), calls=%async_computation | async-start | bytes 2097152 | tf_op jit(solution)/shard_map/all_to_all | solution.py:350
  32.6 0.0 copy-start.4
  32.6 0.1 pad_add_fusion.place
  32.6 0.0 copy-done.3
  32.7 0.6 copy-done.4
  33.2 2.6 %shard_map.95 = (f32[4,136,128]{2,1,0:T(8,128)S(1)}, f32[2,136,128]{2,1,0:T(8,128)}) custom-call(s32[1,4]{1,0:T(1,128)S(1)} %copy-done.4, s32[2]{0:T(128)S(1)} %pad_add_fusion.place, f32[8,2,128,128]{3,2,1,0:T(8,128)S(1)} %all-to-all-done.1.all_ref.key_ref, f32[128,128]{1,0:T(8,128)S(1)} %copy-done.3), custom_call_target="tpu_custom_call" | custom-call | tf_op jit(solution)/shard_map/pallas_call | solution.py:314
  35.8 11.9 %all-gather = f32[8,136,128]{2,1,0:T(8,128)} all-gather(f32[2,136,128]{2,1,0:T(8,128)} %get-tuple-element.14), channel_id=2, replica_groups=mesh['grp'=16,'row'=4,'col'=8] {'row'}, dimensions={0}, use_global_device_ids=true | all-gather | bytes 696320 | tf_op jit(solution)/shard_map/all_gather | solution.py:361
  47.7 0.0 all-to-all-done.wait_ref.all_ref
  47.7 0.0 copy-start
  47.7 1.0 copy-done
  48.7 0.0 copy-start.2
  48.7 1.4 %shard_map.96 = f32[16,8,128]{2,1,0:T(8,128)} custom-call(f32[4,2,136,128]{3,2,1,0:T(8,128)} %bitcast.12, f32[8,2,128,128]{3,2,1,0:T(8,128)} %copy-done), custom_call_target="tpu_custom_call" | custom-call | tf_op jit(solution)/shard_map/pallas_call | solution.py:363
  50.1 25.0 %all_to_all.25.z_ref = f32[16,8,128]{2,1,0:T(8,128)S(1)} all-to-all(f32[16,8,128]{2,1,0:T(8,128)} %shard_map.96), channel_id=1, replica_groups=mesh['grp'=16,'row'=4,'col'=8] {'grp'}, dimensions={0} | all-to-all | bytes 131072 | tf_op jit(solution)/shard_map/all_to_all | solution.py:370
  75.1 0.0 copy-done.2
  75.1 0.0 copy-start.1
  75.1 1.2 copy-done.1
  76.3 3.8 %shard_map.97 = (f32[8,2,128,128]{3,2,1,0:T(8,128)}, f32[264,128]{1,0:T(8,128)}, f32[4,128,128]{2,1,0:T(8,128)S(1)}, f32[8,128]{1,0:T(8,128)S(1)}) custom-call(s32[1,4]{1,0:T(1,128)S(1)} %copy-done.4, s32[2]{0:T(128)S(1)} %pad_add_fusion.place, f32[8,2,128,128]{3,2,1,0:T(8,128)S(1)} %copy-done.1, f32[128,128]{1,0:T(8,128)S(1)} %copy-done.3, ...), custom_call_target="tpu_custom_call" | custom-call | tf_op jit(solution)/shard_map/pallas_call | solution.py:314
  80.1 8.3 %all-to-all-start.3 = ((f32[8,2,128,128]{3,2,1,0:T(8,128)}), f32[8,2,128,128]{3,2,1,0:T(8,128)S(1)}, u32[]{:S(2)}, u32[]{:S(2)}) async-start(f32[8,2,128,128]{3,2,1,0:T(8,128)} %get-tuple-element.16), calls=%async_computation.3 | async-start | bytes 2097152 | tf_op jit(solution)/shard_map/all_to_all | solution.py:384
  88.5 0.0 copy-start.5
  88.5 0.7 shard_map.99.er_ref
  89.2 0.2 copy-done.5
  89.4 10.8 %all-gather.1 = f32[1056,128]{1,0:T(8,128)S(1)} all-gather(f32[264,128]{1,0:T(8,128)S(1)} %copy-done.5), channel_id=3, replica_groups=mesh['grp'=16,'row'=4,'col'=8] {'row'}, dimensions={0}, use_global_device_ids=true | all-gather | bytes 675840 | tf_op jit(solution)/shard_map/all_gather | solution.py:385
  100.2 2.7 %shard_map.100 = f32[8,2,128,128]{3,2,1,0:T(8,128)} custom-call(s32[1,4]{1,0:T(1,128)S(1)} %copy-done.4, s32[2]{0:T(128)S(1)} %pad_add_fusion.place, f32[8,2,128,128]{3,2,1,0:T(8,128)S(1)} %all-to-all-done.1.all_ref.key_ref, f32[128,128]{1,0:T(8,128)S(1)} %copy-done.3, f32[8,128,128]{2,1,0:T(8,128)S(1)} %shard_map.99.er_ref, ...), custom_call_target="tpu_custom_call" | custom-call | tf_op jit(solution)/shard_map/pallas_call | solution.py:314
  102.9 0.6 all-to-all-done.3.res_ref
  103.6 6.2 %all-to-all-start.4 = ((f32[8,2,128,128]{3,2,1,0:T(8,128)}), f32[8,2,128,128]{3,2,1,0:T(8,128)S(1)}, u32[]{:S(2)}, u32[]{:S(2)}) async-start(f32[8,2,128,128]{3,2,1,0:T(8,128)} %shard_map.100), calls=%async_computation.4 | async-start | bytes 2097152 | tf_op jit(solution)/shard_map/all_to_all | solution.py:394
  109.8 0.9 shard_map.98
  110.7 14.2 %all-to-all-done.4.res_ref = f32[8,2,128,128]{3,2,1,0:T(8,128)S(1)} async-done(((f32[8,2,128,128]{3,2,1,0:T(8,128)}), f32[8,2,128,128]{3,2,1,0:T(8,128)S(1)}, u32[]{:S(2)}, u32[]{:S(2)}) %all-to-all-start.4) | async-done | bytes 1048608 | tf_op jit(solution)/shard_map/all_to_all | solution.py:394
  124.9 0.9 shard_map.101
Async XLA Ops:
  2.8 25.5 %all-to-all-start.1 = ((f32[8,2,128,128]{3,2,1,0:T(8,128)}), f32[8,2,128,128]{3,2,1,0:T(8,128)S(1)}, u32[]{:S(2)}, u32[]{:S(2)}) async-start(f32[8,2,128,128]{3,2,1,0:T(8,128)} %shard_map.94), calls=%async_computation.1 | async-start | bytes 2097152 | tf_op jit(solution)/shard_map/all_to_all | solution.py:350
  15.2 17.4 %copy-start.3 = (f32[128,128]{1,0:T(8,128)S(1)}, f32[128,128]{1,0:T(8,128)}, u32[]{:S(2)}) copy-start(f32[128,128]{1,0:T(8,128)} %f_ref.7) | copy-start | bytes 196612
  28.2 19.5 %all-to-all-start = ((f32[8,2,128,128]{3,2,1,0:T(8,128)}), f32[8,2,128,128]{3,2,1,0:T(8,128)S(1)}, u32[]{:S(2)}, u32[]{:S(2)}) async-start(f32[8,2,128,128]{3,2,1,0:T(8,128)} %shard_map.93), calls=%async_computation | async-start | bytes 2097152 | tf_op jit(solution)/shard_map/all_to_all | solution.py:350
  32.6 0.7 copy-start.4
  47.7 1.0 copy-start
  48.7 26.4 %copy-start.2 = (f32[8,136,128]{2,1,0:T(8,128)S(1)}, f32[8,136,128]{2,1,0:T(8,128)}, u32[]{:S(2)}) copy-start(f32[8,136,128]{2,1,0:T(8,128)} %all-gather) | copy-start | bytes 1671172
  75.1 1.2 copy-start.1
  80.1 23.4 %all-to-all-start.3 = ((f32[8,2,128,128]{3,2,1,0:T(8,128)}), f32[8,2,128,128]{3,2,1,0:T(8,128)S(1)}, u32[]{:S(2)}, u32[]{:S(2)}) async-start(f32[8,2,128,128]{3,2,1,0:T(8,128)} %get-tuple-element.16), calls=%async_computation.3 | async-start | bytes 2097152 | tf_op jit(solution)/shard_map/all_to_all | solution.py:384
  88.5 0.9 copy-start.5
  103.6 21.3 %all-to-all-start.4 = ((f32[8,2,128,128]{3,2,1,0:T(8,128)}), f32[8,2,128,128]{3,2,1,0:T(8,128)S(1)}, u32[]{:S(2)}, u32[]{:S(2)}) async-start(f32[8,2,128,128]{3,2,1,0:T(8,128)} %shard_map.100), calls=%async_computation.4 | async-start | bytes 2097152 | tf_op jit(solution)/shard_map/all_to_all | solution.py:394

commit v11 on v6

--- a/solution.py
+++ b/solution.py
@@ -335,7 +335,7 @@
     )(k, v, q, g)
     own = lax.all_to_all(packed, "col", 0, 0, tiled=True)
     states = (CHAINS, M + 8, D)
-    peers = (groups * lines, 8, M)
+    peers = (groups * lines, 1, M)
     dma = pltpu.SemaphoreType.DMA
     peaks, own_states, ends = call(
         state_kernel,

time: 128 us -> 120 us (0.938)
  waiting for transfers between devices: 47 us -> 41.7 us
  Pallas kernels: 14.2 us -> 16.7 us
  starting transfers between devices: 39.4 us -> 37 us
    all_to_all x1, waiting for transfers between devices: 6.22 us -> 1.25 us  [on_device(): peaks = lax.all_to_all(peaks, ('grp', 'row'), 0, 0, tiled=True)]
    pallas_call x5, Pallas kernels: 11.6 us -> 14 us  [call(): pl.pallas_call(kernel, out_shape=shapes, in_specs=[smem] * scalars + [vme...]
    all_to_all x1, starting transfers between devices: 8.01 us -> 5.77 us  [on_device(): first = lax.all_to_all(first, 'col', 0, 0, tiled=True)]
    all_to_all x1, starting transfers between devices: 14.8 us -> 13.4 us  [on_device(): peaks = lax.all_to_all(peaks, ('grp', 'row'), 0, 0, tiled=True)]
  transfers between devices with their start and end apart: 4 -> 4, of which waited for: 4 -> 3; matrix products, arithmetic and copies ran while one was open for 0% -> 0% of each run, Pallas kernels for 3% -> 4%
where the time goes in v11:
time: 120 us; the launch traced here: 119 us
  waiting for transfers between devices  41.7 us (35%)
  starting transfers between devices  37 us (31%)
  blocking collectives  23.3 us (19%)
  Pallas kernels  16.7 us (14%)
    all_to_all x1, waiting for transfers between devices, on_device(): own = lax.all_to_all(packed, 'col', 0, 0, tiled=True)  26.3 us
    all_to_all x1, waiting for transfers between devices, on_device(): second = lax.all_to_all(second, 'col', 0, 0, tiled=True)  14.2 us
    pallas_call x5, Pallas kernels, call(): pl.pallas_call(kernel, out_shape=shapes, in_specs=[smem] * scalars + [vme...  14 us
    all_to_all x1, starting transfers between devices, on_device(): peaks = lax.all_to_all(peaks, ('grp', 'row'), 0, 0, tiled=True)  13.4 us
    all_gather x1, blocking collectives, on_device(): ends = lax.all_gather(ends, 'row')  12.1 us
    all_gather x1, blocking collectives, on_device(): back_ends = lax.all_gather(back_ends, 'row')  11.2 us
    all_to_all x1, starting transfers between devices, on_device(): own = lax.all_to_all(packed, 'col', 0, 0, tiled=True)  10.5 us
    all_to_all x1, starting transfers between devices, on_device(): second = lax.all_to_all(second, 'col', 0, 0, tiled=True)  7.35 us
  transfers between devices with their start and end apart: 4, of which 3 were waited for; matrix products, arithmetic and copies ran while one was open for 0% of the time, Pallas kernels for 4%

profile of v11, /device:TPU:1, one launch (start us, length us, event | category | flops | bytes accessed | tf_op | source)
XLA Modules:
  0.0 119.5 jit_solution(17229896585373149950)
XLA Ops:
  0.6 2.7 %shard_map.93 = f32[8,4,128,128]{3,2,1,0:T(8,128)} custom-call(bf16[128,1024]{1,0:T(8,128)(2,1)} %bitcast.14, bf16[128,1024]{1,0:T(8,128)(2,1)} %bitcast.15, bf16[128,1024]{1,0:T(8,128)(2,1)} %bitcast.16, bf16[128,1024]{1,0:T(8,128)(2,1)} %bitcast.17), custom_call_target="tpu_custom_call" | custom-call | tf_op jit(solution)/shard_map/pallas_call | solution.py:323
  3.3 0.0 copy-start
  3.3 0.0 copy-start.1
  3.3 10.5 %all-to-all-start = ((f32[8,4,128,128]{3,2,1,0:T(8,128)}), f32[8,4,128,128]{3,2,1,0:T(8,128)S(1)}, u32[]{:S(2)}, u32[]{:S(2)}) async-start(f32[8,4,128,128]{3,2,1,0:T(8,128)} %shard_map.93), calls=%async_computation | async-start | bytes 4194304 | tf_op jit(solution)/shard_map/all_to_all | solution.py:336
  13.8 0.1 pad_add_fusion.place
  13.9 26.3 %all-to-all-done.all_ref = f32[8,4,128,128]{3,2,1,0:T(8,128)S(1)} async-done(((f32[8,4,128,128]{3,2,1,0:T(8,128)}), f32[8,4,128,128]{3,2,1,0:T(8,128)S(1)}, u32[]{:S(2)}, u32[]{:S(2)}) %all-to-all-start) | async-done | bytes 2097184 | tf_op jit(solution)/shard_map/all_to_all | solution.py:336
  40.2 0.0 copy-done
  40.2 0.0 copy-done.1
  40.2 3.1 %shard_map.94 = (f32[64,1,128]{2,1,0:T(1,128)}, f32[4,136,128]{2,1,0:T(8,128)S(1)}, f32[2,136,128]{2,1,0:T(8,128)}) custom-call(s32[1,4]{1,0:T(1,128)S(1)} %copy-done.1, s32[2]{0:T(128)S(1)} %pad_add_fusion.place, f32[8,4,128,128]{3,2,1,0:T(8,128)S(1)} %all-to-all-done.all_ref, f32[128,128]{1,0:T(8,128)S(1)} %copy-done), custom_call_target="tpu_custom_call" | custom-call | tf_op jit(solution)/shard_map/pallas_call | solution.py:301
  43.3 13.4 %all-to-all-start.1 = ((f32[64,1,128]{2,1,0:T(1,128)}), f32[64,1,128]{2,1,0:T(1,128)S(1)}, u32[]{:S(2)}, u32[]{:S(2)}) async-start(f32[64,1,128]{2,1,0:T(1,128)} %get-tuple-element.15), calls=%async_computation.1 | async-start | bytes 65536 | tf_op jit(solution)/shard_map/all_to_all | solution.py:347
  56.7 12.1 %all-gather = f32[8,136,128]{2,1,0:T(8,128)S(1)} all-gather(f32[2,136,128]{2,1,0:T(8,128)} %get-tuple-element.17), channel_id=2, replica_groups=mesh['grp'=16,'row'=4,'col'=8] {'row'}, dimensions={0}, use_global_device_ids=true | all-gather | bytes 696320 | tf_op jit(solution)/shard_map/all_gather | solution.py:348
  68.8 1.2 %all-to-all-done.1.z_ref = f32[64,1,128]{2,1,0:T(1,128)S(1)} async-done(((f32[64,1,128]{2,1,0:T(1,128)}), f32[64,1,128]{2,1,0:T(1,128)S(1)}, u32[]{:S(2)}, u32[]{:S(2)}) %all-to-all-start.1) | async-done | bytes 32800 | tf_op jit(solution)/shard_map/all_to_all | solution.py:347
  70.1 5.0 %shard_map.95 = (f32[8,2,128,128]{3,2,1,0:T(8,128)}, f32[264,128]{1,0:T(8,128)}, f32[4,128,128]{2,1,0:T(8,128)S(1)}, f32[8,128]{1,0:T(8,128)S(1)}) custom-call(s32[1,4]{1,0:T(1,128)S(1)} %copy-done.1, s32[2]{0:T(128)S(1)} %pad_add_fusion.place, f32[8,4,128,128]{3,2,1,0:T(8,128)S(1)} %all-to-all-done.all_ref, f32[128,128]{1,0:T(8,128)S(1)} %copy-done, ...), custom_call_target="tpu_custom_call" | custom-call | tf_op jit(solution)/shard_map/pallas_call | solution.py:301
  75.1 5.8 %all-to-all-start.2 = ((f32[8,2,128,128]{3,2,1,0:T(8,128)}), f32[8,2,128,128]{3,2,1,0:T(8,128)S(1)}, u32[]{:S(2)}, u32[]{:S(2)}) async-start(f32[8,2,128,128]{3,2,1,0:T(8,128)} %get-tuple-element.18), calls=%async_computation.2 | async-start | bytes 2097152 | tf_op jit(solution)/shard_map/all_to_all | solution.py:362
  80.8 11.2 %all-gather.1 = f32[1056,128]{1,0:T(8,128)S(1)} all-gather(f32[264,128]{1,0:T(8,128)} %get-tuple-element.23), channel_id=3, replica_groups=mesh['grp'=16,'row'=4,'col'=8] {'row'}, dimensions={0}, use_global_device_ids=true | all-gather | bytes 675840 | tf_op jit(solution)/shard_map/all_gather | solution.py:363
  92.0 4.1 %shard_map.97 = f32[8,2,128,128]{3,2,1,0:T(8,128)} custom-call(s32[1,4]{1,0:T(1,128)S(1)} %copy-done.1, s32[2]{0:T(128)S(1)} %pad_add_fusion.place, f32[8,4,128,128]{3,2,1,0:T(8,128)S(1)} %all-to-all-done.all_ref, f32[128,128]{1,0:T(8,128)S(1)} %copy-done, f32[8,128]{1,0:T(8,128)S(1)} %get-tuple-element.21.peak_ref, ...), custom_call_target="tpu_custom_call" | custom-call | tf_op jit(solution)/shard_map/pallas_call | solution.py:301
  96.1 0.0 all-to-all-done.2.res_ref
  96.1 7.3 %all-to-all-start.3 = ((f32[8,2,128,128]{3,2,1,0:T(8,128)}), f32[8,2,128,128]{3,2,1,0:T(8,128)S(1)}, u32[]{:S(2)}, u32[]{:S(2)}) async-start(f32[8,2,128,128]{3,2,1,0:T(8,128)} %shard_map.97), calls=%async_computation.3 | async-start | bytes 2097152 | tf_op jit(solution)/shard_map/all_to_all | solution.py:372
  103.5 0.9 shard_map.96
  104.4 14.2 %all-to-all-done.3.res_ref = f32[8,2,128,128]{3,2,1,0:T(8,128)S(1)} async-done(((f32[8,2,128,128]{3,2,1,0:T(8,128)}), f32[8,2,128,128]{3,2,1,0:T(8,128)S(1)}, u32[]{:S(2)}, u32[]{:S(2)}) %all-to-all-start.3) | async-done | bytes 1048608 | tf_op jit(solution)/shard_map/all_to_all | solution.py:372
  118.6 0.9 shard_map.98
Async XLA Ops:
  3.3 36.9 %copy-start = (f32[128,128]{1,0:T(8,128)S(1)}, f32[128,128]{1,0:T(8,128)}, u32[]{:S(2)}) copy-start(f32[128,128]{1,0:T(8,128)} %f_ref.5) | copy-start | bytes 196612
  3.3 36.9 %copy-start.1 = (s32[1,4]{1,0:T(1,128)S(1)}, s32[1,4]{1,0:T(1,128)}, u32[]{:S(2)}) copy-start(s32[1,4]{1,0:T(1,128)} %lens.5) | copy-start | bytes 52
  3.3 36.9 %all-to-all-start = ((f32[8,4,128,128]{3,2,1,0:T(8,128)}), f32[8,4,128,128]{3,2,1,0:T(8,128)S(1)}, u32[]{:S(2)}, u32[]{:S(2)}) async-start(f32[8,4,128,128]{3,2,1,0:T(8,128)} %shard_map.93), calls=%async_computation | async-start | bytes 4194304 | tf_op jit(solution)/shard_map/all_to_all | solution.py:336
  43.3 26.8 %all-to-all-start.1 = ((f32[64,1,128]{2,1,0:T(1,128)}), f32[64,1,128]{2,1,0:T(1,128)S(1)}, u32[]{:S(2)}, u32[]{:S(2)}) async-start(f32[64,1,128]{2,1,0:T(1,128)} %get-tuple-element.15), calls=%async_computation.1 | async-start | bytes 65536 | tf_op jit(solution)/shard_map/all_to_all | solution.py:347
  75.1 21.1 %all-to-all-start.2 = ((f32[8,2,128,128]{3,2,1,0:T(8,128)}), f32[8,2,128,128]{3,2,1,0:T(8,128)S(1)}, u32[]{:S(2)}, u32[]{:S(2)}) async-start(f32[8,2,128,128]{3,2,1,0:T(8,128)} %get-tuple-element.18), calls=%async_computation.2 | async-start | bytes 2097152 | tf_op jit(solution)/shard_map/all_to_all | solution.py:362
  96.1 22.4 %all-to-all-start.3 = ((f32[8,2,128,128]{3,2,1,0:T(8,128)}), f32[8,2,128,128]{3,2,1,0:T(8,128)S(1)}, u32[]{:S(2)}, u32[]{:S(2)}) async-start(f32[8,2,128,128]{3,2,1,0:T(8,128)} %shard_map.97), calls=%async_computation.3 | async-start | bytes 2097152 | tf_op jit(solution)/shard_map/all_to_all | solution.py:372

commit v12 on v11

--- a/solution.py
+++ b/solution.py
@@ -339,7 +339,7 @@
     dma = pltpu.SemaphoreType.DMA
     peaks, own_states, ends = call(
         state_kernel,
-        [pltpu.HBM(peers, F32), f32(*states), pltpu.HBM((2, M + 8, D), F32)],
+        [pltpu.HBM(peers, F32), pltpu.VMEM(states, F32), pltpu.HBM((2, M + 8, D), F32)],
         (*where, own, features),
         2,
         [pltpu.VMEM(wide, F32), pltpu.VMEM((2, M + 8, D), F32), pltpu.VMEM(peers, F32), dma, dma],
@@ -351,7 +351,7 @@
     small = (2 * CHAINS, M)
     first, back_ends, backs, peak = call(
         query_kernel,
-        [pltpu.HBM(pair, F32), pltpu.HBM(back, F32), f32(CHAINS, M, D), f32(*small)],
+        [pltpu.HBM(pair, F32), pltpu.HBM(back, F32), pltpu.VMEM((CHAINS, M, D), F32), f32(*small)],
         (*where, own, features, peaks, own_states, ends),
         2,
         [pltpu.VMEM(wide, F32), pltpu.VMEM(states, F32)]

time: 120 us -> 121 us (level); the launches traced: 119 us -> 122 us
  Pallas kernels: 16.7 us -> 19 us
    pallas_call x5, Pallas kernels: 14 us -> 16.4 us  [call(): pl.pallas_call(kernel, out_shape=shapes, in_specs=[smem] * scalars + [vme...]
  transfers between devices with their start and end apart: 4 -> 4, of which waited for: 3 -> 3; matrix products, arithmetic and copies ran while one was open for 0% -> 0% of each run, Pallas kernels for 4% -> 5%
where the time goes in v12:
time: 121 us; the launch traced here: 122 us
  waiting for transfers between devices  41.7 us (34%)
  starting transfers between devices  36.9 us (30%)
  blocking collectives  23.3 us (19%)
  Pallas kernels  19 us (16%)
    all_to_all x1, waiting for transfers between devices, on_device(): own = lax.all_to_all(packed, 'col', 0, 0, tiled=True)  26.3 us
    pallas_call x5, Pallas kernels, call(): pl.pallas_call(kernel, out_shape=shapes, in_specs=[smem] * scalars + [vme...  16.4 us
    all_to_all x1, waiting for transfers between devices, on_device(): second = lax.all_to_all(second, 'col', 0, 0, tiled=True)  14.2 us
    all_to_all x1, starting transfers between devices, on_device(): peaks = lax.all_to_all(peaks, ('grp', 'row'), 0, 0, tiled=True)  13.4 us
    all_gather x1, blocking collectives, on_device(): ends = lax.all_gather(ends, 'row')  12.1 us
    all_gather x1, blocking collectives, on_device(): back_ends = lax.all_gather(back_ends, 'row')  11.2 us
    all_to_all x1, starting transfers between devices, on_device(): own = lax.all_to_all(packed, 'col', 0, 0, tiled=True)  10.5 us
    all_to_all x1, starting transfers between devices, on_device(): second = lax.all_to_all(second, 'col', 0, 0, tiled=True)  7.27 us
  transfers between devices with their start and end apart: 4, of which 3 were waited for; matrix products, arithmetic and copies ran while one was open for 0% of the time, Pallas kernels for 5%

profile of v12, /device:TPU:1, one launch (start us, length us, event | category | flops | bytes accessed | tf_op | source)
XLA Modules:
  0.0 121.8 jit_solution(17229896585373149950)
XLA Ops:
  0.6 2.7 %shard_map.93 = f32[8,4,128,128]{3,2,1,0:T(8,128)} custom-call(bf16[128,1024]{1,0:T(8,128)(2,1)} %bitcast.14, bf16[128,1024]{1,0:T(8,128)(2,1)} %bitcast.15, bf16[128,1024]{1,0:T(8,128)(2,1)} %bitcast.16, bf16[128,1024]{1,0:T(8,128)(2,1)} %bitcast.17), custom_call_target="tpu_custom_call" | custom-call | tf_op jit(solution)/shard_map/pallas_call | solution.py:323
  3.3 0.0 copy-start
  3.3 0.0 copy-start.1
  3.3 10.5 %all-to-all-start = ((f32[8,4,128,128]{3,2,1,0:T(8,128)}), f32[8,4,128,128]{3,2,1,0:T(8,128)S(1)}, u32[]{:S(2)}, u32[]{:S(2)}) async-start(f32[8,4,128,128]{3,2,1,0:T(8,128)} %shard_map.93), calls=%async_computation | async-start | bytes 4194304 | tf_op jit(solution)/shard_map/all_to_all | solution.py:336
  13.8 0.1 pad_add_fusion.place
  13.9 26.3 %all-to-all-done.all_ref = f32[8,4,128,128]{3,2,1,0:T(8,128)S(1)} async-done(((f32[8,4,128,128]{3,2,1,0:T(8,128)}), f32[8,4,128,128]{3,2,1,0:T(8,128)S(1)}, u32[]{:S(2)}, u32[]{:S(2)}) %all-to-all-start) | async-done | bytes 2097184 | tf_op jit(solution)/shard_map/all_to_all | solution.py:336
  40.2 0.0 copy-done
  40.2 0.0 copy-done.1
  40.2 3.6 %shard_map.94 = (f32[64,1,128]{2,1,0:T(1,128)}, f32[4,136,128]{2,1,0:T(8,128)S(1)}, f32[2,136,128]{2,1,0:T(8,128)}) custom-call(s32[1,4]{1,0:T(1,128)S(1)} %copy-done.1, s32[2]{0:T(128)S(1)} %pad_add_fusion.place, f32[8,4,128,128]{3,2,1,0:T(8,128)S(1)} %all-to-all-done.all_ref, f32[128,128]{1,0:T(8,128)S(1)} %copy-done), custom_call_target="tpu_custom_call" | custom-call | tf_op jit(solution)/shard_map/pallas_call | solution.py:301
  43.8 13.4 %all-to-all-start.1 = ((f32[64,1,128]{2,1,0:T(1,128)}), f32[64,1,128]{2,1,0:T(1,128)S(1)}, u32[]{:S(2)}, u32[]{:S(2)}) async-start(f32[64,1,128]{2,1,0:T(1,128)} %get-tuple-element.15), calls=%async_computation.1 | async-start | bytes 65536 | tf_op jit(solution)/shard_map/all_to_all | solution.py:347
  57.2 12.1 %all-gather = f32[8,136,128]{2,1,0:T(8,128)S(1)} all-gather(f32[2,136,128]{2,1,0:T(8,128)} %get-tuple-element.17), channel_id=2, replica_groups=mesh['grp'=16,'row'=4,'col'=8] {'row'}, dimensions={0}, use_global_device_ids=true | all-gather | bytes 696320 | tf_op jit(solution)/shard_map/all_gather | solution.py:348
  69.3 1.2 %all-to-all-done.1.z_ref = f32[64,1,128]{2,1,0:T(1,128)S(1)} async-done(((f32[64,1,128]{2,1,0:T(1,128)}), f32[64,1,128]{2,1,0:T(1,128)S(1)}, u32[]{:S(2)}, u32[]{:S(2)}) %all-to-all-start.1) | async-done | bytes 32800 | tf_op jit(solution)/shard_map/all_to_all | solution.py:347
  70.6 6.1 %shard_map.95 = (f32[8,2,128,128]{3,2,1,0:T(8,128)}, f32[264,128]{1,0:T(8,128)}, f32[4,128,128]{2,1,0:T(8,128)S(1)}, f32[8,128]{1,0:T(8,128)S(1)}) custom-call(s32[1,4]{1,0:T(1,128)S(1)} %copy-done.1, s32[2]{0:T(128)S(1)} %pad_add_fusion.place, f32[8,4,128,128]{3,2,1,0:T(8,128)S(1)} %all-to-all-done.all_ref, f32[128,128]{1,0:T(8,128)S(1)} %copy-done, ...), custom_call_target="tpu_custom_call" | custom-call | tf_op jit(solution)/shard_map/pallas_call | solution.py:301
  76.7 5.8 %all-to-all-start.2 = ((f32[8,2,128,128]{3,2,1,0:T(8,128)}), f32[8,2,128,128]{3,2,1,0:T(8,128)S(1)}, u32[]{:S(2)}, u32[]{:S(2)}) async-start(f32[8,2,128,128]{3,2,1,0:T(8,128)} %get-tuple-element.18), calls=%async_computation.2 | async-start | bytes 2097152 | tf_op jit(solution)/shard_map/all_to_all | solution.py:362
  82.4 11.2 %all-gather.1 = f32[1056,128]{1,0:T(8,128)S(1)} all-gather(f32[264,128]{1,0:T(8,128)} %get-tuple-element.23), channel_id=3, replica_groups=mesh['grp'=16,'row'=4,'col'=8] {'row'}, dimensions={0}, use_global_device_ids=true | all-gather | bytes 675840 | tf_op jit(solution)/shard_map/all_gather | solution.py:363
  93.6 4.8 %shard_map.97 = f32[8,2,128,128]{3,2,1,0:T(8,128)} custom-call(s32[1,4]{1,0:T(1,128)S(1)} %copy-done.1, s32[2]{0:T(128)S(1)} %pad_add_fusion.place, f32[8,4,128,128]{3,2,1,0:T(8,128)S(1)} %all-to-all-done.all_ref, f32[128,128]{1,0:T(8,128)S(1)} %copy-done, f32[8,128]{1,0:T(8,128)S(1)} %get-tuple-element.21.peak_ref, ...), custom_call_target="tpu_custom_call" | custom-call | tf_op jit(solution)/shard_map/pallas_call | solution.py:301
  98.5 0.0 all-to-all-done.2.res_ref
  98.5 7.3 %all-to-all-start.3 = ((f32[8,2,128,128]{3,2,1,0:T(8,128)}), f32[8,2,128,128]{3,2,1,0:T(8,128)S(1)}, u32[]{:S(2)}, u32[]{:S(2)}) async-start(f32[8,2,128,128]{3,2,1,0:T(8,128)} %shard_map.97), calls=%async_computation.3 | async-start | bytes 2097152 | tf_op jit(solution)/shard_map/all_to_all | solution.py:372
  105.8 0.9 shard_map.96
  106.7 14.2 %all-to-all-done.3.res_ref = f32[8,2,128,128]{3,2,1,0:T(8,128)S(1)} async-done(((f32[8,2,128,128]{3,2,1,0:T(8,128)}), f32[8,2,128,128]{3,2,1,0:T(8,128)S(1)}, u32[]{:S(2)}, u32[]{:S(2)}) %all-to-all-start.3) | async-done | bytes 1048608 | tf_op jit(solution)/shard_map/all_to_all | solution.py:372
  120.9 0.9 shard_map.98
Async XLA Ops:
  3.3 36.9 %copy-start = (f32[128,128]{1,0:T(8,128)S(1)}, f32[128,128]{1,0:T(8,128)}, u32[]{:S(2)}) copy-start(f32[128,128]{1,0:T(8,128)} %f_ref.5) | copy-start | bytes 196612
  3.3 36.9 %copy-start.1 = (s32[1,4]{1,0:T(1,128)S(1)}, s32[1,4]{1,0:T(1,128)}, u32[]{:S(2)}) copy-start(s32[1,4]{1,0:T(1,128)} %lens.5) | copy-start | bytes 52
  3.3 36.9 %all-to-all-start = ((f32[8,4,128,128]{3,2,1,0:T(8,128)}), f32[8,4,128,128]{3,2,1,0:T(8,128)S(1)}, u32[]{:S(2)}, u32[]{:S(2)}) async-start(f32[8,4,128,128]{3,2,1,0:T(8,128)} %shard_map.93), calls=%async_computation | async-start | bytes 4194304 | tf_op jit(solution)/shard_map/all_to_all | solution.py:336
  43.8 26.7 %all-to-all-start.1 = ((f32[64,1,128]{2,1,0:T(1,128)}), f32[64,1,128]{2,1,0:T(1,128)S(1)}, u32[]{:S(2)}, u32[]{:S(2)}) async-start(f32[64,1,128]{2,1,0:T(1,128)} %get-tuple-element.15), calls=%async_computation.1 | async-start | bytes 65536 | tf_op jit(solution)/shard_map/all_to_all | solution.py:347
  76.7 21.8 %all-to-all-start.2 = ((f32[8,2,128,128]{3,2,1,0:T(8,128)}), f32[8,2,128,128]{3,2,1,0:T(8,128)S(1)}, u32[]{:S(2)}, u32[]{:S(2)}) async-start(f32[8,2,128,128]{3,2,1,0:T(8,128)} %get-tuple-element.18), calls=%async_computation.2 | async-start | bytes 2097152 | tf_op jit(solution)/shard_map/all_to_all | solution.py:362
  98.5 22.4 %all-to-all-start.3 = ((f32[8,2,128,128]{3,2,1,0:T(8,128)}), f32[8,2,128,128]{3,2,1,0:T(8,128)S(1)}, u32[]{:S(2)}, u32[]{:S(2)}) async-start(f32[8,2,128,128]{3,2,1,0:T(8,128)} %shard_map.97), calls=%async_computation.3 | async-start | bytes 2097152 | tf_op jit(solution)/shard_map/all_to_all | solution.py:372
